TPU v7x, 128 devices: a whole 4x4x4 slice. The times are simulated.
128 devices in a mesh: ha: 8 (over y_hi, z), wa: 16 (over y_lo, x, core).
Axes of the slice: x: 4, y: 4 (y_hi: 2, y_lo: 2; y = y_hi * 2 + y_lo), z: 4, core: 2. Of those that a mesh axis runs over, the one named last changes fastest.
Arguments:
- clip: bfloat16 [3, 17, 256, 512], P(None, None, 'ha', 'wa'), may hold values from -6 to 6
- w_first: bfloat16 [3, 3, 3, 3, 64], replicated, may hold values from -0.625 to 0.625
- b_first: float32 [64], replicated, may hold values from -3 to 3
- w_second: bfloat16 [3, 3, 3, 64, 128], replicated, may hold values from -0.15625 to 0.15625
- b_second: float32 [128], replicated, may hold values from -3 to 3
- upstream: bfloat16 [9, 128, 256, 128], P(None, 'ha', 'wa'), may hold values from -6 to 6
Outputs:
- input_grad: float32 [3, 17, 256, 512], P(None, None, 'ha', 'wa')
- grad_first: float32 [3, 3, 3, 3, 64], replicated
- grad_second: float32 [3, 3, 3, 64, 128], P(None, None, None, 'ha', 'wa')
All inputs are finite; a program needn't handle non-finite values.
Results may differ from a plain program's by a relative error of at most 0.015.
The roundings to bfloat16 on the way count: a program that leaves them out, or rounds other values in their place, can miss the bound.
Values may be sent and summed in bfloat16 or wider, within the bound.
No kernel may reach another device: no remote copies, remote signals or barrier semaphores. Data moves between devices by JAX's collectives and lax.ppermute only.
A program may use at most 192 MiB of HBM per device.

v0:
```python
import jax
import jax.numpy as jnp
from jax import lax
from jax.sharding import PartitionSpec as P

LEAK = 0.2


def padded(value, sides, width):
    for axis, dim in sides:
        size, length = (lax.axis_size(axis), value.shape[dim])
        up = [(i, (i + 1) % size) for i in range(size - 1)]
        down = [(j, i) for i, j in up]
        last = lax.slice_in_dim(value, length - width, length, axis=dim)
        first = lax.slice_in_dim(value, 0, width, axis=dim)
        before = lax.ppermute(last, axis, up)
        after = lax.ppermute(first, axis, down)
        value = jnp.concatenate([before, value, after], axis=dim)
    return value


def from_behind(value, axis, by):
    size = lax.axis_size(axis)
    pairs = [(i, i + by) for i in range(size) if 0 <= i + by < size]
    return lax.ppermute(value, axis, pairs)


def convolve(source, kernel, specs, strides, padding, dilation):
    return lax.conv_general_dilated(
        source,
        kernel,
        strides,
        padding,
        lhs_dilation=dilation,
        dimension_numbers=specs,
        preferred_element_type=jnp.float32,
    )


def kernel_terms_first(source, cotangent):
    result = lax.conv_general_dilated(
        source[None],
        cotangent[..., None],
        (1, 1, 1),
        "VALID",
        dimension_numbers=("CNDHW", "DHWOI", "NDHWC"),
        preferred_element_type=jnp.float32,
    )
    return jnp.moveaxis(result, 0, 3)


def kernel_terms_second(source, cotangent):
    result = lax.conv_general_dilated(
        source[None],
        cotangent[None],
        (1, 1, 1),
        "VALID",
        rhs_dilation=(2, 2, 2),
        dimension_numbers=("CDHWN", "IDHWO", "NDHWC"),
        preferred_element_type=jnp.float32,
    )
    return jnp.moveaxis(result, 0, 3)


def body(clip, w_first, b_first, w_second, b_second, upstream):
    frames, rows, cols = (clip.shape[1], clip.shape[2], clip.shape[3])
    unit = (1, 1, 1)
    time_only = ((1, 1), (0, 0), (0, 0))
    first_in = ("NCDHW", "DHWIO", "NDHWC")
    clip_ext = padded(clip, (("ha", 2), ("wa", 3)), 1)
    pre_first = convolve(clip_ext[None], w_first, first_in, unit, time_only, unit)[0] + b_first
    slope_first = jnp.where(pre_first > 0, 1.0, LEAK)
    hidden = (pre_first * slope_first).astype(jnp.bfloat16)
    hidden_low = from_behind(hidden[:, -1:], "ha", 1)
    hidden_rowed = jnp.concatenate([hidden_low, hidden], axis=1)
    hidden_left = from_behind(hidden_rowed[:, :, -1:], "wa", 1)
    hidden_ext = jnp.concatenate([hidden_left, hidden_rowed], axis=2)
    pre_second = (
        convolve(
            hidden_ext[None], w_second, ("NDHWC", "DHWIO", "NDHWC"), (2, 2, 2), time_only, unit
        )[0]
        + b_second
    )
    slope_second = jnp.where(pre_second > 0, 1.0, LEAK)
    score_delta = (upstream.astype(jnp.float32) * slope_second).astype(jnp.bfloat16)
    score_high = from_behind(score_delta[:, :1], "ha", -1)
    score_rowed = jnp.concatenate([score_delta, score_high], axis=1)
    score_right = from_behind(score_rowed[:, :, :1], "wa", -1)
    score_ext = jnp.concatenate([score_rowed, score_right], axis=2)
    back_hidden = convolve(
        score_ext[None],
        w_second[::-1, ::-1, ::-1],
        ("NDHWC", "DHWOI", "NDHWC"),
        unit,
        ((1, 1), (1, 0), (1, 0)),
        (2, 2, 2),
    )[0]
    hidden_delta = (back_hidden * slope_first).astype(jnp.bfloat16)
    flipped = w_first[::-1, ::-1, ::-1]
    delta_ext = padded(hidden_delta, (("ha", 1), ("wa", 2)), 1)
    input_grad = convolve(
        delta_ext[None], flipped, ("NDHWC", "DHWOI", "NCDHW"), unit, time_only, unit
    )[0]
    tangent = input_grad.astype(jnp.bfloat16)
    tangent_ext = padded(tangent, (("ha", 2), ("wa", 3)), 1)
    pre_tangent = convolve(tangent_ext[None], w_first, first_in, unit, time_only, unit)[0]
    tangent_hidden = (pre_tangent * slope_first).astype(jnp.bfloat16)
    tangent_low = from_behind(tangent_hidden[:, -1:], "ha", 1)
    tangent_rowed = jnp.concatenate([tangent_low, tangent_hidden], axis=1)
    tangent_left = from_behind(tangent_rowed[:, :, -1:], "wa", 1)
    tangent_hidden_ext = jnp.concatenate([tangent_left, tangent_rowed], axis=2)
    scale = 1.0 / (frames * rows * lax.axis_size("ha") * cols * lax.axis_size("wa"))
    tangent_pad = jnp.pad(tangent_ext, ((0, 0), (1, 1), (0, 0), (0, 0)))
    term_first = kernel_terms_first(tangent_pad, hidden_delta) * scale
    hidden_pad = jnp.pad(tangent_hidden_ext, ((1, 1), (0, 0), (0, 0), (0, 0)))
    term_second = kernel_terms_second(hidden_pad, score_delta) * scale
    grad_first, second_whole = lax.psum((term_first, term_second), ("ha", "wa"))
    in_share = second_whole.shape[3] // lax.axis_size("ha")
    out_share = second_whole.shape[4] // lax.axis_size("wa")
    second_rows = lax.dynamic_slice_in_dim(
        second_whole, lax.axis_index("ha") * in_share, in_share, 3
    )
    grad_second = lax.dynamic_slice_in_dim(
        second_rows, lax.axis_index("wa") * out_share, out_share, 4
    )
    return (input_grad, grad_first, grad_second)


def solution(mesh):
    placed = (P(None, None, "ha", "wa"), P(), P(), P(), P(), P(None, "ha", "wa", None))
    return jax.shard_map(
        body,
        mesh=mesh,
        in_specs=placed,
        out_specs=(P(None, None, "ha", "wa"), P(), P(None, None, None, "ha", "wa")),
        check_vma=False,
    )
```

profile of v0, /device:TPU:0, one launch (start us, length us, event | category | flops | bytes accessed | tf_op | source)
XLA Modules:
  0.0 913.5 jit_solution(14861359208373537133)
XLA Ops:
  8.3 3.9 collective-permute-start
  12.2 1.3 collective-permute-start.1
  13.7 4.2 collective-permute-done.1
  17.9 1.2 pad_maximum_fusion
  19.4 1.3 collective-permute-start.2
  20.7 1.3 collective-permute-start.3
  22.2 4.0 collective-permute-done.3
  26.2 1.7 maximum_bitcast_fusion.3
  29.6 7.0 copy.73
  37.3 23.0 %broadcast_select_fusion.1 = f32[17,32,8,5,64]{4,2,3,1,0:T(8,128)} fusion(pred[8,5]{0,1:T(8,128)(4,1)S(1)} %copy-done.12, bf16[3,3,3,3,64]{4,3,2,1,0:T(4,128)(2,1)S(1)} %copy-done.10, bf16[3,17,34,1,7,2]{4,0,5,2,1,3:T(4,128)(2,1)S(1)} %slice.84, bf16[3,17,34,1,8,5]{4,0,5,2,1,3:T(4,128)(2,1)S(1)} %copy.73), kind=kOutput, calls=%fused_computation.46 | convolution fusion | flops 218735584 | bytes 5768240 | tf_op jit(solution)/shard_map/conv_general_dilated | solution.py:29
  60.3 10.3 %copy.74 = f32[17,32,8,5,64]{4,1,3,2,0:T(8,128)} copy(f32[17,32,8,5,64]{4,2,3,1,0:T(8,128)} %broadcast_select_fusion.1) | data formatting | bytes 11141120 | tf_op jit(solution)/shard_map/conv_general_dilated | solution.py:29
  70.6 4.8 fusion.9
  75.8 3.8 collective-permute-start.4
  79.6 4.0 collective-permute-done.4
  83.7 8.4 collective-permute-start.5
  93.0 4.2 maximum_bitcast_fusion.1
  97.2 4.6 pad.12
  101.9 4.6 copy.77
  106.5 2.3 slice.87
  108.8 6.3 fusion.60
  115.8 1.3 collective-permute-start.6
  117.1 5.1 collective-permute-done.6
  122.2 1.5 collective-permute-start.7
  123.8 4.7 collective-permute-done.7
  129.5 8.5 convolution_select_fusion
  138.0 13.9 %copy.82 = f32[17,32,8,6,64]{4,1,3,2,0:T(8,128)} copy(f32[17,32,8,6,64]{4,2,3,1,0:T(8,128)} %convolution_select_fusion) | data formatting | bytes 13369344 | tf_op jit(solution)/shard_map/conv_general_dilated | solution.py:29
  151.9 5.1 fusion.10
  157.6 6.5 collective-permute-start.8
  164.2 1.3 collective-permute-start.9
  165.5 2.7 collective-permute-done.8
  168.2 4.9 collective-permute-done.9
  173.9 5.2 collective-permute-start.10
  179.1 1.8 collective-permute-start.11
  180.9 4.1 collective-permute-done.11
  185.0 5.4 maximum_bitcast_fusion
  190.4 1.7 pad.16
  193.6 338.0 %broadcast_select_fusion.2 = f32[17,32,8,5,3]{2,4,3,1,0:T(4,128)} fusion(pred[8,5]{0,1:T(8,128)(4,1)S(1)} %copy-done.12, bf16[3,3,3,3,64]{4,3,2,1,0:T(4,128)(2,1)S(1)} %copy-done.11, bf16[17,34,1,7,2,64]{5,3,4,1,0,2:T(8,128)(2,1)S(1)} %slice.94, bf16[17,34,1,8,5,64]{5,3,4,1,0,2:T(8,128)(2,1)S(1)} %copy.84), kind=kOutput, calls=%fused_computation.61 | convolution fusion | flops 229254912 | bytes 4266664 | tf_op jit(solution)/shard_map/conv_general_dilated | solution.py:29
  531.6 6.1 copy.85
  537.7 2.4 reshape.64
  540.1 1.2 fusion.91
  541.5 7.6 collective-permute-start.12
  549.1 1.4 collective-permute-start.13
  550.5 9.4 %fusion.13 = bf16[17,32,32,64,1]{3,1,2,0,4:T(8,128)(2,1)} fusion(f32[17,32,1,48,64]{4,1,3,0,2:T(8,128)} %bitcast.106, f32[17,32,1,40,64]{4,1,3,0,2:T(8,128)} %bitcast.104, f32[64]{0:T(128)S(1)} %copy-done.8), kind=kLoop, calls=%fused_computation.23 | loop fusion | flops 5570560 | bytes 11141376 | tf_op jit(solution)/shard_map/convert_element_type | solution.py:98
  561.3 4.8 collective-permute-start.14
  566.2 1.3 collective-permute-start.15
  568.5 2.3 copy.96
  570.8 3.5 collective-permute-done.15
  574.4 1.5 fusion.103
  576.8 2.3 reshape.107
  579.2 6.1 copy.91
  585.2 2.0 slice.98
  587.2 23.1 %broadcast_select_fusion = f32[17,32,8,5,64]{4,2,3,1,0:T(8,128)} fusion(pred[8,5]{0,1:T(8,128)(4,1)S(1)} %copy-done.12, bf16[3,3,3,3,64]{4,3,2,1,0:T(4,128)(2,1)} %param.7, bf16[3,17,34,1,7,2]{4,0,5,2,1,3:T(4,128)(2,1)S(1)} %slice.98, bf16[3,17,34,1,8,5]{4,0,5,2,1,3:T(4,128)(2,1)} %copy.91), kind=kOutput, calls=%fused_computation.45 | convolution fusion | flops 218735584 | bytes 5768240 | tf_op jit(solution)/shard_map/conv_general_dilated | solution.py:29
  610.3 10.2 %copy.92 = f32[17,32,8,5,64]{4,1,3,2,0:T(8,128)} copy(f32[17,32,8,5,64]{4,2,3,1,0:T(8,128)} %broadcast_select_fusion) | data formatting | bytes 11141120 | tf_op jit(solution)/shard_map/conv_general_dilated | solution.py:29
  620.5 5.1 fusion.11
  626.0 5.8 collective-permute-start.16
  631.8 1.5 pad_maximum_fusion.1
  633.4 3.8 collective-permute-done.16
  637.3 3.7 collective-permute-start.17
  641.1 28.0 %copy.87 = bf16[1,3,19,34,34]{1,0,4,3,2:T(2,128)(2,1)} copy(bf16[1,3,19,34,34]{3,4,1,2,0:T(8,128)(2,1)S(1)} %pad_bitcast_fusion) | data formatting | bytes 263568 | tf_op jit(solution)/shard_map/broadcast_in_dim | solution.py:42
  669.1 4.6 fusion.30
  673.7 31.6 %fusion.57 = f32[3,3,3,64,128]{4,3,2,1,0:T(8,128)} fusion(bf16[1,19,33,33,64]{4,2,3,1,0:T(8,128)(2,1)S(1)} %fusion.30, bf16[1,9,16,16,128]{4,2,3,1,0:T(8,128)(2,1)S(1)} %bitcast.110), kind=kOutput, calls=%fused_computation.66 | convolution fusion | flops 1019437056 | bytes 4123008 | tf_op jit(solution)/shard_map/transpose | solution.py:62
  705.3 121.1 %fusion.72 = f32[3,3,3,3,64]{4,3,2,1,0:T(4,128)S(1)} fusion(bf16[1,3,19,34,34]{1,0,4,3,2:T(2,128)(2,1)} %copy.87, bf16[17,32,32,64,1]{3,1,2,0,4:T(8,128)(2,1)} %fusion.13), kind=kOutput, calls=%fused_computation.78 | convolution fusion | flops 180491328 | bytes 2380744 | tf_op jit(solution)/shard_map/transpose | solution.py:49
  826.5 78.1 %psum.14 = f32[3,3,3,3,64]{4,3,2,1,0:T(4,128)} all-reduce(f32[3,3,3,3,64]{4,3,2,1,0:T(4,128)S(1)} %fusion.72), channel_id=1, replica_groups=mesh['ha'=8,'wa'=16] {'ha','wa'}, use_global_device_ids=true, to_apply=%region_0.1 | all-reduce | flops 5184 | bytes 41472 | tf_op jit(solution)/shard_map/psum | solution.py:117
  904.5 1.7 constant_dynamic-slice_fusion
  (69 shorter events, 13.7 us)
Async XLA Ops:
  7.2 101.6 %copy-start = (bf16[3,3,3,64,128]{4,3,2,1,0:T(8,128)(2,1)S(1)}, bf16[3,3,3,64,128]{4,3,2,1,0:T(8,128)(2,1)}, u32[]{:S(2)}) copy-start(bf16[3,3,3,64,128]{4,3,2,1,0:T(8,128)(2,1)} %param.9) | copy-start | bytes 1327108
  7.2 897.4 %all-reduce.4.cloned.1.call-start = ((), (), s32[]{:S(2)}) async-start(), calls=%async_computation | async-start | bytes 1769472 | tf_op jit(solution)/shard_map/psum | solution.py:117
  8.3 5.4 collective-permute-start
  12.2 5.7 collective-permute-start.1
  19.2 18.2 %copy-start.10 = (bf16[3,3,3,3,64]{4,3,2,1,0:T(4,128)(2,1)S(1)}, bf16[3,3,3,3,64]{4,3,2,1,0:T(4,128)(2,1)}, u32[]{:S(2)}) copy-start(bf16[3,3,3,3,64]{4,3,2,1,0:T(4,128)(2,1)} %param.7) | copy-start | bytes 31108
  19.2 18.2 %copy-start.12 = (pred[8,5]{0,1:T(8,128)(4,1)S(1)}, pred[8,5]{0,1:T(8,128)(4,1)}, u32[]{:S(2)}) copy-start(pred[8,5]{0,1:T(8,128)(4,1)} %constant.78) | copy-start | bytes 124
  19.4 2.8 collective-permute-start.2
  20.7 5.5 collective-permute-start.3
  60.3 10.3 %copy-start.8 = (f32[64]{0:T(128)S(1)}, f32[64]{0:T(128)}, u32[]{:S(2)}) copy-start(f32[64]{0:T(128)} %param.8) | copy-start | bytes 772
  75.8 7.9 collective-permute-start.4
  83.7 9.3 %collective-permute-start.5 = (bf16[17,33,1,64]{3,1,2,0:T(8,128)(2,1)S(1)}, bf16[17,33,1,64]{3,1,2,0:T(8,128)(2,1)S(1)}, u32[]{:S(2)}, u32[]{:S(2)}) collective-permute-start(bf16[17,33,1,64]{3,1,2,0:T(8,128)(2,1)S(1)} %pad_maximum_fusion.6), channel_id=1, source_target_pairs={{0,1},{1,2},{2,3},{3,4},{4,5},{5,6},{6,7},{7,8},{8,9},{9,10},{10,1... | collective-permute-start | bytes 215432 | tf_op jit(solution)/shard_map/ppermute | solution.py:25
  101.9 6.9 copy-start.14
  108.8 6.6 copy-start.7
  108.8 6.6 copy-start.9
  115.4 14.0 %copy-start.13 = (pred[8,6]{0,1:T(8,128)(4,1)S(1)}, pred[8,6]{0,1:T(8,128)(4,1)}, u32[]{:S(2)}) copy-start(pred[8,6]{0,1:T(8,128)(4,1)} %constant.79) | copy-start | bytes 148
  115.7 12.8 %copy-start.4 = (bf16[9,16,16,128]{3,1,2,0:T(8,128)(2,1)}, bf16[9,16,16,128]{3,1,2,0:T(8,128)(2,1)S(1)}, u32[]{:S(2)}) copy-start(bf16[9,16,16,128]{3,1,2,0:T(8,128)(2,1)S(1)} %multiply_convert_fusion) | copy-start | bytes 1769476
  115.8 6.4 collective-permute-start.6
  122.2 6.3 collective-permute-start.7
  157.0 16.0 %copy-start.2 = (bf16[17,32,32,64]{3,1,2,0:T(8,128)(2,1)}, bf16[17,32,32,64]{3,1,2,0:T(8,128)(2,1)S(1)}, u32[]{:S(2)}) copy-start(bf16[17,32,32,64]{3,1,2,0:T(8,128)(2,1)S(1)} %fusion.10) | copy-start | bytes 6684676
  157.6 10.5 %collective-permute-start.8 = (bf16[17,1,32,64]{3,1,2,0:T(2,128)(2,1)S(1)}, bf16[17,1,32,64]{3,1,2,0:T(2,128)(2,1)S(1)}, u32[]{:S(2)}, u32[]{:S(2)}) collective-permute-start(bf16[17,1,32,64]{3,1,2,0:T(2,128)(2,1)S(1)} %get-tuple-element.19), channel_id=1, source_target_pairs={{0,16},{16,32},{32,48},{48,64},{64,80},{80,96},{96,112},{1,17},{17... | collective-permute-start | bytes 208904 | tf_op jit(solution)/shard_map/ppermute | solution.py:16
  164.2 8.9 collective-permute-start.9
  173.9 7.1 collective-permute-start.10
  179.1 5.9 collective-permute-start.11
  192.2 1.4 copy-start.11
  541.5 18.5 %collective-permute-start.12 = (bf16[3,17,1,32]{2,3,0,1:T(8,128)(2,1)S(1)}, bf16[3,17,1,32]{2,3,0,1:T(8,128)(2,1)S(1)}, u32[]{:S(2)}, u32[]{:S(2)}) collective-permute-start(bf16[3,17,1,32]{2,3,0,1:T(8,128)(2,1)S(1)} %get-tuple-element.25), channel_id=1, source_target_pairs={{0,16},{16,32},{32,48},{48,64},{64,80},{80,96},{96,112},{1,17},{17... | collective-permute-start | bytes 9800 | tf_op jit(solution)/shard_map/ppermute | solution.py:16
  549.1 18.4 %copy-start.6 = (f32[17,32,1,40,3]{1,3,4,0,2:T(8,128)S(1)}, f32[17,32,1,40,3]{1,3,4,0,2:T(8,128)}, u32[]{:S(2)}) copy-start(f32[17,32,1,40,3]{1,3,4,0,2:T(8,128)} %reshape.64) | copy-start | bytes 783364
  549.1 11.4 %collective-permute-start.13 = (bf16[3,17,1,32]{2,3,0,1:T(8,128)(2,1)S(1)}, bf16[3,17,1,32]{2,3,0,1:T(8,128)(2,1)S(1)}, u32[]{:S(2)}, u32[]{:S(2)}) collective-permute-start(bf16[3,17,1,32]{2,3,0,1:T(8,128)(2,1)S(1)} %get-tuple-element.26), channel_id=1, source_target_pairs={{16,0},{32,16},{48,32},{64,48},{80,64},{96,80},{112,96},{17,1},{33... | collective-permute-start | bytes 9800 | tf_op jit(solution)/shard_map/ppermute | solution.py:17
  561.3 9.5 %collective-permute-start.14 = (bf16[3,17,34,1]{2,3,0,1:T(2,128)(2,1)}, bf16[3,17,34,1]{2,3,0,1:T(2,128)(2,1)S(1)}, u32[]{:S(2)}, u32[]{:S(2)}) collective-permute-start(bf16[3,17,34,1]{2,3,0,1:T(2,128)(2,1)} %get-tuple-element.21), channel_id=1, source_target_pairs={{0,1},{1,2},{2,3},{3,4},{4,5},{5,6},{6,7},{7,8},{8,9},{9,10},{10,1... | collective-permute-start | bytes 10412 | tf_op jit(solution)/shard_map/ppermute | solution.py:16
  566.2 8.2 collective-permute-start.15
  625.7 11.5 %copy-start.3 = (bf16[17,32,32,64]{3,1,2,0:T(8,128)(2,1)}, bf16[17,32,32,64]{3,1,2,0:T(8,128)(2,1)S(1)}, u32[]{:S(2)}) copy-start(bf16[17,32,32,64]{3,1,2,0:T(8,128)(2,1)S(1)} %fusion.11) | copy-start | bytes 6684676
  626.0 11.2 %collective-permute-start.16 = (bf16[17,1,32,64]{3,1,2,0:T(2,128)(2,1)S(1)}, bf16[17,1,32,64]{3,1,2,0:T(2,128)(2,1)S(1)}, u32[]{:S(2)}, u32[]{:S(2)}) collective-permute-start(bf16[17,1,32,64]{3,1,2,0:T(2,128)(2,1)S(1)} %slice.100), channel_id=1, source_target_pairs={{0,16},{16,32},{32,48},{48,64},{64,80},{80,96},{96,112},{1,17},{17... | collective-permute-start | bytes 208904 | tf_op jit(solution)/shard_map/ppermute | solution.py:25
  637.3 31.8 %collective-permute-start.17 = (bf16[17,33,1,64]{3,1,2,0:T(8,128)(2,1)S(1)}, bf16[17,33,1,64]{3,1,2,0:T(8,128)(2,1)S(1)}, u32[]{:S(2)}, u32[]{:S(2)}) collective-permute-start(bf16[17,33,1,64]{3,1,2,0:T(8,128)(2,1)S(1)} %pad_maximum_fusion.2), channel_id=1, source_target_pairs={{0,1},{1,2},{2,3},{3,4},{4,5},{5,6},{6,7},{7,8},{8,9},{9,10},{10,1... | collective-permute-start | bytes 215432 | tf_op jit(solution)/shard_map/ppermute | solution.py:25
  669.1 4.6 copy-start.5
  705.3 200.9 %copy-start.1 = (bf16[3,3,3,64,128]{4,3,2,1,0:T(8,128)(2,1)S(1)}, bf16[3,3,3,64,128]{4,3,2,1,0:T(8,128)(2,1)}, u32[]{:S(2)}) copy-start(bf16[3,3,3,64,128]{4,3,2,1,0:T(8,128)(2,1)} %param.9) | copy-start | bytes 1327108
Sparse Core Ops, SparseCore 0:
  705.4 155.8 all-reduce.3
where the time goes:
time: 924 us; the launch traced here: 913 us
  matrix products  552 us (60%)
  local copies, waits for them, and re-layouts  116 us (13%)
  blocking collectives  78.1 us (8%)
  starting transfers between devices  62.4 us (7%)
  other arithmetic  47.3 us (5%)
  waiting for transfers between devices  42.9 us (5%)
  between operations  15 us (2%)
    conv_general_dilated x5, matrix products, convolve(): lax.conv_general_dilated(source, kernel, strides, padding, lhs_dilation=d...  399 us
    transpose x1, matrix products, kernel_terms_first(): return jnp.moveaxis(result, 0, 3)  121 us
    psum x1, blocking collectives, body(): grad_first, second_whole = lax.psum((term_first, term_second), ('ha', 'wa'))  78.1 us
    conv_general_dilated x18, local copies, waits for them, and re-layouts, convolve(): lax.conv_general_dilated(source, kernel, strides, padding, lhs_dilation=d...  70.9 us
    transpose x1, matrix products, kernel_terms_second(): return jnp.moveaxis(result, 0, 3)  31.6 us
    ppermute x6, starting transfers between devices, padded(): before = lax.ppermute(last, axis, up)  29.4 us
    broadcast_in_dim x2, local copies, waits for them, and re-layouts, kernel_terms_first(): source[None]  28.1 us
    ppermute x6, starting transfers between devices, from_behind(): return lax.ppermute(value, axis, pairs)  24.6 us
  transfers between devices with their start and end apart: 19, of which 14 were waited for; matrix products, arithmetic and copies ran while one was open for 18% of the time, Pallas kernels for 0%

commit v1 on v0

v1 whole, which is shorter than its diff:
```python
import numpy as np
import jax
import jax.numpy as jnp
from jax import lax
from jax.experimental import pallas as pl
from jax.experimental.pallas import tpu as pltpu
from jax.sharding import PartitionSpec as P

LEAK = 0.2
T = 17
TO = 9
S = 24
F32 = jnp.float32
BF16 = jnp.bfloat16


def dot(a, b):
    return jnp.dot(a, b, preferred_element_type=F32)


def pick_columns():
    m = np.zeros((4, S, 48), np.float32)
    for d in range(4):
        for s in range(22):
            if 2 * s + d < 44:
                m[d, s, 2 * s + d] = 1
    return m.reshape(4 * S, 48)


def spread_rows():
    m = np.zeros((4, 144, 11, 2, 64), np.float32)
    for d in range(4):
        for q in range(22):
            for k in range(4):
                for ch in range(3):
                    if 2 * q + k < 44:
                        m[d, ch * 48 + 2 * q + k, q // 2, q % 2, k * 12 + d * 3 + ch] = 1
    return m.reshape(4, 144, 11 * 128)


def first_forward():
    m = np.zeros((3, 128, 2, 4, 81), np.float32)
    for a in range(3):
        for k in range(4):
            for d in range(4):
                for ch in range(3):
                    for rp in range(2):
                        for cp in range(2):
                            b, c = k - rp, d - cp
                            if 0 <= b < 3 and 0 <= c < 3:
                                tap = ((a * 3 + b) * 3 + c) * 3 + ch
                                lane = k * 12 + d * 3 + ch
                                m[a, lane, 0, rp * 2 + cp, tap] = 1
                                m[a, 64 + lane, 1, rp * 2 + cp, tap] = 1
    return m.reshape(384, 2, 4 * 81)


def first_backward():
    m = np.zeros((2, 2, 2, 2, 81, 128), np.float32)
    for di in range(2):
        for dj in range(2):
            for rp in range(2):
                for cp in range(2):
                    for ro in range(2):
                        for co in range(2):
                            b, c = ro + 2 - (2 * di + rp), co + 2 - (2 * dj + cp)
                            if 0 <= b < 3 and 0 <= c < 3:
                                for a in range(3):
                                    for ch in range(3):
                                        tap = ((a * 3 + b) * 3 + c) * 3 + ch
                                        m[di, dj, rp, cp, tap, a * 24 + ro * 12 + co * 3 + ch] = 1
    return m.reshape(16, 81, 128)


BLOCKS = ((1, 1), (1, 2), (2, 1), (2, 2), None, (1, 0), None, (2, 0), (0, 1), (0, 2), None, (0, 0))


def kernel(
    pos, clip, up, sel, spread, w1, b1, w2, b2, wb, wx,
    x_out, g_out,
    ct, p2, mk, sl, hf, h6, dacc, sdf, d4, dt, hdf, hd4, hds, ys, xf, tp, tpt, thf, th6, oacc, gacc, gf,
):
    r0, c0, rows, cols = pos[0], pos[1], pos[2], pos[3]

    def inside(r, c):
        return (r >= 0) & (r < rows) & (c >= 0) & (c < cols)

    sub = lax.broadcasted_iota(jnp.int32, (S, 256), 0)
    lane = lax.broadcasted_iota(jnp.int32, (S, 256), 1)
    for q in range(22):
        r = r0 + 2 * (q - 3) + (lane >> 7)
        c = c0 + 2 * (sub - 3) + ((lane >> 6) & 1)
        mk[q * S : (q + 1) * S, :] = jnp.where(inside(r, c), 1.0, 0.0)

    p2[0] = jnp.zeros(p2.shape[1:], F32)
    p2[T + 1] = jnp.zeros(p2.shape[1:], F32)
    ys[0] = jnp.zeros(ys.shape[1:], F32)
    ys[T + 1] = jnp.zeros(ys.shape[1:], F32)
    tp[0] = jnp.zeros(tp.shape[1:], BF16)
    tp[T + 1] = jnp.zeros(tp.shape[1:], BF16)
    tpt[0] = jnp.zeros(tpt.shape[1:], BF16)
    tpt[T + 1] = jnp.zeros(tpt.shape[1:], BF16)
    oacc[...] = jnp.zeros(oacc.shape, F32)
    gacc[...] = jnp.zeros(gacc.shape, F32)
    sdf[480:496, :] = jnp.zeros((16, 128), F32)
    xf[432:448, :] = jnp.zeros((16, 128), F32)
    gf[...] = jnp.zeros(gf.shape, F32)

    @pl.loop(0, T)
    def _(t):
        whole = jnp.concatenate([clip[0, t], clip[1, t], clip[2, t]], axis=0)
        turned = lax.dot_general(
            sel[...], whole, (((1,), (1,)), ((), ())), preferred_element_type=F32
        )
        at = pl.ds(pl.multiple_of(t * S, 8), S)
        for d in range(4):
            ct[d, at, :] = turned[d * S : (d + 1) * S]

    for n in range(0, 11, 2):
        width = min(2, 11 - n) * 128
        part = jnp.zeros((T * S, width), F32)
        for d in range(4):
            part += dot(ct[d].astype(BF16), spread[d, :, n * 128 : n * 128 + width])
        for k in range(width // 128):
            q = n + k
            p2[1 : T + 1, q * S : (q + 1) * S, :] = part[:, k * 128 : (k + 1) * 128].reshape(T, S, 128)

    for p in range(TO):
        dacc[p] = jnp.broadcast_to(b2[...], (480, 128))

    def forward(t):
        lhs = jnp.concatenate([p2[t], p2[t + 1], p2[t + 2]], axis=1).astype(BF16)
        pre = dot(lhs, w1[...]) + b1[...]
        slope = jnp.where(pre > 0, 1.0, LEAK)
        for q in range(11):
            for e in range(2):
                to = slice((2 * q + e) * S, (2 * q + e + 1) * S)
                of = (slice(q * S, (q + 1) * S), slice(e * 256, (e + 1) * 256))
                masked = slope[of] * mk[to, :]
                sl[t, to, :] = masked
                hf[to, :] = pre[of] * masked
        h6[:, 0:256] = hf[25:505, :].astype(BF16)
        h6[:, 256:512] = hf[24:504, :].astype(BF16)
        h6[:, 512:640] = hf[1:481, 128:256].astype(BF16)
        h6[:, 640:768] = hf[0:480, 128:256].astype(BF16)

    def even_forward(p):
        forward(2 * p)
        dacc[p] += dot(h6[...], w2[:, 256:384])

    @pl.loop(0, TO - 1)
    def _(p):
        even_forward(p)
        forward(2 * p + 1)
        both = dot(h6[...], w2[:, 0:256])
        dacc[p] += both[:, 0:128]
        dacc[p + 1] += both[:, 128:256]

    even_forward(TO - 1)

    at384 = lax.broadcasted_iota(jnp.int32, (384, 128), 0)
    core = jnp.where(at384 % S < 16, 1.0, 0.0)

    @pl.loop(0, TO)
    def _(p):
        slope = jnp.where(dacc[p] > 0, 1.0, LEAK)
        sdf[0:480, :] = up[p].astype(F32) * slope
        d4[p, :, 0:128] = sdf[0:464, :].astype(BF16)
        d4[p, :, 128:256] = sdf[1:465, :].astype(BF16)
        d4[p, :, 256:384] = sdf[24:488, :].astype(BF16)
        d4[p, :, 384:512] = sdf[25:489, :].astype(BF16)
        dt[p] = jnp.transpose(sdf[50:434, :] * core).astype(BF16)

    at416 = lax.broadcasted_iota(jnp.int32, (416, 256), 0)
    core_first = jnp.where(
        (at416 % S >= 1) & (at416 % S <= 16) & (at416 >= S) & (at416 < 17 * S), 1.0, 0.0
    )

    def backward(t, back):
        hdf[...] = back * sl[t, 25:489, :]
        hds[t] = (hdf[25:441, :] * core_first).astype(BF16)
        hd4[:, 0:256] = hdf[0:432, :].astype(BF16)
        hd4[:, 256:512] = hdf[1:433, :].astype(BF16)
        hd4[:, 512:768] = hdf[24:456, :].astype(BF16)
        hd4[:, 768:1024] = hdf[25:457, :].astype(BF16)
        ys[t + 1] = dot(hd4[...], wx[...])

    @pl.loop(0, TO - 1)
    def _(p):
        backward(2 * p, dot(d4[p], wb[0:512, :]))
        backward(2 * p + 1, dot(d4[p], wb[512:1024, :]) + dot(d4[p + 1], wb[1024:1536, :]))

    backward(2 * TO - 2, dot(d4[TO - 1], wb[0:512, :]))

    at432 = lax.broadcasted_iota(jnp.int32, (432, 128), 0)
    lane = lax.broadcasted_iota(jnp.int32, (432, 128), 1)
    second_row = lane >= 12
    in_row = jnp.where(second_row, lane - 12, lane)
    r = r0 + 2 * (at432 // S) - 3 + jnp.where(second_row, 1, 0)
    c = c0 + 2 * (at432 % S) - 3 + jnp.where(in_row >= 3, 1, 0)
    live = inside(r, c) & (in_row < 6)

    @pl.loop(0, T)
    def _(t):
        x = ys[t + 2] + pltpu.roll(ys[t + 1], 104, 1) + pltpu.roll(ys[t], 80, 1)
        x_out[t] = x[:, 0:S]
        xf[0:432, :] = jnp.where(live, x, 0.0)
        wide = (
            xf[0:416, :]
            + pltpu.roll(xf[1:417, :], 6, 1)
            + pltpu.roll(xf[24:440, :], 24, 1)
            + pltpu.roll(xf[25:441, :], 30, 1)
        )
        tp[t + 1] = wide.astype(BF16)
        tpt[t + 1] = jnp.transpose(wide)[0:48].astype(BF16)

    def tangents(t):
        lhs = jnp.concatenate([tp[t], tp[t + 1], tp[t + 2]], axis=1)
        thf[...] = dot(lhs, w1[:, 0:256]) * sl[t, 50:466, :]
        th6[:, 0:256] = thf[25:409, :].astype(BF16)
        th6[:, 256:512] = thf[24:408, :].astype(BF16)
        th6[:, 512:640] = thf[1:385, 128:256].astype(BF16)
        th6[:, 640:768] = thf[0:384, 128:256].astype(BF16)
        turned = jnp.concatenate([tpt[t], tpt[t + 1], tpt[t + 2]], axis=0)
        gacc[...] += dot(turned, hds[t])

    @pl.loop(0, TO - 1)
    def _(p):
        tangents(2 * p)
        oacc[128:256, :] += dot(dt[p], th6[...])
        tangents(2 * p + 1)
        oacc[256:384, :] += dot(dt[p], th6[...])
        oacc[0:128, :] += dot(dt[p + 1], th6[...])

    tangents(2 * TO - 2)
    oacc[128:256, :] += dot(dt[TO - 1], th6[...])

    for a in range(3):
        for b in range(3):
            total = jnp.zeros((9, 64), F32)
            for rp in range(2):
                for cp in range(2):
                    start = a * 48 + (b + rp) * 12 + cp * 3
                    part = (rp * 2 + cp) * 64
                    total += gacc[start : start + 9, part : part + 64]
            gf[a * 27 + b * 9 : a * 27 + b * 9 + 9, :] = total
    flat = jnp.concatenate([gf[k * 8 : (k + 1) * 8, :] for k in range(12)], axis=1)
    for w in range(16):
        for a in range(3):
            g_out[w, a * 8 : (a + 1) * 8, :] = oacc[a * 128 + w * 8 : a * 128 + w * 8 + 8, :]
        g_out[w, 24:32, :] = flat


def run_kernel(*args):
    vm = lambda shape, kind=F32: pltpu.VMEM(shape, kind)
    vmem = pl.BlockSpec(memory_space=pltpu.VMEM)
    return pl.pallas_call(
        kernel,
        out_shape=(
            jax.ShapeDtypeStruct((T, 432, S), F32),
            jax.ShapeDtypeStruct((16, 32, 768), F32),
        ),
        in_specs=[pl.BlockSpec(memory_space=pltpu.SMEM)] + [vmem] * 10,
        out_specs=(vmem, vmem),
        scratch_shapes=[
            vm((4, T * S, 144)),
            vm((T + 2, 264, 128)),
            vm((528, 256)),
            vm((T, 528, 256)),
            vm((528, 256)),
            vm((480, 768), BF16),
            vm((TO, 480, 128)),
            vm((496, 128)),
            vm((TO, 464, 512), BF16),
            vm((TO, 128, 384), BF16),
            vm((464, 256)),
            vm((432, 1024), BF16),
            vm((T, 416, 256), BF16),
            vm((T + 2, 432, 128)),
            vm((448, 128)),
            vm((T + 2, 416, 128), BF16),
            vm((T + 2, 48, 416), BF16),
            vm((416, 256)),
            vm((384, 768), BF16),
            vm((384, 768)),
            vm((144, 256)),
            vm((96, 64)),
        ],
        compiler_params=pltpu.CompilerParams(vmem_limit_bytes=60 * 1024 * 1024),
        cost_estimate=pl.CostEstimate(flops=10**10, bytes_accessed=2 * 10**7, transcendentals=0),
    )(*args)


def shifted(value, axis, by):
    size = lax.axis_size(axis)
    pairs = [(i, i + by) for i in range(size) if 0 <= i + by < size]
    return lax.ppermute(value, axis, pairs)


def around(value, axis, dim, before, after):
    length = value.shape[dim]
    low = shifted(lax.slice_in_dim(value, length - before, length, axis=dim), axis, 1)
    high = shifted(lax.slice_in_dim(value, 0, after, axis=dim), axis, -1)
    return jnp.concatenate([low, value, high], axis=dim)


def body(clip, w_first, b_first, w_second, b_second, upstream):
    rows = clip.shape[2] * lax.axis_size("ha")
    cols = clip.shape[3] * lax.axis_size("wa")
    ha, wa = lax.axis_index("ha"), lax.axis_index("wa")
    pos = jnp.stack([ha * 32, wa * 32, jnp.int32(rows), jnp.int32(cols)]).astype(jnp.int32)

    clip_ext = around(around(clip, "ha", 2, 7, 5), "wa", 3, 7, 5)
    clip_ext = jnp.pad(clip_ext, ((0, 0), (0, 0), (0, 4), (0, 4)))
    up = around(around(upstream, "ha", 1, 2, 2), "wa", 2, 2, 2)
    up = jnp.pad(up, ((0, 0), (0, 0), (0, 4), (0, 0))).reshape(TO, 480, 128)

    w_flat = w_first.reshape(81, 64)
    diagonal = jnp.concatenate(
        [jnp.pad(w_flat, ((0, 0), (64 * k, 192 - 64 * k))) for k in range(4)], axis=0
    )
    forward_pick = jnp.asarray(first_forward(), BF16)
    w1 = jnp.concatenate(
        [dot(forward_pick[:, e], diagonal).astype(BF16) for e in range(2)], axis=1
    )
    b1 = jnp.tile(b_first, 8)[None]
    wx = jnp.einsum(
        "ko,bkl->bol", w_flat, jnp.asarray(first_backward(), BF16), preferred_element_type=F32
    )
    wx = wx.astype(BF16).reshape(1024, 128)
    nothing = jnp.zeros((64, 128), BF16)
    w2 = jnp.concatenate(
        [
            jnp.concatenate(
                [nothing if k is None else w_second[a, k[0], k[1]] for k in BLOCKS], axis=0
            )
            for a in (2, 0, 1)
        ],
        axis=1,
    )
    turned = jnp.swapaxes(w_second, 3, 4)
    blank = jnp.zeros((128, 64), BF16)
    pieces = []
    for a in (1, 2, 0):
        for dq in range(2):
            for ds in range(2):
                line = []
                for rp in range(2):
                    for cp in range(2):
                        b, c = rp + 1 - 2 * dq, cp + 1 - 2 * ds
                        line.append(turned[a, b, c] if b >= 0 and c >= 0 else blank)
                pieces.append(jnp.concatenate(line, axis=1))
    wb = jnp.concatenate(pieces, axis=0)

    x_out, g_out = run_kernel(
        pos,
        clip_ext,
        up,
        jnp.asarray(pick_columns(), BF16),
        jnp.asarray(spread_rows(), BF16),
        w1,
        b1,
        w2,
        b_second[None],
        wb,
        wx,
    )

    scale = 1.0 / (T * rows * cols)
    size_w, size_h = lax.axis_size("wa"), lax.axis_size("ha")
    part = lax.all_to_all(g_out.astype(BF16), "wa", 0, 0, tiled=True)
    part = part.astype(F32).sum(0) * scale
    second = part[0:24].reshape(3, 8, 12, 8, 8)
    keep = [BLOCKS.index((b, c)) for b in range(3) for c in range(3)]
    second = jnp.stack([second[:, :, k] for k in keep], axis=0)
    second = second.transpose(3, 0, 1, 2, 4).reshape(8, 9 * 3 * 8 * 8)
    first = jnp.broadcast_to(part[24:32].reshape(1, 6144), (8, 6144))
    both = lax.all_to_all(jnp.concatenate([second, first], axis=1), "ha", 0, 0, tiled=True).sum(0)
    grad_second = both[:1728].reshape(3, 3, 3, 8, 8).transpose(2, 0, 1, 4, 3)
    grad_first = both[1728:].reshape(8, 12, 64).transpose(1, 0, 2).reshape(96, 64)[:81]
    grad_first = grad_first.reshape(3, 3, 3, 3, 64)

    x = x_out.reshape(T, 18, S, 2, 12)[:, :, :, :, :6].reshape(T, 18, S, 2, 2, 3)
    x = x.transpose(5, 0, 1, 3, 2, 4).reshape(3, T, 36, 48)
    input_grad = x[:, :, 3:35, 3:35]
    return (input_grad, grad_first, grad_second)


def solution(mesh):
    placed = (P(None, None, "ha", "wa"), P(), P(), P(), P(), P(None, "ha", "wa", None))
    return jax.shard_map(
        body,
        mesh=mesh,
        in_specs=placed,
        out_specs=(P(None, None, "ha", "wa"), P(), P(None, None, None, "ha", "wa")),
        check_vma=False,
    )
```

time: 924 us -> 162 us (0.18)
  matrix products: 552 us -> 3.64 us
  local copies, waits for them, and re-layouts: 116 us -> 32.8 us
  Pallas kernels: 0 us -> 53.5 us
  blocking collectives: 78.1 us -> 25.8 us
  waiting for transfers between devices: 42.9 us -> 1.71 us
  other arithmetic: 47.3 us -> 8.86 us
  starting transfers between devices: 62.4 us -> 32.9 us
  between operations: 15 us -> 1.27 us
    conv_general_dilated x5 -> x0, matrix products: 399 us -> none  [convolve(): lax.conv_general_dilated(source, kernel, strides, padding, lhs_dilation=d...]
    transpose x2 -> x0, matrix products: 153 us -> none  [the longest x1 121 us: kernel_terms_first(): return jnp.moveaxis(result, 0, 3)]
    psum x1 -> x0, blocking collectives: 78.1 us -> none  [body(): grad_first, second_whole = lax.psum((term_first, term_second), ('ha', 'wa'))]
    conv_general_dilated x18 -> x0, local copies, waits for them, and re-layouts: 70.9 us -> none  [convolve(): lax.conv_general_dilated(source, kernel, strides, padding, lhs_dilation=d...]
    pallas_call x0 -> x1, Pallas kernels: none -> 53.5 us  [run_kernel(): pl.pallas_call(kernel, out_shape=(jax.ShapeDtypeStruct((T, 432, S), F32),...]
    ppermute x18 -> x8, waiting for transfers between devices: 42.9 us -> 1.7 us  [shifted(): return lax.ppermute(value, axis, pairs)]
    ppermute x18 -> x8, starting transfers between devices: 62.4 us -> 21.3 us  [shifted(): return lax.ppermute(value, axis, pairs)]
    broadcast_in_dim x7 -> x2, local copies, waits for them, and re-layouts: 35.8 us -> 0.01 us  [the longest x1 0.01 us: body(): blank = jnp.zeros((128, 64), BF16)]
  transfers between devices with their start and end apart: 19 -> 9, of which waited for: 14 -> 1; matrix products, arithmetic and copies ran while one was open for 18% -> 21% of each run, Pallas kernels for 0% -> 0%
where the time goes in v1:
time: 162 us; the launch traced here: 160 us
  Pallas kernels  53.5 us (33%)
  starting transfers between devices  32.9 us (20%)
  local copies, waits for them, and re-layouts  32.8 us (20%)
  blocking collectives  25.8 us (16%)
  other arithmetic  8.86 us (5%)
  matrix products  3.64 us (2%)
  waiting for transfers between devices  1.71 us (1%)
    pallas_call x1, Pallas kernels, run_kernel(): pl.pallas_call(kernel, out_shape=(jax.ShapeDtypeStruct((T, 432, S), F32),...  53.5 us
    all_to_all x1, blocking collectives, body(): part = lax.all_to_all(g_out.astype(BF16), 'wa', 0, 0, tiled=True)  25.8 us
    ppermute x8, starting transfers between devices, shifted(): return lax.ppermute(value, axis, pairs)  21.3 us
    all_to_all x1, starting transfers between devices, body(): lax.all_to_all(jnp.concatenate([second, first], axis=1), 'ha', 0, 0, tile...  11.6 us
    unnamed x59, local copies, waits for them, and re-layouts  7.34 us
    transpose x1, local copies, waits for them, and re-layouts, body(): x = x.transpose(5, 0, 1, 3, 2, 4).reshape(3, T, 36, 48)  3.91 us
    concatenate x3, other arithmetic, around(): return jnp.concatenate([low, value, high], axis=dim)  3.79 us
    reshape x1, local copies, waits for them, and re-layouts, body(): x_out.reshape(T, 18, S, 2, 12)[:, :, :, :, :6].reshape(T, 18, S, 2, 2, 3)  3.58 us
  transfers between devices with their start and end apart: 9, of which 1 were waited for; matrix products, arithmetic and copies ran while one was open for 21% of the time, Pallas kernels for 0%

profile of v1, /device:TPU:0, one launch (start us, length us, event | category | flops | bytes accessed | tf_op | source)
XLA Modules:
  0.0 160.4 jit_solution(4002802498801637676)
XLA Ops:
  0.6 0.9 slice.241
  1.5 1.3 collective-permute-start.1
  2.8 0.9 slice.240
  3.8 4.6 %collective-permute-start = (bf16[3,17,7,32]{3,2,1,0:T(8,128)(2,1)S(1)}, bf16[3,17,7,32]{3,2,1,0:T(8,128)(2,1)S(1)}, u32[]{:S(2)}, u32[]{:S(2)}) collective-permute-start(bf16[3,17,7,32]{3,2,1,0:T(8,128)(2,1)S(1)} %slice.240), channel_id=1, source_target_pairs={{0,16},{16,32},{32,48},{48,64},{64,80},{80,96},{96,112},{1,17},{17... | collective-permute-start | bytes 68552 | tf_op jit(solution)/shard_map/ppermute | solution.py:297
  8.3 1.6 fusion.47
  9.9 1.3 collective-permute-start.5
  11.2 5.2 %collective-permute-start.4 = (bf16[9,2,16,128]{3,2,1,0:T(8,128)(2,1)}, bf16[9,2,16,128]{3,2,1,0:T(8,128)(2,1)}, u32[]{:S(2)}, u32[]{:S(2)}) collective-permute-start(bf16[9,2,16,128]{3,2,1,0:T(8,128)(2,1)} %get-tuple-element.46), channel_id=1, source_target_pairs={{0,16},{16,32},{32,48},{48,64},{64,80},{80,96},{96,112},{1,17},{17... | collective-permute-start | bytes 221192 | tf_op jit(solution)/shard_map/ppermute | solution.py:297
  16.4 0.7 constant_dynamic-update-slice_fusion.14
  17.1 1.5 copy.93
  18.8 1.0 convolution_convert_fusion
  19.8 1.1 fusion.33
  20.8 0.2 fusion.35
  21.3 0.3 convolution_add_fusion.5
  21.6 0.1 copy-done.6
  21.7 0.2 convolution_add_fusion.4
  22.0 0.3 fusion.12
  22.3 0.3 convolution_add_fusion.2
  22.5 0.1 copy-done.4
  22.6 0.2 convolution_add_fusion.1
  22.9 0.3 fusion.11
  23.2 0.9 pad_maximum_fusion.2.w1
  24.0 0.1 constant_dynamic-update-slice_fusion.50
  24.4 0.1 constant_dynamic-update-slice_fusion.46
  24.8 0.9 pad_maximum_fusion.1.w2
  25.7 0.1 constant_dynamic-update-slice_fusion.42
  26.1 0.9 copy-done.12
  27.0 0.3 pad_maximum_fusion
  27.3 0.2 slice.328
  27.5 0.5 copy.82
  28.0 1.4 collective-permute-start.3
  29.5 0.4 copy.81
  29.9 3.0 %collective-permute-start.2 = (bf16[3,17,44,7]{2,3,1,0:T(8,128)(2,1)S(1)}, bf16[3,17,44,7]{2,3,1,0:T(8,128)(2,1)S(1)}, u32[]{:S(2)}, u32[]{:S(2)}) collective-permute-start(bf16[3,17,44,7]{2,3,1,0:T(8,128)(2,1)S(1)} %copy.81), channel_id=1, source_target_pairs={{0,1},{1,2},{2,3},{3,4},{4,5},{5,6},{6,7},{7,8},{8,9},{9,10},{10,1... | collective-permute-start | bytes 94256 | tf_op jit(solution)/shard_map/ppermute | solution.py:297
  32.9 0.6 pad_add_fusion.pos
  33.6 0.7 broadcast_in_dim_tile.3.b1
  34.2 0.5 copy.84
  34.7 0.5 copy.83
  35.2 0.9 constant_dynamic-update-slice_fusion.2
  36.1 0.1 constant_dynamic-update-slice_fusion.1
  36.2 0.9 constant_dynamic-update-slice_fusion
  37.1 0.1 fusion.46
  37.3 3.1 %collective-permute-start.6 = (bf16[9,20,2,128]{3,2,1,0:T(2,128)(2,1)S(1)}, bf16[9,20,2,128]{3,2,1,0:T(2,128)(2,1)S(1)}, u32[]{:S(2)}, u32[]{:S(2)}) collective-permute-start(bf16[9,20,2,128]{3,2,1,0:T(2,128)(2,1)S(1)} %get-tuple-element.43), channel_id=1, source_target_pairs={{0,1},{1,2},{2,3},{3,4},{4,5},{5,6},{6,7},{7,8},{8,9},{9,10},{10,1... | collective-permute-start | bytes 276488 | tf_op jit(solution)/shard_map/ppermute | solution.py:297
  40.4 1.5 collective-permute-start.7
  41.9 1.8 %fusion.17.clip = bf16[3,17,48,48]{3,2,1,0:T(8,128)(2,1)} fusion(bf16[3,17,44,5]{3,2,1,0:T(8,128)(2,1)S(1)} %copy.84, bf16[3,17,44,7]{3,2,1,0:T(8,128)(2,1)S(1)} %copy.83, bf16[3,17,5,32]{3,2,1,0:T(8,128)(2,1)S(1)} %collective-permute-done.1, bf16[3,17,32,32]{3,2,1,0:T(8,128)(2,1)S(1)} %copy-done, bf16[3,17,7,32]{3,2,1,0:T(8,128)(2,1)S(1)} %collective-permute-done), kind=kLoop, calls=%fused_computation.28 | loop fusion | flops 2702592 | bytes 432480 | tf_op jit(solution)/shard_map/concatenate | solution.py:304
  43.7 1.7 %collective-permute-done.7 = bf16[9,20,2,128]{3,2,1,0:T(2,128)(2,1)S(1)} collective-permute-done((bf16[9,20,2,128]{3,2,1,0:T(2,128)(2,1)S(1)}, bf16[9,20,2,128]{3,2,1,0:T(2,128)(2,1)S(1)}, u32[]{:S(2)}, u32[]{:S(2)}) %collective-permute-start.7) | collective-permute-done | bytes 92192 | tf_op jit(solution)/shard_map/ppermute | solution.py:297
  45.4 1.7 %fusion.14 = bf16[9,20,24,128]{3,2,1,0:T(8,128)(2,1)} fusion(bf16[9,20,2,128]{3,2,1,0:T(2,128)(2,1)S(1)} %collective-permute-done.7, bf16[9,20,16,128]{3,2,1,0:T(8,128)(2,1)S(1)} %constant_dynamic-update-slice_fusion, bf16[9,20,2,128]{3,2,1,0:T(2,128)(2,1)S(1)} %collective-permute-done.6), kind=kLoop, calls=%fused_computation.25 | loop fusion | flops 5529600 | bytes 2027520 | tf_op jit(solution)/shard_map/concatenate | solution.py:304
  47.1 53.5 %shard_map.121 = (f32[17,432,24]{2,1,0:T(8,128)}, f32[16,32,768]{2,1,0:T(8,128)}) custom-call(s32[4]{0:T(128)} %pad_add_fusion.pos, bf16[3,17,48,48]{3,2,1,0:T(8,128)(2,1)} %fusion.17.clip, bf16[9,480,128]{2,1,0:T(8,128)(2,1)} %bitcast.204, bf16[96,48]{1,0:T(8,128)(2,1)} %constant.36.clone.sel, bf16[4,144,1408]{2,1,0:T(8,128)(2,1)} %constant.37.clone.spread, ...), custom_call_target="tpu_custom_call" | custom-call | flops 10000000000 | bytes 20000000 | tf_op jit(solution)/shard_map/pallas_call | solution.py:257
  100.6 1.5 convert_element_type.42
  102.1 25.8 %all_to_all.14 = bf16[16,32,768]{2,1,0:T(8,128)(2,1)S(1)} all-to-all(bf16[16,32,768]{2,1,0:T(8,128)(2,1)S(1)} %convert_element_type.42), channel_id=1, replica_groups=mesh['ha'=8,'wa'=16] {'wa'}, dimensions={0} | all-to-all | bytes 1572864 | tf_op jit(solution)/shard_map/all_to_all | solution.py:371
  127.8 0.1 convert_reduce_fusion
  128.0 0.6 reshape.53
  128.8 0.2 copy.106
  129.0 0.3 reshape.54
  129.4 0.9 all_to_all.10
  130.3 11.6 %all-to-all-start.1 = ((f32[8,1,7872]{2,1,0:T(1,128)}), f32[8,1,7872]{2,1,0:T(1,128)S(1)}, u32[]{:S(2)}, u32[]{:S(2)}) async-start(f32[8,1,7872]{2,1,0:T(1,128)} %all_to_all.10), calls=%async_computation.1 | async-start | bytes 507904 | tf_op jit(solution)/shard_map/all_to_all | solution.py:378
  141.9 3.0 %copy.95 = f32[17,432,24]{1,2,0:T(8,128)S(1)} copy(f32[17,432,24]{2,1,0:T(8,128)} %get-tuple-element.5) | data formatting | bytes 1410048 | tf_op jit(solution)/shard_map/pallas_call | solution.py:257
  144.9 3.6 %reshape.50 = f32[17,18,24,2,12]{2,1,4,3,0:T(8,128)} reshape(f32[17,432,24]{1,2,0:T(8,128)S(1)} %copy.95) | data formatting | bytes 1410048 | tf_op jit(solution)/shard_map/reshape | solution.py:383
  148.5 1.7 %slice-done = f32[17,18,24,2,6]{2,1,4,3,0:T(8,128)S(1)} async-done(((f32[17,18,24,2,12]{2,1,4,3,0:T(8,128)}), f32[17,18,24,2,6]{2,1,4,3,0:T(8,128)S(1)}, s32[]{:S(2)}) %slice-start) | async-done | bytes 352536 | tf_op jit(solution)/shard_map/slice | solution.py:383
  150.2 1.0 copy.96
  151.2 3.9 %copy.97 = f32[3,17,18,2,24,2]{1,5,4,3,2,0:T(2,128)} copy(f32[3,17,18,2,24,2]{4,3,0,5,2,1:T(2,128)S(1)} %bitcast.199) | data formatting | bytes 705024 | tf_op jit(solution)/shard_map/transpose | solution.py:384
  155.1 1.8 %slice.360 = f32[3,17,32,32]{1,3,2,0:T(8,128)S(1)} slice(f32[3,17,36,48]{1,3,2,0:T(8,128)} %bitcast.200), slice={[0:3], [0:17], [3:35], [3:35]} | slice | bytes 417792 | tf_op jit(solution)/shard_map/slice | solution.py:385
  156.9 1.6 %copy.108 = f32[3,17,32,32]{3,2,1,0:T(8,128)} copy(f32[3,17,32,32]{1,3,2,0:T(8,128)S(1)} %slice.360) | data formatting | bytes 417792
  158.5 0.2 reduce_sum.19
  158.9 0.6 reshape.57
  159.6 0.7 copy.109
  (88 shorter events, 1.9 us)
Async XLA Ops:
  1.5 25.4 %collective-permute-start.1 = (bf16[3,17,5,32]{3,2,1,0:T(8,128)(2,1)S(1)}, bf16[3,17,5,32]{3,2,1,0:T(8,128)(2,1)S(1)}, u32[]{:S(2)}, u32[]{:S(2)}) collective-permute-start(bf16[3,17,5,32]{3,2,1,0:T(8,128)(2,1)S(1)} %slice.241), channel_id=1, source_target_pairs={{16,0},{32,16},{48,32},{64,48},{80,64},{96,80},{112,96},{17,1},{33... | collective-permute-start | bytes 48968 | tf_op jit(solution)/shard_map/ppermute | solution.py:297
  3.8 23.2 %collective-permute-start = (bf16[3,17,7,32]{3,2,1,0:T(8,128)(2,1)S(1)}, bf16[3,17,7,32]{3,2,1,0:T(8,128)(2,1)S(1)}, u32[]{:S(2)}, u32[]{:S(2)}) collective-permute-start(bf16[3,17,7,32]{3,2,1,0:T(8,128)(2,1)S(1)} %slice.240), channel_id=1, source_target_pairs={{0,16},{16,32},{32,48},{48,64},{64,80},{80,96},{96,112},{1,17},{17... | collective-permute-start | bytes 68552 | tf_op jit(solution)/shard_map/ppermute | solution.py:297
  9.9 26.3 %collective-permute-start.5 = (bf16[9,2,16,128]{3,2,1,0:T(8,128)(2,1)}, bf16[9,2,16,128]{3,2,1,0:T(8,128)(2,1)}, u32[]{:S(2)}, u32[]{:S(2)}) collective-permute-start(bf16[9,2,16,128]{3,2,1,0:T(8,128)(2,1)} %get-tuple-element.45), channel_id=1, source_target_pairs={{16,0},{32,16},{48,32},{64,48},{80,64},{96,80},{112,96},{17,1},{33... | collective-permute-start | bytes 221192 | tf_op jit(solution)/shard_map/ppermute | solution.py:297
  11.2 24.0 %collective-permute-start.4 = (bf16[9,2,16,128]{3,2,1,0:T(8,128)(2,1)}, bf16[9,2,16,128]{3,2,1,0:T(8,128)(2,1)}, u32[]{:S(2)}, u32[]{:S(2)}) collective-permute-start(bf16[9,2,16,128]{3,2,1,0:T(8,128)(2,1)} %get-tuple-element.46), channel_id=1, source_target_pairs={{0,16},{16,32},{32,48},{48,64},{64,80},{80,96},{96,112},{1,17},{17... | collective-permute-start | bytes 221192 | tf_op jit(solution)/shard_map/ppermute | solution.py:297
  17.1 1.6 copy-start.11
  17.1 1.6 %copy-start.3 = (bf16[16,81,128]{2,1,0:T(8,128)(2,1)S(1)}, bf16[16,81,128]{2,1,0:T(8,128)(2,1)}, u32[]{:S(2)}) copy-start(bf16[16,81,128]{2,1,0:T(8,128)(2,1)} %constant.35.clone) | copy-start | bytes 995332
  18.6 2.2 %copy-start.10 = (bf16[384,81]{1,0:T(8,128)(2,1)S(1)}, bf16[384,81]{1,0:T(8,128)(2,1)}, u32[]{:S(2)}) copy-start(bf16[384,81]{1,0:T(8,128)(2,1)} %constant.64) | copy-start | bytes 186628
  18.6 2.4 %copy-start.1 = (bf16[3,3,3,64,128]{4,3,2,1,0:T(8,128)(2,1)S(1)}, bf16[3,3,3,64,128]{4,3,2,1,0:T(8,128)(2,1)}, u32[]{:S(2)}) copy-start(bf16[3,3,3,64,128]{4,3,2,1,0:T(8,128)(2,1)} %param.13) | copy-start | bytes 1327108
  18.8 2.6 %copy-start.7 = (bf16[384,81]{1,0:T(8,128)(2,1)S(1)}, bf16[384,81]{1,0:T(8,128)(2,1)}, u32[]{:S(2)}) copy-start(bf16[384,81]{1,0:T(8,128)(2,1)} %constant.61) | copy-start | bytes 186628
  20.8 0.9 copy-start.6
  21.1 0.9 copy-start.9
  21.3 0.9 copy-start.5
  21.7 0.9 copy-start.4
  22.0 0.9 copy-start.8
  24.3 2.6 %copy-start = (bf16[3,17,32,32]{3,2,1,0:T(8,128)(2,1)S(1)}, bf16[3,17,32,32]{3,2,1,0:T(8,128)(2,1)}, u32[]{:S(2)}) copy-start(bf16[3,17,32,32]{3,2,1,0:T(8,128)(2,1)} %param.10) | copy-start | bytes 313348
  26.1 0.9 copy-start.12
  27.2 6.3 %copy-start.13 = (f32[64]{0:T(128)S(1)}, f32[64]{0:T(128)}, u32[]{:S(2)}) copy-start(f32[64]{0:T(128)} %param.12) | copy-start | bytes 772
  28.0 8.1 %copy-start.2 = (bf16[9,16,16,128]{3,2,1,0:T(8,128)(2,1)S(1)}, bf16[9,16,16,128]{3,2,1,0:T(8,128)(2,1)}, u32[]{:S(2)}) copy-start(bf16[9,16,16,128]{3,2,1,0:T(8,128)(2,1)} %param.15) | copy-start | bytes 1769476
  28.0 6.2 %collective-permute-start.3 = (bf16[3,17,44,5]{2,0,3,1:T(4,128)(2,1)S(1)}, bf16[3,17,44,5]{2,0,3,1:T(4,128)(2,1)S(1)}, u32[]{:S(2)}, u32[]{:S(2)}) collective-permute-start(bf16[3,17,44,5]{2,0,3,1:T(4,128)(2,1)S(1)} %copy.82), channel_id=1, source_target_pairs={{1,0},{2,1},{3,2},{4,3},{5,4},{6,5},{7,6},{8,7},{9,8},{10,9},{11,1... | collective-permute-start | bytes 67328 | tf_op jit(solution)/shard_map/ppermute | solution.py:297
  29.9 4.8 %collective-permute-start.2 = (bf16[3,17,44,7]{2,3,1,0:T(8,128)(2,1)S(1)}, bf16[3,17,44,7]{2,3,1,0:T(8,128)(2,1)S(1)}, u32[]{:S(2)}, u32[]{:S(2)}) collective-permute-start(bf16[3,17,44,7]{2,3,1,0:T(8,128)(2,1)S(1)} %copy.81), channel_id=1, source_target_pairs={{0,1},{1,2},{2,3},{3,4},{4,5},{5,6},{6,7},{7,8},{8,9},{9,10},{10,1... | collective-permute-start | bytes 94256 | tf_op jit(solution)/shard_map/ppermute | solution.py:297
  37.3 6.4 %collective-permute-start.6 = (bf16[9,20,2,128]{3,2,1,0:T(2,128)(2,1)S(1)}, bf16[9,20,2,128]{3,2,1,0:T(2,128)(2,1)S(1)}, u32[]{:S(2)}, u32[]{:S(2)}) collective-permute-start(bf16[9,20,2,128]{3,2,1,0:T(2,128)(2,1)S(1)} %get-tuple-element.43), channel_id=1, source_target_pairs={{0,1},{1,2},{2,3},{3,4},{4,5},{5,6},{6,7},{7,8},{8,9},{9,10},{10,1... | collective-permute-start | bytes 276488 | tf_op jit(solution)/shard_map/ppermute | solution.py:297
  40.4 5.0 %collective-permute-start.7 = (bf16[9,20,2,128]{3,2,1,0:T(2,128)(2,1)S(1)}, bf16[9,20,2,128]{3,2,1,0:T(2,128)(2,1)S(1)}, u32[]{:S(2)}, u32[]{:S(2)}) collective-permute-start(bf16[9,20,2,128]{3,2,1,0:T(2,128)(2,1)S(1)} %get-tuple-element.44), channel_id=1, source_target_pairs={{1,0},{2,1},{3,2},{4,3},{5,4},{6,5},{7,6},{8,7},{9,8},{10,9},{11,1... | collective-permute-start | bytes 276488 | tf_op jit(solution)/shard_map/ppermute | solution.py:297
  130.3 28.2 %all-to-all-start.1 = ((f32[8,1,7872]{2,1,0:T(1,128)}), f32[8,1,7872]{2,1,0:T(1,128)S(1)}, u32[]{:S(2)}, u32[]{:S(2)}) async-start(f32[8,1,7872]{2,1,0:T(1,128)} %all_to_all.10), calls=%async_computation.1 | async-start | bytes 507904 | tf_op jit(solution)/shard_map/all_to_all | solution.py:378
  148.5 1.7 %slice-start = ((f32[17,18,24,2,12]{2,1,4,3,0:T(8,128)}), f32[17,18,24,2,6]{2,1,4,3,0:T(8,128)S(1)}, s32[]{:S(2)}) async-start(f32[17,18,24,2,12]{2,1,4,3,0:T(8,128)} %reshape.50), calls=%async_computation.2 | async-start | bytes 5013504 | tf_op jit(solution)/shard_map/slice | solution.py:383

commit v2 on v1

v2 whole, which is shorter than its diff:
```python
import numpy as np
import jax
import jax.numpy as jnp
from jax import lax
from jax.experimental import pallas as pl
from jax.experimental.pallas import tpu as pltpu
from jax.sharding import PartitionSpec as P

LEAK = 0.2
T = 17
TO = 9
S = 24
F32 = jnp.float32
BF16 = jnp.bfloat16


def dot(a, b):
    return jnp.dot(a, b, preferred_element_type=F32)


def dot_nt(a, b):
    return lax.dot_general(a, b, (((1,), (1,)), ((), ())), preferred_element_type=F32)


def pick_columns():
    m = np.zeros((4, S, 48), np.float32)
    for d in range(4):
        for s in range(22):
            m[d, s, 2 * s + d + 1] = 1
    m = m.reshape(4 * S, 48)
    return m[:, 8:40], m[:, :8], m[:, 40:]


def place_columns():
    m = np.zeros((2, 512, 18, 32), np.float32)
    for p in range(18):
        for s in range(18):
            for co in range(2):
                if 0 <= 2 * s - 3 + co < 32:
                    m[co, p * S + s, p, 2 * s - 3 + co] = 1
    return m.reshape(1024, 576)


def spread_rows():
    m = np.zeros((4, 144, 11, 2, 64), np.float32)
    for d in range(4):
        for q in range(22):
            for k in range(4):
                for ch in range(3):
                    if 2 * q + k + 1 < 48:
                        m[d, ch * 48 + 2 * q + k + 1, q // 2, q % 2, k * 12 + d * 3 + ch] = 1
    return m.reshape(4, 144, 11 * 128)


def first_forward():
    m = np.zeros((3, 128, 2, 4, 81), np.float32)
    for a in range(3):
        for k in range(4):
            for d in range(4):
                for ch in range(3):
                    for rp in range(2):
                        for cp in range(2):
                            b, c = k - rp, d - cp
                            if 0 <= b < 3 and 0 <= c < 3:
                                tap = ((a * 3 + b) * 3 + c) * 3 + ch
                                lane = k * 12 + d * 3 + ch
                                m[a, lane, 0, rp * 2 + cp, tap] = 1
                                m[a, 64 + lane, 1, rp * 2 + cp, tap] = 1
    return m.reshape(384, 2, 4 * 81)


def first_backward():
    m = np.zeros((2, 2, 2, 2, 81, 80), np.float32)
    for di in range(2):
        for dj in range(2):
            for rp in range(2):
                for cp in range(2):
                    for ro in range(2):
                        for co in range(2):
                            b, c = ro + 2 - (2 * di + rp), co + 2 - (2 * dj + cp)
                            if 0 <= b < 3 and 0 <= c < 3:
                                for a in range(3):
                                    for ch in range(3):
                                        tap = ((a * 3 + b) * 3 + c) * 3 + ch
                                        m[di, dj, rp, cp, tap, a * 24 + ro * 12 + co * 3 + ch] = 1
    return m.reshape(16, 81, 80)


BLOCKS = ((1, 1), (1, 2), (2, 1), (2, 2), None, (1, 0), None, (2, 0), (0, 1), (0, 2), None, (0, 0))


def kernel(
    pos, clip, side, up, sel_mid, sel_side, spread, w1, b1, w2, b2, wb, wx, place,
    x_out, g_out,
    ct, p2, mk, sl, hf_a, hf_b, h6_a, h6_b, dacc, sdf, d4, dt, hdf_a, hdf_b, hd4_a, hd4_b, hds, yt, xs, tp, tpt,
    thf_a, thf_b, th6_a, th6_b, oacc, gacc, gf,
):
    r0, c0, rows, cols = pos[0], pos[1], pos[2], pos[3]

    def inside(r, c):
        return (r >= 0) & (r < rows) & (c >= 0) & (c < cols)

    sub = lax.broadcasted_iota(jnp.int32, (S, 256), 0)
    lane = lax.broadcasted_iota(jnp.int32, (S, 256), 1)
    for q in range(22):
        r = r0 + 2 * (q - 3) + (lane >> 7)
        c = c0 + 2 * (sub - 3) + ((lane >> 6) & 1)
        mk[q * S : (q + 1) * S, :] = jnp.where(inside(r, c), 1.0, 0.0)

    p2[0] = jnp.zeros(p2.shape[1:], F32)
    p2[T + 1] = jnp.zeros(p2.shape[1:], F32)
    yt[...] = jnp.zeros(yt.shape, F32)
    tp[...] = jnp.zeros(tp.shape, BF16)
    tpt[0] = jnp.zeros(tpt.shape[1:], BF16)
    tpt[T + 1] = jnp.zeros(tpt.shape[1:], BF16)
    oacc[...] = jnp.zeros(oacc.shape, F32)
    gacc[...] = jnp.zeros(gacc.shape, F32)
    sdf[480:496, :] = jnp.zeros((16, 128), F32)
    gf[...] = jnp.zeros(gf.shape, F32)
    h6_b[...] = jnp.zeros(h6_b.shape, BF16)
    hd4_b[...] = jnp.zeros(hd4_b.shape, BF16)
    th6_b[...] = jnp.zeros(th6_b.shape, BF16)

    @pl.loop(0, T)
    def _(t):
        middle = jnp.concatenate([clip[0, t], clip[1, t], clip[2, t]], axis=0)
        edges = jnp.concatenate([side[0, t], side[1, t], side[2, t]], axis=1)
        turned = dot_nt(sel_mid[...], middle) + dot(sel_side[...], edges)
        at = pl.ds(pl.multiple_of(t * S, 8), S)
        for d in range(4):
            ct[d, at, :] = turned[d * S : (d + 1) * S]

    for n in range(0, 11, 2):
        width = min(2, 11 - n) * 128
        part = jnp.zeros((T * S, width), F32)
        for d in range(4):
            part += dot(ct[d].astype(BF16), spread[d, :, n * 128 : n * 128 + width])
        for k in range(width // 128):
            q = n + k
            p2[1 : T + 1, q * S : (q + 1) * S, :] = part[:, k * 128 : (k + 1) * 128].reshape(T, S, 128)

    for p in range(TO + 1):
        dacc[p] = jnp.broadcast_to(b2[...], (480, 128))

    def hidden(t, hf, h6):
        lhs = jnp.concatenate([p2[t], p2[t + 1], p2[t + 2]], axis=1).astype(BF16)
        pre = dot(lhs, w1[...]) + b1[...]
        slope = jnp.where(pre > 0, 1.0, LEAK)
        for q in range(11):
            for e in range(2):
                to = slice((2 * q + e) * S, (2 * q + e + 1) * S)
                of = (slice(q * S, (q + 1) * S), slice(e * 256, (e + 1) * 256))
                masked = slope[of] * mk[to, :]
                sl[t, to, :] = masked
                hf[to, :] = pre[of] * masked
        h6[:, 0:256] = hf[25:505, :].astype(BF16)
        h6[:, 256:512] = hf[24:504, :].astype(BF16)
        h6[:, 512:640] = hf[1:481, 128:256].astype(BF16)
        h6[:, 640:768] = hf[0:480, 128:256].astype(BF16)

    def odd_second(p):
        both = dot(h6_b[...], w2[:, 0:256])
        dacc[p + 1] += both[:, 0:128]
        dacc[p + 2] += both[:, 128:256]

    def even_second(p):
        dacc[p + 1] += dot(h6_a[...], w2[:, 256:384])

    @pl.loop(0, TO - 1)
    def _(p):
        hidden(2 * p, hf_a, h6_a)
        odd_second(p - 1)
        hidden(2 * p + 1, hf_b, h6_b)
        even_second(p)

    hidden(2 * TO - 2, hf_a, h6_a)
    odd_second(TO - 2)
    even_second(TO - 1)

    at384 = lax.broadcasted_iota(jnp.int32, (384, 128), 0)
    core = jnp.where(at384 % S < 16, 1.0, 0.0)

    @pl.loop(0, TO)
    def _(p):
        slope = jnp.where(dacc[p + 1] > 0, 1.0, LEAK)
        sdf[0:480, :] = up[p].astype(F32) * slope
        d4[p, :, 0:128] = sdf[0:464, :].astype(BF16)
        d4[p, :, 128:256] = sdf[1:465, :].astype(BF16)
        d4[p, :, 256:384] = sdf[24:488, :].astype(BF16)
        d4[p, :, 384:512] = sdf[25:489, :].astype(BF16)
        dt[p] = jnp.transpose(sdf[50:434, :] * core).astype(BF16)

    at416 = lax.broadcasted_iota(jnp.int32, (416, 256), 0)
    core_first = jnp.where(
        (at416 % S >= 1) & (at416 % S <= 16) & (at416 >= S) & (at416 < 17 * S), 1.0, 0.0
    )

    def delta(t, back, hdf, hd4):
        hdf[...] = back * sl[t, 25:489, :]
        hds[t] = (hdf[25:441, :] * core_first).astype(BF16)
        hd4[:, 0:256] = hdf[0:432, :].astype(BF16)
        hd4[:, 256:512] = hdf[1:433, :].astype(BF16)
        hd4[:, 512:768] = hdf[24:456, :].astype(BF16)
        hd4[:, 768:1024] = hdf[25:457, :].astype(BF16)

    def products(t, hd4):
        yt[t + 2, :, 0:432] = dot_nt(wx[...], hd4[...])

    @pl.loop(0, TO - 1)
    def _(p):
        delta(2 * p, dot(d4[p], wb[0:512, :]), hdf_a, hd4_a)
        products(2 * p - 1, hd4_b)
        back = dot(d4[p], wb[512:1024, :]) + dot(d4[p + 1], wb[1024:1536, :])
        delta(2 * p + 1, back, hdf_b, hd4_b)
        products(2 * p, hd4_a)

    delta(2 * TO - 2, dot(d4[TO - 1], wb[0:512, :]), hdf_a, hd4_a)
    products(2 * TO - 3, hd4_b)
    products(2 * TO - 2, hd4_a)

    index = lax.broadcasted_iota(jnp.int32, (S, 512), 0)
    cell = lax.broadcasted_iota(jnp.int32, (S, 512), 1)
    second_row = index >= 12
    in_row = jnp.where(second_row, index - 12, index)
    r = r0 + 2 * (cell // S) - 3 + jnp.where(second_row, 1, 0)
    c = c0 + 2 * (cell % S) - 3 + jnp.where(in_row >= 3, 1, 0)
    live = inside(r, c) & (in_row < 6) & (cell < 432)

    @pl.loop(0, T)
    def _(t):
        x = yt[t + 3, 0:24, :] + yt[t + 2, 24:48, :] + yt[t + 1, 48:72, :]
        at = pl.ds(pl.multiple_of(t * 48, 16), 48)
        for co in range(2):
            here = x if co == 0 else pltpu.roll(x, 21, 0)
            high = here.astype(BF16).astype(F32)
            xs[at, co * 512 : (co + 1) * 512] = jnp.concatenate([high, here - high], axis=0).astype(BF16)
        m = jnp.where(live, x, 0.0)
        upper = m + pltpu.roll(pltpu.roll(m, 511, 1), 6, 0)
        lower = pltpu.roll(m, 488, 1) + pltpu.roll(pltpu.roll(m, 487, 1), 6, 0)
        wide = jnp.concatenate([upper, lower], axis=0)
        tpt[t + 1] = wide[:, 0:416].astype(BF16)
        tp[t + 1, :, 0:48] = jnp.transpose(wide)[0:416].astype(BF16)

    for n in range(T):
        placed = dot(xs[n * 48 : (n + 1) * 48, :], place[...])
        placed = placed[0:24] + placed[24:48]
        for p in range(18):
            for ro in range(2):
                row = 2 * p - 3 + ro
                if 0 <= row < 32:
                    for ch in range(3):
                        k = ro * 12 + ch
                        x_out[ch, n, row : row + 1, :] = placed[k : k + 1, p * 32 : p * 32 + 32]

    def tangents(t, thf, th6):
        lhs = jnp.concatenate([tp[t], tp[t + 1], tp[t + 2]], axis=1)
        thf[...] = dot(lhs, w1[:, 0:256]) * sl[t, 50:466, :]
        th6[:, 0:256] = thf[25:409, :].astype(BF16)
        th6[:, 256:512] = thf[24:408, :].astype(BF16)
        th6[:, 512:640] = thf[1:385, 128:256].astype(BF16)
        th6[:, 640:768] = thf[0:384, 128:256].astype(BF16)
        turned = jnp.concatenate([tpt[t], tpt[t + 1], tpt[t + 2]], axis=0)
        gacc[...] += dot(turned, hds[t])

    def odd_terms(p):
        oacc[256:384, :] += dot(dt[jnp.maximum(p, 0)], th6_b[...])
        oacc[0:128, :] += dot(dt[p + 1], th6_b[...])

    def even_terms(p):
        oacc[128:256, :] += dot(dt[p], th6_a[...])

    @pl.loop(0, TO - 1)
    def _(p):
        tangents(2 * p, thf_a, th6_a)
        odd_terms(p - 1)
        tangents(2 * p + 1, thf_b, th6_b)
        even_terms(p)

    tangents(2 * TO - 2, thf_a, th6_a)
    odd_terms(TO - 2)
    even_terms(TO - 1)

    for a in range(3):
        for b in range(3):
            total = jnp.zeros((9, 64), F32)
            for rp in range(2):
                for cp in range(2):
                    start = a * 48 + (b + rp) * 12 + cp * 3
                    part = (rp * 2 + cp) * 64
                    total += gacc[start : start + 9, part : part + 64]
            gf[a * 27 + b * 9 : a * 27 + b * 9 + 9, :] = total

    left_half = lax.broadcasted_iota(jnp.int32, (8, 128), 1) < 64
    ends = jnp.concatenate([gf[24:56, :], gf[53:85, :]], axis=1)
    ends = jnp.concatenate([ends, jnp.zeros((8, 128), F32)], axis=0)
    start = jnp.concatenate([gf[0:24, :], jnp.zeros((24, 64), F32)], axis=1)
    for w in range(16):
        tiles = [[oacc[a * 128 + w * 8 : a * 128 + w * 8 + 8, k * 128 : k * 128 + 128] for a in range(3)] for k in range(6)]
        mixed = [jnp.where(left_half, pltpu.roll(tiles[2][a], 64, 1), tiles[3][a]) for a in range(3)]
        last = [jnp.where(left_half, start[a * 8 : a * 8 + 8], tiles[5][a]) for a in range(3)]
        g_out[w] = jnp.concatenate(tiles[0] + tiles[1] + mixed + tiles[4] + last + [ends], axis=0).astype(BF16)


TAPS = ((1, 1), (1, 2), (2, 1), (2, 2), (1, 0), (2, 0), (0, 1), (0, 2), None, (0, 0))


def run_kernel(*args):
    vm = lambda shape, kind=F32: pltpu.VMEM(shape, kind)
    vmem = pl.BlockSpec(memory_space=pltpu.VMEM)
    return pl.pallas_call(
        kernel,
        out_shape=(
            jax.ShapeDtypeStruct((3, T, 32, 32), F32),
            jax.ShapeDtypeStruct((16, 160, 128), BF16),
        ),
        in_specs=[pl.BlockSpec(memory_space=pltpu.SMEM)] + [vmem] * 13,
        out_specs=(vmem, vmem),
        scratch_shapes=[
            vm((4, T * S, 144)),
            vm((T + 2, 264, 128)),
            vm((528, 256)),
            vm((T, 528, 256)),
            vm((528, 256)),
            vm((528, 256)),
            vm((480, 768), BF16),
            vm((480, 768), BF16),
            vm((TO + 1, 480, 128)),
            vm((496, 128)),
            vm((TO, 464, 512), BF16),
            vm((TO, 128, 384), BF16),
            vm((464, 256)),
            vm((464, 256)),
            vm((432, 1024), BF16),
            vm((432, 1024), BF16),
            vm((T, 416, 256), BF16),
            vm((T + 3, 80, 512)),
            vm((T * 48, 1024), BF16),
            vm((T + 2, 416, 128), BF16),
            vm((T + 2, 48, 416), BF16),
            vm((416, 256)),
            vm((416, 256)),
            vm((384, 768), BF16),
            vm((384, 768), BF16),
            vm((384, 768)),
            vm((144, 256)),
            vm((96, 64)),
        ],
        compiler_params=pltpu.CompilerParams(vmem_limit_bytes=60 * 1024 * 1024),
        cost_estimate=pl.CostEstimate(flops=10**10, bytes_accessed=2 * 10**7, transcendentals=0),
    )(*args)


def swapped(to_next, to_prev, axis):
    size, at = lax.axis_size(axis), lax.axis_index(axis)
    ring = [(i, (i + 1) % size) for i in range(size)]
    before = lax.ppermute(to_next, axis, ring)
    after = lax.ppermute(to_prev, axis, [(j, i) for i, j in ring])
    nothing = jnp.zeros_like(before)
    return jnp.where(at > 0, before, nothing), jnp.where(at < size - 1, after, nothing)


def packed(clip_part, up_part):
    flat = clip_part.reshape(408, clip_part.shape[3])
    flat = jnp.pad(flat, ((0, 0), (0, 128 - flat.shape[1])))
    return jnp.concatenate([flat, up_part.reshape(-1, 128)], axis=0)


def body(clip, w_first, b_first, w_second, b_second, upstream):
    rows = clip.shape[2] * lax.axis_size("ha")
    cols = clip.shape[3] * lax.axis_size("wa")
    ha, wa = lax.axis_index("ha"), lax.axis_index("wa")
    pos = jnp.stack([ha * 32, wa * 32, jnp.int32(rows), jnp.int32(cols)]).astype(jnp.int32)

    above, below = swapped(
        packed(clip[:, :, 24:32], upstream[:, 14:16]), packed(clip[:, :, 0:8], upstream[:, 0:2]), "ha"
    )
    clip_part = lambda v, width: v[:408, :width].reshape(3, T, 8, width)
    clip_rows = jnp.concatenate([clip_part(above, 32), clip, clip_part(below, 32)], axis=2)
    up_part = lambda v: v[408:].reshape(TO, 2, 16, 128)
    up_rows = jnp.concatenate([up_part(above), upstream, up_part(below)], axis=1)
    left, right = swapped(
        packed(jnp.swapaxes(clip_rows[:, :, :, 24:32], 2, 3), up_rows[:, :, 14:16]),
        packed(jnp.swapaxes(clip_rows[:, :, :, 0:8], 2, 3), up_rows[:, :, 0:2]),
        "wa",
    )
    side = jnp.concatenate([clip_part(left, 48), clip_part(right, 48)], axis=2)
    up_part = lambda v: v[408:].reshape(TO, 20, 2, 128)
    spare = jnp.zeros((TO, 20, 4, 128), BF16)
    up = jnp.concatenate([up_part(left), up_rows, up_part(right), spare], axis=2).reshape(TO, 480, 128)

    w_flat = w_first.reshape(81, 64)
    diagonal = jnp.concatenate(
        [jnp.pad(w_flat, ((0, 0), (64 * k, 192 - 64 * k))) for k in range(4)], axis=0
    )
    forward_pick = jnp.asarray(first_forward(), BF16)
    w1 = jnp.concatenate(
        [dot(forward_pick[:, e], diagonal).astype(BF16) for e in range(2)], axis=1
    )
    b1 = jnp.tile(b_first, 8)[None]
    wx = jnp.einsum(
        "ko,bkl->lbo", w_flat, jnp.asarray(first_backward(), BF16), preferred_element_type=F32
    )
    wx = wx.astype(BF16).reshape(80, 1024)
    nothing = jnp.zeros((64, 128), BF16)
    w2 = jnp.concatenate(
        [
            jnp.concatenate(
                [nothing if k is None else w_second[a, k[0], k[1]] for k in BLOCKS], axis=0
            )
            for a in (2, 0, 1)
        ],
        axis=1,
    )
    turned = jnp.swapaxes(w_second, 3, 4)
    blank = jnp.zeros((128, 64), BF16)
    pieces = []
    for a in (1, 2, 0):
        for dq in range(2):
            for ds in range(2):
                line = []
                for rp in range(2):
                    for cp in range(2):
                        b, c = rp + 1 - 2 * dq, cp + 1 - 2 * ds
                        line.append(turned[a, b, c] if b >= 0 and c >= 0 else blank)
                pieces.append(jnp.concatenate(line, axis=1))
    wb = jnp.concatenate(pieces, axis=0)

    middle, first8, last8 = pick_columns()
    input_grad, terms = run_kernel(
        pos,
        clip_rows,
        side,
        up,
        jnp.asarray(middle, BF16),
        jnp.asarray(np.concatenate([first8, last8], axis=1), BF16),
        jnp.asarray(spread_rows(), BF16),
        w1,
        b1,
        w2,
        b_second[None],
        wb,
        wx,
        jnp.asarray(place_columns(), BF16),
    )

    scale = 1.0 / (T * rows * cols)
    part = lax.all_to_all(terms, "wa", 0, 0, tiled=True)
    part = part.astype(F32).sum(0) * scale
    second = part[0:120].reshape(120, 2, 8, 8).transpose(2, 0, 1, 3).reshape(8, 15, 128)
    first = jnp.broadcast_to(part[96:160], (8, 64, 128))
    both = lax.all_to_all(jnp.concatenate([second, first], axis=1), "ha", 0, 0, tiled=True).sum(0)
    second = both[:15].reshape(5, 3, 8, 2, 8)
    keep = [TAPS.index((b, c)) for b in range(3) for c in range(3)]
    second = second.transpose(0, 3, 1, 4, 2).reshape(10, 3, 8, 8)
    grad_second = jnp.stack([second[k] for k in keep], axis=1).reshape(3, 3, 3, 8, 8)
    first = both[15:]
    grad_first = jnp.concatenate([first[0:24, 0:64], first[24:53, 0:64], first[24:53, 64:128]], axis=0)
    grad_first = grad_first[:81].reshape(3, 3, 3, 3, 64)
    return (input_grad, grad_first, grad_second)


def solution(mesh):
    placed = (P(None, None, "ha", "wa"), P(), P(), P(), P(), P(None, "ha", "wa", None))
    return jax.shard_map(
        body,
        mesh=mesh,
        in_specs=placed,
        out_specs=(P(None, None, "ha", "wa"), P(), P(None, None, None, "ha", "wa")),
        check_vma=False,
    )
```

time: 162 us -> 121 us (0.75)
  starting transfers between devices: 32.9 us -> 9.26 us
  local copies, waits for them, and re-layouts: 32.8 us -> 12.3 us
  blocking collectives: 25.8 us -> 32.4 us
  Pallas kernels: 53.5 us -> 47.2 us
  waiting for transfers between devices: 1.71 us -> 7.14 us
  other arithmetic: 8.86 us -> 6.33 us
    ppermute x8 -> x4, starting transfers between devices: 21.3 us -> 9.26 us  [the longest x2 8.93 us: swapped(): after = lax.ppermute(to_prev, axis, [(j, i) for i, j in ring])]
    all_to_all x1 -> x0, starting transfers between devices: 11.6 us -> none  [body(): lax.all_to_all(jnp.concatenate([second, first], axis=1), 'ha', 0, 0, tile...]
    slice x16, local copies, waits for them, and re-layouts: 9.34 us -> 2.21 us  [the longest x1 0.99 us: body(): upstream[:, 14:16]]
    all_to_all x1 -> x2, blocking collectives: 25.8 us -> 32.4 us  [the longest x1 16.8 us: body(): lax.all_to_all(jnp.concatenate([second, first], axis=1), 'ha', 0, 0, tile...]
    pallas_call x1, Pallas kernels: 53.5 us -> 47.2 us  [run_kernel(): pl.pallas_call(kernel, out_shape=(jax.ShapeDtypeStruct((3, T, 32, 32), F3...]
    ppermute x8 -> x4, waiting for transfers between devices: 1.7 us -> 7.14 us  [the longest x2 5.12 us: swapped(): before = lax.ppermute(to_next, axis, ring)]
    unnamed x59 -> x80, local copies, waits for them, and re-layouts: 7.34 us -> 3.47 us
    pallas_call x1 -> x0, local copies, waits for them, and re-layouts: 3.02 us -> none  [run_kernel(): pl.pallas_call(kernel, out_shape=(jax.ShapeDtypeStruct((T, 432, S), F32),...]
  transfers between devices with their start and end apart: 9 -> 4, of which waited for: 1 -> 2; matrix products, arithmetic and copies ran while one was open for 21% -> 9% of each run, Pallas kernels for 0% -> 0%
where the time goes in v2:
time: 121 us; the launch traced here: 120 us
  Pallas kernels  47.2 us (39%)
  blocking collectives  32.4 us (27%)
  local copies, waits for them, and re-layouts  12.3 us (10%)
  starting transfers between devices  9.26 us (8%)
  waiting for transfers between devices  7.14 us (6%)
  other arithmetic  6.33 us (5%)
  matrix products  4 us (3%)
  between operations  1.39 us (1%)
    pallas_call x1, Pallas kernels, run_kernel(): pl.pallas_call(kernel, out_shape=(jax.ShapeDtypeStruct((3, T, 32, 32), F3...  47.2 us
    all_to_all x1, blocking collectives, body(): lax.all_to_all(jnp.concatenate([second, first], axis=1), 'ha', 0, 0, tile...  16.8 us
    all_to_all x1, blocking collectives, body(): part = lax.all_to_all(terms, 'wa', 0, 0, tiled=True)  15.6 us
    ppermute x2, starting transfers between devices, swapped(): after = lax.ppermute(to_prev, axis, [(j, i) for i, j in ring])  8.93 us
    ppermute x2, waiting for transfers between devices, swapped(): before = lax.ppermute(to_next, axis, ring)  5.12 us
    dot_general x8, matrix products, dot(): return jnp.dot(a, b, preferred_element_type=F32)  3.59 us
    unnamed x80, local copies, waits for them, and re-layouts  3.47 us
  transfers between devices with their start and end apart: 4, of which 2 were waited for; matrix products, arithmetic and copies ran while one was open for 9% of the time, Pallas kernels for 0%

profile of v2, /device:TPU:0, one launch (start us, length us, event | category | flops | bytes accessed | tf_op | source)
XLA Modules:
  0.0 120.1 jit_solution(4491844664798777167)
XLA Ops:
  0.6 1.0 fusion.34
  1.6 1.0 fusion.35
  2.6 6.8 %collective-permute-start.1 = (bf16[696,128]{1,0:T(8,128)(2,1)S(1)}, bf16[696,128]{1,0:T(8,128)(2,1)S(1)}, u32[]{:S(2)}, u32[]{:S(2)}) collective-permute-start(bf16[696,128]{1,0:T(8,128)(2,1)S(1)} %fusion.11), channel_id=1, source_target_pairs={{16,0},{32,16},{48,32},{64,48},{80,64},{96,80},{112,96},{0,112},{1... | collective-permute-start | bytes 534536 | tf_op jit(solution)/shard_map/ppermute | solution.py:357
  9.5 0.1 collective-permute-start
  9.6 0.0 copy-start.4
  9.6 0.4 copy.135
  10.1 0.7 slice_bitcast_fusion.22
  10.7 0.7 slice_bitcast_fusion.2
  11.5 0.4 convolution_convert_fusion
  11.9 1.1 fusion.21
  12.9 1.1 fusion.23
  14.4 0.3 convolution_add_fusion.5
  14.7 0.2 convolution_add_fusion.4
  14.9 0.1 copy-done.22
  15.0 0.3 fusion.3
  15.3 0.3 convolution_add_fusion.2
  15.5 0.0 copy-done.17
  15.6 0.2 convolution_add_fusion.1
  15.8 0.1 copy-done.21
  15.9 0.3 fusion.2
  16.2 0.8 pad_maximum_fusion.2.w1
  17.0 0.1 constant_dynamic-update-slice_fusion.47
  17.1 0.1 constant_dynamic-update-slice_fusion.46
  17.3 0.1 constant_dynamic-update-slice_fusion.45
  17.4 0.1 constant_dynamic-update-slice_fusion.44
  17.5 0.1 constant_dynamic-update-slice_fusion.43
  17.6 0.1 constant_dynamic-update-slice_fusion.42
  17.7 0.1 constant_dynamic-update-slice_fusion.41
  17.8 0.1 constant_dynamic-update-slice_fusion.40
  17.9 0.1 constant_dynamic-update-slice_fusion.39
  18.0 0.1 constant_dynamic-update-slice_fusion.38
  18.1 0.1 constant_dynamic-update-slice_fusion.37
  18.2 0.1 constant_dynamic-update-slice_fusion.36.wb
  18.3 0.9 copy-done.24
  19.1 0.1 pad.88.clone
  19.2 0.7 broadcast_in_dim_tile.3.b1
  19.9 0.8 copy.153.wx
  20.7 0.9 pad_maximum_fusion.1.w2
  21.8 0.1 pad_maximum_fusion.clip
  21.9 0.2 slice_bitcast_fusion.1
  22.2 0.6 copy-done
  22.7 0.2 copy.126
  23.0 0.2 copy-done.1
  23.2 0.1 pad_maximum_fusion.13
  23.4 2.1 %collective-permute-start.3 = (bf16[768,128]{1,0:T(8,128)(2,1)S(1)}, bf16[768,128]{1,0:T(8,128)(2,1)S(1)}, u32[]{:S(2)}, u32[]{:S(2)}) collective-permute-start(bf16[768,128]{1,0:T(8,128)(2,1)S(1)} %fusion.9), channel_id=1, source_target_pairs={{1,0},{2,1},{3,2},{4,3},{5,4},{6,5},{7,6},{8,7},{9,8},{10,9},{11,1... | collective-permute-start | bytes 589832 | tf_op jit(solution)/shard_map/ppermute | solution.py:357
  25.5 0.6 pad_add_fusion.pos
  26.1 0.2 copy.125
  26.4 0.3 collective-permute-start.2
  26.7 2.0 %collective-permute-done.3 = bf16[768,128]{1,0:T(8,128)(2,1)S(1)} collective-permute-done((bf16[768,128]{1,0:T(8,128)(2,1)S(1)}, bf16[768,128]{1,0:T(8,128)(2,1)S(1)}, u32[]{:S(2)}, u32[]{:S(2)}) %collective-permute-start.3) | collective-permute-done | bytes 196640 | tf_op jit(solution)/shard_map/ppermute | solution.py:357
  28.7 5.1 %collective-permute-done.2 = bf16[768,128]{1,0:T(8,128)(2,1)S(1)} collective-permute-done((bf16[768,128]{1,0:T(8,128)(2,1)S(1)}, bf16[768,128]{1,0:T(8,128)(2,1)S(1)}, u32[]{:S(2)}, u32[]{:S(2)}) %collective-permute-start.2) | collective-permute-done | bytes 196640 | tf_op jit(solution)/shard_map/ppermute | solution.py:356
  33.9 0.7 pad_maximum_fusion.4.side
  34.7 1.7 %maximum_maximum_fusion = bf16[9,20,24,128]{3,2,1,0:T(8,128)(2,1)} fusion(bf16[9,20,2,128]{3,2,1,0:T(2,128)(2,1)S(1)} %bitcast.222, bf16[9,2,16,128]{3,2,1,0:T(8,128)(2,1)S(1)} %bitcast.200, bf16[9,16,16,128]{3,2,1,0:T(8,128)(2,1)S(1)} %copy-done.1, bf16[9,2,16,128]{3,2,1,0:T(8,128)(2,1)S(1)} %bitcast.202, bf16[9,20,2,128]{3,2,1,0:T(2,128)(2,1)S(1)} %bitcast.223, ...), kind=kLoop, calls=%fused_computation.12 | loop fusion | flops 6635520 | bytes 2027568 | tf_op jit(solution)/shard_map/concatenate | solution.py:389
  36.4 47.2 %shard_map.139 = (f32[3,17,32,32]{3,2,1,0:T(8,128)}, bf16[16,160,128]{2,1,0:T(8,128)(2,1)}) custom-call(s32[4]{0:T(128)} %pad_add_fusion.pos, bf16[3,17,48,32]{3,2,1,0:T(8,128)(2,1)} %copy-done, bf16[3,17,16,48]{3,2,1,0:T(8,128)(2,1)} %pad_maximum_fusion.4.side, bf16[9,480,128]{2,1,0:T(8,128)(2,1)} %bitcast.197, bf16[96,32]{1,0:T(8,128)(2,1)} %constant.48.clone.sel_mid, ...), custom_call_target="tpu_custom_call" | custom-call | flops 10000000000 | bytes 20000000 | tf_op jit(solution)/shard_map/pallas_call | solution.py:310
  83.6 15.6 %all_to_all.10 = bf16[16,160,128]{2,1,0:T(8,128)(2,1)S(1)} all-to-all(bf16[16,160,128]{2,1,0:T(8,128)(2,1)} %get-tuple-element.6), channel_id=1, replica_groups=mesh['ha'=8,'wa'=16] {'wa'}, dimensions={0} | all-to-all | bytes 1310720 | tf_op jit(solution)/shard_map/all_to_all | solution.py:447
  99.2 0.1 convert_reduce_fusion
  99.3 0.1 copy.138
  99.4 0.5 copy.139
  99.9 1.4 %reshape.102 = f32[8,15,128]{2,1,0:T(8,128)S(1)} reshape(f32[8,120,2,8]{3,2,1,0:T(2,128)S(1)} %copy.139) | data formatting | bytes 122880 | tf_op jit(solution)/shard_map/reshape | solution.py:449
  101.4 16.8 %all_to_all.11 = f32[8,79,128]{2,1,0:T(8,128)S(1)} all-to-all(f32[8,79,128]{2,1,0:T(8,128)S(1)} %pad_maximum_fusion.3), channel_id=1, replica_groups=mesh['ha'=8,'wa'=16] {'ha'}, dimensions={0} | all-to-all | bytes 647168 | tf_op jit(solution)/shard_map/all_to_all | solution.py:451
  118.2 0.1 slice.402
  118.3 0.6 reshape.103
  119.0 0.2 reshape.104
  119.2 0.1 copy.141
  119.4 0.7 copy.142
  (105 shorter events, 0.8 us)
Async XLA Ops:
  0.6 8.9 %copy-start.2 = (bf16[3,3,3,64,128]{4,3,2,1,0:T(8,128)(2,1)S(1)}, bf16[3,3,3,64,128]{4,3,2,1,0:T(8,128)(2,1)}, u32[]{:S(2)}) copy-start(bf16[3,3,3,64,128]{4,3,2,1,0:T(8,128)(2,1)} %param.15) | copy-start | bytes 1327108
  2.6 18.9 %collective-permute-start.1 = (bf16[696,128]{1,0:T(8,128)(2,1)S(1)}, bf16[696,128]{1,0:T(8,128)(2,1)S(1)}, u32[]{:S(2)}, u32[]{:S(2)}) collective-permute-start(bf16[696,128]{1,0:T(8,128)(2,1)S(1)} %fusion.11), channel_id=1, source_target_pairs={{16,0},{32,16},{48,32},{64,48},{80,64},{96,80},{112,96},{0,112},{1... | collective-permute-start | bytes 534536 | tf_op jit(solution)/shard_map/ppermute | solution.py:357
  9.5 12.2 %collective-permute-start = (bf16[696,128]{1,0:T(8,128)(2,1)S(1)}, bf16[696,128]{1,0:T(8,128)(2,1)S(1)}, u32[]{:S(2)}, u32[]{:S(2)}) collective-permute-start(bf16[696,128]{1,0:T(8,128)(2,1)S(1)} %fusion.10), channel_id=1, source_target_pairs={{0,16},{16,32},{32,48},{48,64},{64,80},{80,96},{96,112},{112,0},{1... | collective-permute-start | bytes 534536 | tf_op jit(solution)/shard_map/ppermute | solution.py:356
  9.6 1.8 %copy-start.23 = (bf16[3,3,3,3,64]{4,3,2,1,0:T(4,128)(2,1)S(1)}, bf16[3,3,3,3,64]{4,3,2,1,0:T(4,128)(2,1)}, u32[]{:S(2)}) copy-start(bf16[3,3,3,3,64]{4,3,2,1,0:T(4,128)(2,1)} %param.13) | copy-start | bytes 31108
  9.6 1.8 %copy-start.4 = (bf16[16,81,80]{1,2,0:T(8,128)(2,1)S(1)}, bf16[16,81,80]{1,2,0:T(8,128)(2,1)}, u32[]{:S(2)}) copy-start(bf16[16,81,80]{1,2,0:T(8,128)(2,1)} %constant.17.clone) | copy-start | bytes 622084
  11.4 2.9 %copy-start.20 = (bf16[384,81]{1,0:T(8,128)(2,1)S(1)}, bf16[384,81]{1,0:T(8,128)(2,1)}, u32[]{:S(2)}) copy-start(bf16[384,81]{1,0:T(8,128)(2,1)} %constant.79) | copy-start | bytes 186628
  12.9 1.7 %copy-start.19 = (bf16[384,81]{1,0:T(8,128)(2,1)S(1)}, bf16[384,81]{1,0:T(8,128)(2,1)}, u32[]{:S(2)}) copy-start(bf16[384,81]{1,0:T(8,128)(2,1)} %constant.80) | copy-start | bytes 186628
  14.1 0.9 copy-start.22
  14.3 0.9 copy-start.18
  14.6 0.9 copy-start.17
  15.0 0.9 copy-start.21
  15.6 1.4 %copy-start.13 = (bf16[128,64]{1,0:T(8,128)(2,1)S(1)}, bf16[128,64]{1,0:T(8,128)(2,1)}, u32[]{:S(2)}) copy-start(bf16[128,64]{1,0:T(8,128)(2,1)} %get-tuple-element.36) | copy-start | bytes 49156
  15.6 1.4 %copy-start.14 = (bf16[128,64]{1,0:T(8,128)(2,1)S(1)}, bf16[128,64]{1,0:T(8,128)(2,1)}, u32[]{:S(2)}) copy-start(bf16[128,64]{1,0:T(8,128)(2,1)} %get-tuple-element.37) | copy-start | bytes 49156
  15.6 1.4 %copy-start.15 = (bf16[128,64]{1,0:T(8,128)(2,1)S(1)}, bf16[128,64]{1,0:T(8,128)(2,1)}, u32[]{:S(2)}) copy-start(bf16[128,64]{1,0:T(8,128)(2,1)} %get-tuple-element.38) | copy-start | bytes 49156
  15.6 1.4 %copy-start.16 = (bf16[128,64]{1,0:T(8,128)(2,1)S(1)}, bf16[128,64]{1,0:T(8,128)(2,1)}, u32[]{:S(2)}) copy-start(bf16[128,64]{1,0:T(8,128)(2,1)} %get-tuple-element.39) | copy-start | bytes 49156
  15.6 1.7 %copy-start.11 = (bf16[128,64]{1,0:T(8,128)(2,1)S(1)}, bf16[128,64]{1,0:T(8,128)(2,1)}, u32[]{:S(2)}) copy-start(bf16[128,64]{1,0:T(8,128)(2,1)} %get-tuple-element.32) | copy-start | bytes 49156
  15.6 1.7 %copy-start.12 = (bf16[128,64]{1,0:T(8,128)(2,1)S(1)}, bf16[128,64]{1,0:T(8,128)(2,1)}, u32[]{:S(2)}) copy-start(bf16[128,64]{1,0:T(8,128)(2,1)} %get-tuple-element.33) | copy-start | bytes 49156
  15.9 1.5 %copy-start.7 = (bf16[128,64]{1,0:T(8,128)(2,1)S(1)}, bf16[128,64]{1,0:T(8,128)(2,1)}, u32[]{:S(2)}) copy-start(bf16[128,64]{1,0:T(8,128)(2,1)} %get-tuple-element.27) | copy-start | bytes 49156
  15.9 1.5 %copy-start.8 = (bf16[128,64]{1,0:T(8,128)(2,1)S(1)}, bf16[128,64]{1,0:T(8,128)(2,1)}, u32[]{:S(2)}) copy-start(bf16[128,64]{1,0:T(8,128)(2,1)} %get-tuple-element.28) | copy-start | bytes 49156
  15.9 1.5 %copy-start.9 = (bf16[128,64]{1,0:T(8,128)(2,1)S(1)}, bf16[128,64]{1,0:T(8,128)(2,1)}, u32[]{:S(2)}) copy-start(bf16[128,64]{1,0:T(8,128)(2,1)} %get-tuple-element.29) | copy-start | bytes 49156
  15.9 1.5 %copy-start.10 = (bf16[128,64]{1,0:T(8,128)(2,1)S(1)}, bf16[128,64]{1,0:T(8,128)(2,1)}, u32[]{:S(2)}) copy-start(bf16[128,64]{1,0:T(8,128)(2,1)} %get-tuple-element.30) | copy-start | bytes 49156
  15.9 1.8 %copy-start.5 = (bf16[128,64]{1,0:T(8,128)(2,1)S(1)}, bf16[128,64]{1,0:T(8,128)(2,1)}, u32[]{:S(2)}) copy-start(bf16[128,64]{1,0:T(8,128)(2,1)} %get-tuple-element.23) | copy-start | bytes 49156
  15.9 1.8 %copy-start.6 = (bf16[128,64]{1,0:T(8,128)(2,1)S(1)}, bf16[128,64]{1,0:T(8,128)(2,1)}, u32[]{:S(2)}) copy-start(bf16[128,64]{1,0:T(8,128)(2,1)} %get-tuple-element.24) | copy-start | bytes 49156
  16.2 3.0 %copy-start.25 = (f32[64]{0:T(128)S(1)}, f32[64]{0:T(128)}, u32[]{:S(2)}) copy-start(f32[64]{0:T(128)} %param.14) | copy-start | bytes 772
  18.3 0.9 copy-start.24
  20.7 1.1 copy-start.3
  21.9 0.9 copy-start
  21.9 1.3 %copy-start.1 = (bf16[9,16,16,128]{3,2,1,0:T(8,128)(2,1)S(1)}, bf16[9,16,16,128]{3,2,1,0:T(8,128)(2,1)}, u32[]{:S(2)}) copy-start(bf16[9,16,16,128]{3,2,1,0:T(8,128)(2,1)} %param.17) | copy-start | bytes 1769476
  23.4 5.3 %collective-permute-start.3 = (bf16[768,128]{1,0:T(8,128)(2,1)S(1)}, bf16[768,128]{1,0:T(8,128)(2,1)S(1)}, u32[]{:S(2)}, u32[]{:S(2)}) collective-permute-start(bf16[768,128]{1,0:T(8,128)(2,1)S(1)} %fusion.9), channel_id=1, source_target_pairs={{1,0},{2,1},{3,2},{4,3},{5,4},{6,5},{7,6},{8,7},{9,8},{10,9},{11,1... | collective-permute-start | bytes 589832 | tf_op jit(solution)/shard_map/ppermute | solution.py:357
  26.4 7.5 %collective-permute-start.2 = (bf16[768,128]{1,0:T(8,128)(2,1)S(1)}, bf16[768,128]{1,0:T(8,128)(2,1)S(1)}, u32[]{:S(2)}, u32[]{:S(2)}) collective-permute-start(bf16[768,128]{1,0:T(8,128)(2,1)S(1)} %fusion.8), channel_id=1, source_target_pairs={{0,1},{1,2},{2,3},{3,4},{4,5},{5,6},{6,7},{7,8},{8,9},{9,10},{10,1... | collective-permute-start | bytes 589832 | tf_op jit(solution)/shard_map/ppermute | solution.py:356

commit v3 on v2

--- a/solution.py
+++ b/solution.py
@@ -90,10 +90,10 @@
 
 
 def kernel(
-    pos, clip, side, up, sel_mid, sel_side, spread, w1, b1, w2, b2, wb, wx, place,
+    pos, clip, left, right, up, sel_mid, sel_side, spread, w1, b1, w2, b2, wb, wx, place,
     x_out, g_out,
     ct, p2, mk, sl, hf_a, hf_b, h6_a, h6_b, dacc, sdf, d4, dt, hdf_a, hdf_b, hd4_a, hd4_b, hds, yt, xs, tp, tpt,
-    thf_a, thf_b, th6_a, th6_b, oacc, gacc, gf,
+    thf_a, thf_b, th6_a, th6_b, oacc, gacc, gf, strips, upf,
 ):
     r0, c0, rows, cols = pos[0], pos[1], pos[2], pos[3]
 
@@ -109,7 +109,7 @@
 
     p2[0] = jnp.zeros(p2.shape[1:], F32)
     p2[T + 1] = jnp.zeros(p2.shape[1:], F32)
-    yt[...] = jnp.zeros(yt.shape, F32)
+    yt[T + 2] = jnp.zeros(yt.shape[1:], F32)
     tp[...] = jnp.zeros(tp.shape, BF16)
     tpt[0] = jnp.zeros(tpt.shape[1:], BF16)
     tpt[T + 1] = jnp.zeros(tpt.shape[1:], BF16)
@@ -117,14 +117,26 @@
     gacc[...] = jnp.zeros(gacc.shape, F32)
     sdf[480:496, :] = jnp.zeros((16, 128), F32)
     gf[...] = jnp.zeros(gf.shape, F32)
+    upf[...] = jnp.zeros(upf.shape, F32)
+    strips[0] = jnp.where(c0 > 0, left[...].astype(F32), 0.0)
+    strips[1] = jnp.where(c0 + 32 < cols, right[...].astype(F32), 0.0)
     h6_b[...] = jnp.zeros(h6_b.shape, BF16)
     hd4_b[...] = jnp.zeros(hd4_b.shape, BF16)
+    hds[0] = jnp.zeros(hds.shape[1:], BF16)
     th6_b[...] = jnp.zeros(th6_b.shape, BF16)
 
-    @pl.loop(0, T)
+    @pl.loop(0, T, unroll=True)
     def _(t):
         middle = jnp.concatenate([clip[0, t], clip[1, t], clip[2, t]], axis=0)
-        edges = jnp.concatenate([side[0, t], side[1, t], side[2, t]], axis=1)
+        edges = jnp.concatenate(
+            [
+                jnp.concatenate(
+                    [strips[k, pl.ds(pl.multiple_of((ch * T + t) * 8, 8), 8), 0:48] for ch in range(3)], axis=1
+                )
+                for k in range(2)
+            ],
+            axis=0,
+        ).astype(BF16)
         turned = dot_nt(sel_mid[...], middle) + dot(sel_side[...], edges)
         at = pl.ds(pl.multiple_of(t * S, 8), S)
         for d in range(4):
@@ -144,7 +156,7 @@
 
     def hidden(t, hf, h6):
         lhs = jnp.concatenate([p2[t], p2[t + 1], p2[t + 2]], axis=1).astype(BF16)
-        pre = dot(lhs, w1[...]) + b1[...]
+        pre = dot(lhs, w1[...]) + jnp.concatenate([b1[...]] * 8, axis=1)
         slope = jnp.where(pre > 0, 1.0, LEAK)
         for q in range(11):
             for e in range(2):
@@ -166,7 +178,7 @@
     def even_second(p):
         dacc[p + 1] += dot(h6_a[...], w2[:, 256:384])
 
-    @pl.loop(0, TO - 1)
+    @pl.loop(0, TO - 1, unroll=True)
     def _(p):
         hidden(2 * p, hf_a, h6_a)
         odd_second(p - 1)
@@ -180,38 +192,37 @@
     at384 = lax.broadcasted_iota(jnp.int32, (384, 128), 0)
     core = jnp.where(at384 % S < 16, 1.0, 0.0)
 
-    @pl.loop(0, TO)
-    def _(p):
+    for p in range(TO):
         slope = jnp.where(dacc[p + 1] > 0, 1.0, LEAK)
-        sdf[0:480, :] = up[p].astype(F32) * slope
+        for q in range(20):
+            upf[q * S + 2 : q * S + 18, :] = up[p, q].astype(F32)
+        for s in range(2):
+            of = slice(408 + (p * 2 + s) * 20, 428 + (p * 2 + s) * 20)
+            upf[pl.ds(s, 20, stride=S), :] = strips[0, of, :]
+            upf[pl.ds(18 + s, 20, stride=S), :] = strips[1, of, :]
+        sdf[0:480, :] = upf[...] * slope
         d4[p, :, 0:128] = sdf[0:464, :].astype(BF16)
         d4[p, :, 128:256] = sdf[1:465, :].astype(BF16)
         d4[p, :, 256:384] = sdf[24:488, :].astype(BF16)
         d4[p, :, 384:512] = sdf[25:489, :].astype(BF16)
         dt[p] = jnp.transpose(sdf[50:434, :] * core).astype(BF16)
 
-    at416 = lax.broadcasted_iota(jnp.int32, (416, 256), 0)
-    core_first = jnp.where(
-        (at416 % S >= 1) & (at416 % S <= 16) & (at416 >= S) & (at416 < 17 * S), 1.0, 0.0
-    )
-
     def delta(t, back, hdf, hd4):
         hdf[...] = back * sl[t, 25:489, :]
-        hds[t] = (hdf[25:441, :] * core_first).astype(BF16)
+        hds[t + 1] = hdf[25:457, :].astype(BF16)
         hd4[:, 0:256] = hdf[0:432, :].astype(BF16)
         hd4[:, 256:512] = hdf[1:433, :].astype(BF16)
         hd4[:, 512:768] = hdf[24:456, :].astype(BF16)
-        hd4[:, 768:1024] = hdf[25:457, :].astype(BF16)
 
     def products(t, hd4):
-        yt[t + 2, :, 0:432] = dot_nt(wx[...], hd4[...])
-
-    @pl.loop(0, TO - 1)
+        yt[t + 2, :, 0:432] = dot_nt(wx[:, 0:768], hd4[...]) + dot_nt(wx[:, 768:1024], hds[t + 1])
+
+    @pl.loop(0, TO - 1, unroll=True)
     def _(p):
         delta(2 * p, dot(d4[p], wb[0:512, :]), hdf_a, hd4_a)
         products(2 * p - 1, hd4_b)
-        back = dot(d4[p], wb[512:1024, :]) + dot(d4[p + 1], wb[1024:1536, :])
-        delta(2 * p + 1, back, hdf_b, hd4_b)
+        lhs = jnp.concatenate([d4[p], d4[p + 1]], axis=1)
+        delta(2 * p + 1, dot(lhs, wb[512:1536, :]), hdf_b, hd4_b)
         products(2 * p, hd4_a)
 
     delta(2 * TO - 2, dot(d4[TO - 1], wb[0:512, :]), hdf_a, hd4_a)
@@ -225,10 +236,14 @@
     r = r0 + 2 * (cell // S) - 3 + jnp.where(second_row, 1, 0)
     c = c0 + 2 * (cell % S) - 3 + jnp.where(in_row >= 3, 1, 0)
     live = inside(r, c) & (in_row < 6) & (cell < 432)
-
-    @pl.loop(0, T)
+    cell = lax.broadcasted_iota(jnp.int32, (48, 416), 1)
+    core_first = (cell % S >= 1) & (cell % S <= 16) & (cell >= S) & (cell < 17 * S)
+    cell = lax.broadcasted_iota(jnp.int32, (S, 512), 1)
+
+    @pl.loop(0, T, unroll=True)
     def _(t):
         x = yt[t + 3, 0:24, :] + yt[t + 2, 24:48, :] + yt[t + 1, 48:72, :]
+        x = jnp.where(cell < 432, x, 0.0)
         at = pl.ds(pl.multiple_of(t * 48, 16), 48)
         for co in range(2):
             here = x if co == 0 else pltpu.roll(x, 21, 0)
@@ -238,7 +253,7 @@
         upper = m + pltpu.roll(pltpu.roll(m, 511, 1), 6, 0)
         lower = pltpu.roll(m, 488, 1) + pltpu.roll(pltpu.roll(m, 487, 1), 6, 0)
         wide = jnp.concatenate([upper, lower], axis=0)
-        tpt[t + 1] = wide[:, 0:416].astype(BF16)
+        tpt[t + 1] = jnp.where(core_first, wide[:, 0:416], 0.0).astype(BF16)
         tp[t + 1, :, 0:48] = jnp.transpose(wide)[0:416].astype(BF16)
 
     for n in range(T):
@@ -260,7 +275,7 @@
         th6[:, 512:640] = thf[1:385, 128:256].astype(BF16)
         th6[:, 640:768] = thf[0:384, 128:256].astype(BF16)
         turned = jnp.concatenate([tpt[t], tpt[t + 1], tpt[t + 2]], axis=0)
-        gacc[...] += dot(turned, hds[t])
+        gacc[...] += dot(turned, hds[t + 1, 0:416, :])
 
     def odd_terms(p):
         oacc[256:384, :] += dot(dt[jnp.maximum(p, 0)], th6_b[...])
@@ -269,7 +284,7 @@
     def even_terms(p):
         oacc[128:256, :] += dot(dt[p], th6_a[...])
 
-    @pl.loop(0, TO - 1)
+    @pl.loop(0, TO - 1, unroll=True)
     def _(p):
         tangents(2 * p, thf_a, th6_a)
         odd_terms(p - 1)
@@ -313,7 +328,7 @@
             jax.ShapeDtypeStruct((3, T, 32, 32), F32),
             jax.ShapeDtypeStruct((16, 160, 128), BF16),
         ),
-        in_specs=[pl.BlockSpec(memory_space=pltpu.SMEM)] + [vmem] * 13,
+        in_specs=[pl.BlockSpec(memory_space=pltpu.SMEM)] + [vmem] * 14,
         out_specs=(vmem, vmem),
         scratch_shapes=[
             vm((4, T * S, 144)),
@@ -330,9 +345,9 @@
             vm((TO, 128, 384), BF16),
             vm((464, 256)),
             vm((464, 256)),
-            vm((432, 1024), BF16),
-            vm((432, 1024), BF16),
-            vm((T, 416, 256), BF16),
+            vm((432, 768), BF16),
+            vm((432, 768), BF16),
+            vm((T + 1, 432, 256), BF16),
             vm((T + 3, 80, 512)),
             vm((T * 48, 1024), BF16),
             vm((T + 2, 416, 128), BF16),
@@ -344,6 +359,8 @@
             vm((384, 768)),
             vm((144, 256)),
             vm((96, 64)),
+            vm((2, 768, 128)),
+            vm((480, 128)),
         ],
         compiler_params=pltpu.CompilerParams(vmem_limit_bytes=60 * 1024 * 1024),
         cost_estimate=pl.CostEstimate(flops=10**10, bytes_accessed=2 * 10**7, transcendentals=0),
@@ -351,12 +368,9 @@
 
 
 def swapped(to_next, to_prev, axis):
-    size, at = lax.axis_size(axis), lax.axis_index(axis)
+    size = lax.axis_size(axis)
     ring = [(i, (i + 1) % size) for i in range(size)]
-    before = lax.ppermute(to_next, axis, ring)
-    after = lax.ppermute(to_prev, axis, [(j, i) for i, j in ring])
-    nothing = jnp.zeros_like(before)
-    return jnp.where(at > 0, before, nothing), jnp.where(at < size - 1, after, nothing)
+    return lax.ppermute(to_next, axis, ring), lax.ppermute(to_prev, axis, [(j, i) for i, j in ring])
 
 
 def packed(clip_part, up_part):
@@ -374,19 +388,18 @@
     above, below = swapped(
         packed(clip[:, :, 24:32], upstream[:, 14:16]), packed(clip[:, :, 0:8], upstream[:, 0:2]), "ha"
     )
+    above, below, w_second = lax.optimization_barrier((above, below, w_second))
+    above = jnp.where(ha > 0, above, jnp.zeros_like(above))
+    below = jnp.where(ha < lax.axis_size("ha") - 1, below, jnp.zeros_like(below))
     clip_part = lambda v, width: v[:408, :width].reshape(3, T, 8, width)
     clip_rows = jnp.concatenate([clip_part(above, 32), clip, clip_part(below, 32)], axis=2)
     up_part = lambda v: v[408:].reshape(TO, 2, 16, 128)
     up_rows = jnp.concatenate([up_part(above), upstream, up_part(below)], axis=1)
     left, right = swapped(
-        packed(jnp.swapaxes(clip_rows[:, :, :, 24:32], 2, 3), up_rows[:, :, 14:16]),
-        packed(jnp.swapaxes(clip_rows[:, :, :, 0:8], 2, 3), up_rows[:, :, 0:2]),
+        packed(jnp.swapaxes(clip_rows[:, :, :, 24:32], 2, 3), jnp.swapaxes(up_rows[:, :, 14:16], 1, 2)),
+        packed(jnp.swapaxes(clip_rows[:, :, :, 0:8], 2, 3), jnp.swapaxes(up_rows[:, :, 0:2], 1, 2)),
         "wa",
     )
-    side = jnp.concatenate([clip_part(left, 48), clip_part(right, 48)], axis=2)
-    up_part = lambda v: v[408:].reshape(TO, 20, 2, 128)
-    spare = jnp.zeros((TO, 20, 4, 128), BF16)
-    up = jnp.concatenate([up_part(left), up_rows, up_part(right), spare], axis=2).reshape(TO, 480, 128)
 
     w_flat = w_first.reshape(81, 64)
     diagonal = jnp.concatenate(
@@ -396,7 +409,6 @@
     w1 = jnp.concatenate(
         [dot(forward_pick[:, e], diagonal).astype(BF16) for e in range(2)], axis=1
     )
-    b1 = jnp.tile(b_first, 8)[None]
     wx = jnp.einsum(
         "ko,bkl->lbo", w_flat, jnp.asarray(first_backward(), BF16), preferred_element_type=F32
     )
@@ -429,13 +441,14 @@
     input_grad, terms = run_kernel(
         pos,
         clip_rows,
-        side,
-        up,
+        left,
+        right,
+        up_rows,
         jnp.asarray(middle, BF16),
         jnp.asarray(np.concatenate([first8, last8], axis=1), BF16),
         jnp.asarray(spread_rows(), BF16),
         w1,
-        b1,
+        b_first[None],
         w2,
         b_second[None],
         wb,
@@ -445,15 +458,21 @@
 
     scale = 1.0 / (T * rows * cols)
     part = lax.all_to_all(terms, "wa", 0, 0, tiled=True)
-    part = part.astype(F32).sum(0) * scale
-    second = part[0:120].reshape(120, 2, 8, 8).transpose(2, 0, 1, 3).reshape(8, 15, 128)
-    first = jnp.broadcast_to(part[96:160], (8, 64, 128))
-    both = lax.all_to_all(jnp.concatenate([second, first], axis=1), "ha", 0, 0, tiled=True).sum(0)
-    second = both[:15].reshape(5, 3, 8, 2, 8)
+    part = part.astype(F32).sum(0)
+    step = 1
+    while step < lax.axis_size("ha"):
+        part = part + lax.ppermute(part, "ha", [(i, i ^ step) for i in range(lax.axis_size("ha"))])
+        step *= 2
+    part = part * scale
+    lane = lax.broadcasted_iota(jnp.int32, (128, 16), 0)
+    mine = lax.broadcasted_iota(jnp.int32, (128, 16), 1)
+    pick = (lane == (mine // 8) * 64 + ha * 8 + mine % 8).astype(F32)
+    second = jnp.dot(part[0:120], pick, precision=lax.Precision.HIGHEST, preferred_element_type=F32)
+    second = second.reshape(5, 3, 8, 2, 8)
     keep = [TAPS.index((b, c)) for b in range(3) for c in range(3)]
     second = second.transpose(0, 3, 1, 4, 2).reshape(10, 3, 8, 8)
     grad_second = jnp.stack([second[k] for k in keep], axis=1).reshape(3, 3, 3, 8, 8)
-    first = both[15:]
+    first = part[96:160]
     grad_first = jnp.concatenate([first[0:24, 0:64], first[24:53, 0:64], first[24:53, 64:128]], axis=0)
     grad_first = grad_first[:81].reshape(3, 3, 3, 3, 64)
     return (input_grad, grad_first, grad_second)

time: 121 us -> 96.3 us (0.80)
  blocking collectives: 32.4 us -> 0 us
  waiting for transfers between devices: 7.14 us -> 28.3 us
  Pallas kernels: 47.2 us -> 31.7 us
  starting transfers between devices: 9.26 us -> 18.1 us
  other arithmetic: 6.33 us -> 3.86 us
  local copies, waits for them, and re-layouts: 12.3 us -> 10 us
  matrix products: 4 us -> 2.38 us
    all_to_all x2 -> x0, blocking collectives: 32.4 us -> none  [the longest x1 16.8 us: body(): lax.all_to_all(jnp.concatenate([second, first], axis=1), 'ha', 0, 0, tile...]
    pallas_call x1, Pallas kernels: 47.2 us -> 31.7 us  [run_kernel(): pl.pallas_call(kernel, out_shape=(jax.ShapeDtypeStruct((3, T, 32, 32), F3...]
    all_to_all x0 -> x1, waiting for transfers between devices: none -> 12.2 us  [body(): part = lax.all_to_all(terms, 'wa', 0, 0, tiled=True)]
    ppermute x4 -> x7, waiting for transfers between devices: 7.14 us -> 16.1 us  [the longest x3 11.3 us: body(): lax.ppermute(part, 'ha', [(i, i ^ step) for i in range(lax.axis_size('ha'...]
    ppermute x4 -> x7, starting transfers between devices: 9.26 us -> 14.5 us  [the longest x2 6.93 us: swapped(): lax.ppermute(to_prev, axis, [(j, i) for i, j in ring])]
    all_to_all x0 -> x1, starting transfers between devices: none -> 3.59 us  [body(): part = lax.all_to_all(terms, 'wa', 0, 0, tiled=True)]
    concatenate x3 -> x1, other arithmetic: 2.51 us -> 0.09 us  [body(): jnp.concatenate([up_part(above), upstream, up_part(below)], axis=1)]
    dot_general x8, matrix products: 3.59 us -> 1.77 us  [dot(): return jnp.dot(a, b, preferred_element_type=F32)]
  transfers between devices with their start and end apart: 4 -> 8, of which waited for: 2 -> 6; matrix products, arithmetic and copies ran while one was open for 9% -> 7% of each run, Pallas kernels for 0% -> 0%
where the time goes in v3:
time: 96.3 us; the launch traced here: 96 us
  Pallas kernels  31.7 us (33%)
  waiting for transfers between devices  28.3 us (29%)
  starting transfers between devices  18.1 us (19%)
  local copies, waits for them, and re-layouts  10 us (10%)
  other arithmetic  3.86 us (4%)
  matrix products  2.38 us (2%)
  between operations  1.6 us (2%)
    pallas_call x1, Pallas kernels, run_kernel(): pl.pallas_call(kernel, out_shape=(jax.ShapeDtypeStruct((3, T, 32, 32), F3...  31.7 us
    all_to_all x1, waiting for transfers between devices, body(): part = lax.all_to_all(terms, 'wa', 0, 0, tiled=True)  12.2 us
    ppermute x3, waiting for transfers between devices, body(): lax.ppermute(part, 'ha', [(i, i ^ step) for i in range(lax.axis_size('ha'...  11.3 us
    ppermute x2, starting transfers between devices, swapped(): lax.ppermute(to_prev, axis, [(j, i) for i, j in ring])  6.93 us
    ppermute x3, starting transfers between devices, body(): lax.ppermute(part, 'ha', [(i, i ^ step) for i in range(lax.axis_size('ha'...  5.25 us
    ppermute x2, waiting for transfers between devices, swapped(): lax.ppermute(to_next, axis, ring)  4.68 us
    all_to_all x1, starting transfers between devices, body(): part = lax.all_to_all(terms, 'wa', 0, 0, tiled=True)  3.59 us
    unnamed x119, local copies, waits for them, and re-layouts  3.33 us
  transfers between devices with their start and end apart: 8, of which 6 were waited for; matrix products, arithmetic and copies ran while one was open for 7% of the time, Pallas kernels for 0%

profile of v3, /device:TPU:0, one launch (start us, length us, event | category | flops | bytes accessed | tf_op | source)
XLA Modules:
  0.0 96.0 jit_solution(8065045099022129988)
XLA Ops:
  0.7 1.0 %fusion.46 = (bf16[3,17,8,32]{3,2,1,0:T(8,128)(2,1)S(1)}, bf16[3,17,8,32]{3,2,1,0:T(8,128)(2,1)S(1)}) fusion(bf16[3,17,32,32]{3,2,1,0:T(8,128)(2,1)} %param.12), kind=kLoop, calls=%fused_computation.176 | loop fusion | bytes 104448 | tf_op jit(solution)/shard_map/slice | solution.py:389
  1.7 0.9 fusion.45
  2.7 2.1 %collective-permute-start = (bf16[696,128]{1,0:T(8,128)(2,1)S(1)}, bf16[696,128]{1,0:T(8,128)(2,1)S(1)}, u32[]{:S(2)}, u32[]{:S(2)}) collective-permute-start(bf16[696,128]{1,0:T(8,128)(2,1)S(1)} %fusion.10), channel_id=1, source_target_pairs={{0,16},{16,32},{32,48},{48,64},{64,80},{80,96},{96,112},{112,0},{1... | collective-permute-start | bytes 534536 | tf_op jit(solution)/shard_map/ppermute | solution.py:373
  4.8 4.8 %collective-permute-start.1 = (bf16[696,128]{1,0:T(8,128)(2,1)S(1)}, bf16[696,128]{1,0:T(8,128)(2,1)S(1)}, u32[]{:S(2)}, u32[]{:S(2)}) collective-permute-start(bf16[696,128]{1,0:T(8,128)(2,1)S(1)} %fusion.11), channel_id=1, source_target_pairs={{16,0},{32,16},{48,32},{64,48},{80,64},{96,80},{112,96},{0,112},{1... | collective-permute-start | bytes 534536 | tf_op jit(solution)/shard_map/ppermute | solution.py:373
  9.7 0.2 fusion.25
  9.9 0.2 fusion.23
  10.0 0.4 convolution_convert_fusion
  10.4 0.8 copy.63.wx
  11.3 0.3 convolution_add_fusion.2
  11.6 0.2 convolution_add_fusion.1
  11.8 0.3 fusion.2
  12.1 0.1 copy-done.35
  12.2 0.3 convolution_add_fusion.5
  12.5 0.2 convolution_add_fusion.4
  12.7 0.3 fusion.3
  13.0 0.7 pad_add_fusion.pos
  13.6 0.8 pad_maximum_fusion.3.w1
  14.4 0.4 copy.48
  14.9 0.7 slice_bitcast_fusion.24
  15.5 0.8 slice_bitcast_fusion.4
  16.4 0.1 broadcast_select_fusion
  16.8 0.6 copy-done.4
  17.4 0.1 pad_maximum_fusion.up
  17.5 0.1 slice_bitcast_fusion.2
  17.8 0.1 copy-done.3
  17.8 0.1 pad_maximum_fusion.1.clip
  18.0 0.2 slice_bitcast_fusion
  18.2 0.2 copy-done.2
  18.4 0.4 copy-done
  18.8 0.2 copy.38
  19.2 2.1 %collective-permute-start.3 = (bf16[768,128]{1,0:T(8,128)(2,1)S(1)}, bf16[768,128]{1,0:T(8,128)(2,1)S(1)}, u32[]{:S(2)}, u32[]{:S(2)}) collective-permute-start(bf16[768,128]{1,0:T(8,128)(2,1)S(1)} %fusion.9), channel_id=1, source_target_pairs={{1,0},{2,1},{3,2},{4,3},{5,4},{6,5},{7,6},{8,7},{9,8},{10,9},{11,1... | collective-permute-start | bytes 589832 | tf_op jit(solution)/shard_map/ppermute | solution.py:373
  21.4 0.2 copy.36
  21.7 0.3 collective-permute-start.2
  22.0 0.1 constant_dynamic-update-slice_fusion.47
  22.2 0.1 constant_dynamic-update-slice_fusion.46
  22.3 0.1 constant_dynamic-update-slice_fusion.45
  22.4 0.1 constant_dynamic-update-slice_fusion.44
  22.5 0.1 constant_dynamic-update-slice_fusion.43
  22.6 0.1 constant_dynamic-update-slice_fusion.42
  22.7 0.1 constant_dynamic-update-slice_fusion.41
  22.8 0.1 constant_dynamic-update-slice_fusion.40
  23.0 0.1 constant_dynamic-update-slice_fusion.39
  23.1 0.1 constant_dynamic-update-slice_fusion.38
  23.2 0.1 constant_dynamic-update-slice_fusion.37
  23.3 0.1 constant_dynamic-update-slice_fusion.36.wb
  23.4 1.0 %pad_maximum_fusion.2.w2 = bf16[768,384]{1,0:T(8,128)(2,1)} fusion(bf16[768,128]{1,0:T(8,128)(2,1)S(1)} %get-tuple-element.50, bf16[768,128]{1,0:T(8,128)(2,1)S(1)} %get-tuple-element.51, bf16[768,128]{1,0:T(8,128)(2,1)S(1)} %get-tuple-element.49), kind=kLoop, calls=%fused_computation.16 | loop fusion | flops 1769472 | bytes 1179648 | tf_op jit(solution)/shard_map/concatenate | solution.py:417
  24.4 0.1 collective-permute-done.3.right
  24.5 4.7 %collective-permute-done.2.left = bf16[768,128]{1,0:T(8,128)(2,1)S(1)} collective-permute-done((bf16[768,128]{1,0:T(8,128)(2,1)S(1)}, bf16[768,128]{1,0:T(8,128)(2,1)S(1)}, u32[]{:S(2)}, u32[]{:S(2)}) %collective-permute-start.2) | collective-permute-done | bytes 196640 | tf_op jit(solution)/shard_map/ppermute | solution.py:373
  29.2 0.7 copy-done.45
  29.9 31.7 %shard_map.139 = (f32[3,17,32,32]{3,2,1,0:T(8,128)}, bf16[16,160,128]{2,1,0:T(8,128)(2,1)}) custom-call(s32[4]{0:T(128)} %pad_add_fusion.pos, bf16[3,17,48,32]{3,2,1,0:T(8,128)(2,1)} %copy-done, bf16[768,128]{1,0:T(8,128)(2,1)} %copy-done.45, bf16[768,128]{1,0:T(8,128)(2,1)} %copy-done.44, bf16[9,20,16,128]{3,2,1,0:T(8,128)(2,1)} %copy-done.2, ...), custom_call_target="tpu_custom_call" | custom-call | flops 10000000000 | bytes 20000000 | tf_op jit(solution)/shard_map/pallas_call | solution.py:325
  61.5 3.6 %all-to-all-start = ((bf16[16,160,128]{2,1,0:T(8,128)(2,1)}), bf16[16,160,128]{2,1,0:T(8,128)(2,1)S(1)}, u32[]{:S(2)}, u32[]{:S(2)}) async-start(bf16[16,160,128]{2,1,0:T(8,128)(2,1)} %get-tuple-element.12), calls=%async_computation | async-start | bytes 1310720 | tf_op jit(solution)/shard_map/all_to_all | solution.py:460
  65.2 12.2 %all-to-all-done = bf16[16,160,128]{2,1,0:T(8,128)(2,1)S(1)} async-done(((bf16[16,160,128]{2,1,0:T(8,128)(2,1)}), bf16[16,160,128]{2,1,0:T(8,128)(2,1)S(1)}, u32[]{:S(2)}, u32[]{:S(2)}) %all-to-all-start) | async-done | bytes 655392 | tf_op jit(solution)/shard_map/all_to_all | solution.py:460
  77.4 0.1 convert_reduce_fusion
  77.5 0.1 collective-permute-start.4
  77.6 4.4 %collective-permute-done.4 = f32[160,128]{1,0:T(8,128)S(1)} collective-permute-done((f32[160,128]{1,0:T(8,128)S(1)}, f32[160,128]{1,0:T(8,128)S(1)}, u32[]{:S(2)}, u32[]{:S(2)}) %collective-permute-start.4) | collective-permute-done | bytes 81952 | tf_op jit(solution)/shard_map/ppermute | solution.py:464
  82.0 2.6 %collective-permute-start.5 = (f32[160,128]{1,0:T(8,128)S(1)}, f32[160,128]{1,0:T(8,128)S(1)}, u32[]{:S(2)}, u32[]{:S(2)}) collective-permute-start(f32[160,128]{1,0:T(8,128)S(1)} %add.49), channel_id=1, source_target_pairs={{0,32},{16,48},{32,0},{48,16},{64,96},{80,112},{96,64},{112,80},{1... | collective-permute-start | bytes 245768 | tf_op jit(solution)/shard_map/ppermute | solution.py:464
  84.6 3.4 %collective-permute-done.5 = f32[160,128]{1,0:T(8,128)S(1)} collective-permute-done((f32[160,128]{1,0:T(8,128)S(1)}, f32[160,128]{1,0:T(8,128)S(1)}, u32[]{:S(2)}, u32[]{:S(2)}) %collective-permute-start.5) | collective-permute-done | bytes 81952 | tf_op jit(solution)/shard_map/ppermute | solution.py:464
  88.0 2.6 %collective-permute-start.6 = (f32[160,128]{1,0:T(8,128)S(1)}, f32[160,128]{1,0:T(8,128)S(1)}, u32[]{:S(2)}, u32[]{:S(2)}) collective-permute-start(f32[160,128]{1,0:T(8,128)S(1)} %add.50), channel_id=1, source_target_pairs={{0,64},{16,80},{32,96},{48,112},{64,0},{80,16},{96,32},{112,48},{1... | collective-permute-start | bytes 245768 | tf_op jit(solution)/shard_map/ppermute | solution.py:464
  90.6 3.4 %collective-permute-done.6 = f32[160,128]{1,0:T(8,128)S(1)} collective-permute-done((f32[160,128]{1,0:T(8,128)S(1)}, f32[160,128]{1,0:T(8,128)S(1)}, u32[]{:S(2)}, u32[]{:S(2)}) %collective-permute-start.6) | collective-permute-done | bytes 81952 | tf_op jit(solution)/shard_map/ppermute | solution.py:464
  94.1 0.1 slice.374
  94.2 0.2 fusion.15
  94.4 0.2 reshape.75
  94.7 0.7 copy.52
  95.3 0.6 reshape.74
  (139 shorter events, 0.8 us)
Async XLA Ops:
  0.6 9.0 %copy-start.41 = (bf16[384,81]{1,0:T(8,128)(2,1)S(1)}, bf16[384,81]{1,0:T(8,128)(2,1)}, u32[]{:S(2)}) copy-start(bf16[384,81]{1,0:T(8,128)(2,1)} %constant.111) | copy-start | bytes 186628
  0.6 9.2 %copy-start.40 = (bf16[384,81]{1,0:T(8,128)(2,1)S(1)}, bf16[384,81]{1,0:T(8,128)(2,1)}, u32[]{:S(2)}) copy-start(bf16[384,81]{1,0:T(8,128)(2,1)} %constant.107) | copy-start | bytes 186628
  0.7 9.4 %copy-start.5 = (bf16[16,81,80]{1,2,0:T(8,128)(2,1)S(1)}, bf16[16,81,80]{1,2,0:T(8,128)(2,1)}, u32[]{:S(2)}) copy-start(bf16[16,81,80]{1,2,0:T(8,128)(2,1)} %constant.76.clone) | copy-start | bytes 622084
  0.7 9.0 %copy-start.42 = (bf16[3,3,3,3,64]{4,3,2,1,0:T(4,128)(2,1)S(1)}, bf16[3,3,3,3,64]{4,3,2,1,0:T(4,128)(2,1)}, u32[]{:S(2)}) copy-start(bf16[3,3,3,3,64]{4,3,2,1,0:T(4,128)(2,1)} %param.13) | copy-start | bytes 31108
  2.7 8.6 %copy-start.37 = (bf16[384,81]{1,0:T(8,128)(2,1)S(1)}, bf16[384,81]{1,0:T(8,128)(2,1)}, u32[]{:S(2)}) copy-start(bf16[384,81]{1,0:T(8,128)(2,1)} %constant.112) | copy-start | bytes 186628
  2.7 11.7 %collective-permute-start = (bf16[696,128]{1,0:T(8,128)(2,1)S(1)}, bf16[696,128]{1,0:T(8,128)(2,1)S(1)}, u32[]{:S(2)}, u32[]{:S(2)}) collective-permute-start(bf16[696,128]{1,0:T(8,128)(2,1)S(1)} %fusion.10), channel_id=1, source_target_pairs={{0,16},{16,32},{32,48},{48,64},{64,80},{80,96},{96,112},{112,0},{1... | collective-permute-start | bytes 534536 | tf_op jit(solution)/shard_map/ppermute | solution.py:373
  4.8 9.6 %collective-permute-start.1 = (bf16[696,128]{1,0:T(8,128)(2,1)S(1)}, bf16[696,128]{1,0:T(8,128)(2,1)S(1)}, u32[]{:S(2)}, u32[]{:S(2)}) collective-permute-start(bf16[696,128]{1,0:T(8,128)(2,1)S(1)} %fusion.11), channel_id=1, source_target_pairs={{16,0},{32,16},{48,32},{64,48},{80,64},{96,80},{112,96},{0,112},{1... | collective-permute-start | bytes 534536 | tf_op jit(solution)/shard_map/ppermute | solution.py:373
  9.8 1.7 %copy-start.36 = (bf16[384,81]{1,0:T(8,128)(2,1)S(1)}, bf16[384,81]{1,0:T(8,128)(2,1)}, u32[]{:S(2)}) copy-start(bf16[384,81]{1,0:T(8,128)(2,1)} %constant.113) | copy-start | bytes 186628
  10.4 1.3 %copy-start.39 = (bf16[384,81]{1,0:T(8,128)(2,1)S(1)}, bf16[384,81]{1,0:T(8,128)(2,1)}, u32[]{:S(2)}) copy-start(bf16[384,81]{1,0:T(8,128)(2,1)} %constant.114) | copy-start | bytes 186628
  11.3 0.9 copy-start.35
  11.6 0.9 copy-start.34
  11.8 0.9 copy-start.38
  12.5 2.0 %copy-start.1 = (bf16[3,3,3,64,128]{4,3,2,1,0:T(8,128)(2,1)S(1)}, bf16[3,3,3,64,128]{4,3,2,1,0:T(8,128)(2,1)}, u32[]{:S(2)}) copy-start(bf16[3,3,3,64,128]{4,3,2,1,0:T(8,128)(2,1)} %param.15) | copy-start | bytes 1327108
  16.4 1.1 %copy-start.4 = (bf16[9,16,16,128]{3,2,1,0:T(8,128)(2,1)S(1)}, bf16[9,16,16,128]{3,2,1,0:T(8,128)(2,1)}, u32[]{:S(2)}) copy-start(bf16[9,16,16,128]{3,2,1,0:T(8,128)(2,1)} %param.17) | copy-start | bytes 1769476
  16.7 1.1 %copy-start.3 = (bf16[3,17,32,32]{3,2,1,0:T(8,128)(2,1)S(1)}, bf16[3,17,32,32]{3,2,1,0:T(8,128)(2,1)}, u32[]{:S(2)}) copy-start(bf16[3,17,32,32]{3,2,1,0:T(8,128)(2,1)} %param.12) | copy-start | bytes 313348
  16.8 1.0 %copy-start.8 = (bf16[768,128]{1,0:T(8,128)(2,1)}, bf16[768,128]{1,0:T(8,128)(2,1)S(1)}, u32[]{:S(2)}) copy-start(bf16[768,128]{1,0:T(8,128)(2,1)S(1)} %constant_dynamic-update-slice_fusion.13) | copy-start | bytes 589828
  16.8 1.0 %copy-start.6 = (bf16[768,128]{1,0:T(8,128)(2,1)}, bf16[768,128]{1,0:T(8,128)(2,1)S(1)}, u32[]{:S(2)}) copy-start(bf16[768,128]{1,0:T(8,128)(2,1)S(1)} %constant_dynamic-update-slice_fusion.25) | copy-start | bytes 589828
  17.5 0.9 copy-start.2
  18.0 0.8 copy-start
  19.0 2.9 %copy-start.30 = (bf16[128,64]{1,0:T(8,128)(2,1)S(1)}, bf16[128,64]{1,0:T(8,128)(2,1)}, u32[]{:S(2)}) copy-start(bf16[128,64]{1,0:T(8,128)(2,1)} %get-tuple-element.39) | copy-start | bytes 49156
  19.0 3.0 %copy-start.31 = (bf16[128,64]{1,0:T(8,128)(2,1)S(1)}, bf16[128,64]{1,0:T(8,128)(2,1)}, u32[]{:S(2)}) copy-start(bf16[128,64]{1,0:T(8,128)(2,1)} %get-tuple-element.40) | copy-start | bytes 49156
  19.0 3.0 %copy-start.32 = (bf16[128,64]{1,0:T(8,128)(2,1)S(1)}, bf16[128,64]{1,0:T(8,128)(2,1)}, u32[]{:S(2)}) copy-start(bf16[128,64]{1,0:T(8,128)(2,1)} %get-tuple-element.41) | copy-start | bytes 49156
  19.1 3.0 %copy-start.33 = (bf16[128,64]{1,0:T(8,128)(2,1)S(1)}, bf16[128,64]{1,0:T(8,128)(2,1)}, u32[]{:S(2)}) copy-start(bf16[128,64]{1,0:T(8,128)(2,1)} %get-tuple-element.42) | copy-start | bytes 49156
  19.1 3.1 %copy-start.14 = (bf16[128,64]{1,0:T(8,128)(2,1)S(1)}, bf16[128,64]{1,0:T(8,128)(2,1)}, u32[]{:S(2)}) copy-start(bf16[128,64]{1,0:T(8,128)(2,1)} %get-tuple-element.37) | copy-start | bytes 49156
  19.1 3.1 %copy-start.15 = (bf16[128,64]{1,0:T(8,128)(2,1)S(1)}, bf16[128,64]{1,0:T(8,128)(2,1)}, u32[]{:S(2)}) copy-start(bf16[128,64]{1,0:T(8,128)(2,1)} %get-tuple-element.38) | copy-start | bytes 49156
  19.1 3.2 %copy-start.28 = (bf16[128,64]{1,0:T(8,128)(2,1)S(1)}, bf16[128,64]{1,0:T(8,128)(2,1)}, u32[]{:S(2)}) copy-start(bf16[128,64]{1,0:T(8,128)(2,1)} %get-tuple-element.35) | copy-start | bytes 49156
  19.1 3.2 %copy-start.29 = (bf16[128,64]{1,0:T(8,128)(2,1)S(1)}, bf16[128,64]{1,0:T(8,128)(2,1)}, u32[]{:S(2)}) copy-start(bf16[128,64]{1,0:T(8,128)(2,1)} %get-tuple-element.36) | copy-start | bytes 49156
  19.1 3.3 %copy-start.13 = (bf16[128,64]{1,0:T(8,128)(2,1)S(1)}, bf16[128,64]{1,0:T(8,128)(2,1)}, u32[]{:S(2)}) copy-start(bf16[128,64]{1,0:T(8,128)(2,1)} %get-tuple-element.34) | copy-start | bytes 49156
  19.1 3.4 %copy-start.24 = (bf16[128,64]{1,0:T(8,128)(2,1)S(1)}, bf16[128,64]{1,0:T(8,128)(2,1)}, u32[]{:S(2)}) copy-start(bf16[128,64]{1,0:T(8,128)(2,1)} %get-tuple-element.30) | copy-start | bytes 49156
  19.1 3.3 %copy-start.25 = (bf16[128,64]{1,0:T(8,128)(2,1)S(1)}, bf16[128,64]{1,0:T(8,128)(2,1)}, u32[]{:S(2)}) copy-start(bf16[128,64]{1,0:T(8,128)(2,1)} %get-tuple-element.31) | copy-start | bytes 49156
  19.1 3.3 %copy-start.26 = (bf16[128,64]{1,0:T(8,128)(2,1)S(1)}, bf16[128,64]{1,0:T(8,128)(2,1)}, u32[]{:S(2)}) copy-start(bf16[128,64]{1,0:T(8,128)(2,1)} %get-tuple-element.32) | copy-start | bytes 49156
  19.1 3.3 %copy-start.27 = (bf16[128,64]{1,0:T(8,128)(2,1)S(1)}, bf16[128,64]{1,0:T(8,128)(2,1)}, u32[]{:S(2)}) copy-start(bf16[128,64]{1,0:T(8,128)(2,1)} %get-tuple-element.33) | copy-start | bytes 49156
  19.2 3.4 %copy-start.11 = (bf16[128,64]{1,0:T(8,128)(2,1)S(1)}, bf16[128,64]{1,0:T(8,128)(2,1)}, u32[]{:S(2)}) copy-start(bf16[128,64]{1,0:T(8,128)(2,1)} %get-tuple-element.28) | copy-start | bytes 49156
  19.2 3.4 %copy-start.12 = (bf16[128,64]{1,0:T(8,128)(2,1)S(1)}, bf16[128,64]{1,0:T(8,128)(2,1)}, u32[]{:S(2)}) copy-start(bf16[128,64]{1,0:T(8,128)(2,1)} %get-tuple-element.29) | copy-start | bytes 49156
  19.2 5.3 %collective-permute-start.3 = (bf16[768,128]{1,0:T(8,128)(2,1)S(1)}, bf16[768,128]{1,0:T(8,128)(2,1)S(1)}, u32[]{:S(2)}, u32[]{:S(2)}) collective-permute-start(bf16[768,128]{1,0:T(8,128)(2,1)S(1)} %fusion.9), channel_id=1, source_target_pairs={{1,0},{2,1},{3,2},{4,3},{5,4},{6,5},{7,6},{8,7},{9,8},{10,9},{11,1... | collective-permute-start | bytes 589832 | tf_op jit(solution)/shard_map/ppermute | solution.py:373
  21.3 1.4 %copy-start.22 = (bf16[128,64]{1,0:T(8,128)(2,1)S(1)}, bf16[128,64]{1,0:T(8,128)(2,1)}, u32[]{:S(2)}) copy-start(bf16[128,64]{1,0:T(8,128)(2,1)} %get-tuple-element.26) | copy-start | bytes 49156
  21.3 1.4 %copy-start.23 = (bf16[128,64]{1,0:T(8,128)(2,1)S(1)}, bf16[128,64]{1,0:T(8,128)(2,1)}, u32[]{:S(2)}) copy-start(bf16[128,64]{1,0:T(8,128)(2,1)} %get-tuple-element.27) | copy-start | bytes 49156
  21.3 1.5 %copy-start.10 = (bf16[128,64]{1,0:T(8,128)(2,1)S(1)}, bf16[128,64]{1,0:T(8,128)(2,1)}, u32[]{:S(2)}) copy-start(bf16[128,64]{1,0:T(8,128)(2,1)} %get-tuple-element.25) | copy-start | bytes 49156
  21.3 1.6 %copy-start.18 = (bf16[128,64]{1,0:T(8,128)(2,1)S(1)}, bf16[128,64]{1,0:T(8,128)(2,1)}, u32[]{:S(2)}) copy-start(bf16[128,64]{1,0:T(8,128)(2,1)} %get-tuple-element.21) | copy-start | bytes 49156
  21.4 1.6 %copy-start.19 = (bf16[128,64]{1,0:T(8,128)(2,1)S(1)}, bf16[128,64]{1,0:T(8,128)(2,1)}, u32[]{:S(2)}) copy-start(bf16[128,64]{1,0:T(8,128)(2,1)} %get-tuple-element.22) | copy-start | bytes 49156
  21.4 1.6 %copy-start.20 = (bf16[128,64]{1,0:T(8,128)(2,1)S(1)}, bf16[128,64]{1,0:T(8,128)(2,1)}, u32[]{:S(2)}) copy-start(bf16[128,64]{1,0:T(8,128)(2,1)} %get-tuple-element.23) | copy-start | bytes 49156
  21.4 1.6 %copy-start.21 = (bf16[128,64]{1,0:T(8,128)(2,1)S(1)}, bf16[128,64]{1,0:T(8,128)(2,1)}, u32[]{:S(2)}) copy-start(bf16[128,64]{1,0:T(8,128)(2,1)} %get-tuple-element.24) | copy-start | bytes 49156
  21.4 1.8 %copy-start.16 = (bf16[128,64]{1,0:T(8,128)(2,1)S(1)}, bf16[128,64]{1,0:T(8,128)(2,1)}, u32[]{:S(2)}) copy-start(bf16[128,64]{1,0:T(8,128)(2,1)} %get-tuple-element.17) | copy-start | bytes 49156
  21.4 1.8 %copy-start.17 = (bf16[128,64]{1,0:T(8,128)(2,1)S(1)}, bf16[128,64]{1,0:T(8,128)(2,1)}, u32[]{:S(2)}) copy-start(bf16[128,64]{1,0:T(8,128)(2,1)} %get-tuple-element.18) | copy-start | bytes 49156
  21.7 1.6 %copy-start.7 = (bf16[768,128]{1,0:T(8,128)(2,1)S(1)}, bf16[768,128]{1,0:T(8,128)(2,1)}, u32[]{:S(2)}) copy-start(bf16[768,128]{1,0:T(8,128)(2,1)} %copy-done.6) | copy-start | bytes 589828
  21.7 1.6 %copy-start.9 = (bf16[768,128]{1,0:T(8,128)(2,1)S(1)}, bf16[768,128]{1,0:T(8,128)(2,1)}, u32[]{:S(2)}) copy-start(bf16[768,128]{1,0:T(8,128)(2,1)} %copy-done.8) | copy-start | bytes 589828
  21.7 7.5 %collective-permute-start.2 = (bf16[768,128]{1,0:T(8,128)(2,1)S(1)}, bf16[768,128]{1,0:T(8,128)(2,1)S(1)}, u32[]{:S(2)}, u32[]{:S(2)}) collective-permute-start(bf16[768,128]{1,0:T(8,128)(2,1)S(1)} %fusion.8), channel_id=1, source_target_pairs={{0,1},{1,2},{2,3},{3,4},{4,5},{5,6},{6,7},{7,8},{8,9},{9,10},{10,1... | collective-permute-start | bytes 589832 | tf_op jit(solution)/shard_map/ppermute | solution.py:373
  23.4 5.8 %copy-start.43 = (bf16[1536,256]{1,0:T(8,128)(2,1)}, bf16[1536,256]{1,0:T(8,128)(2,1)S(1)}, u32[]{:S(2)}) copy-start(bf16[1536,256]{1,0:T(8,128)(2,1)S(1)} %constant_dynamic-update-slice_fusion.36.wb) | copy-start | bytes 2359300
  24.5 4.7 %copy-start.44 = (bf16[768,128]{1,0:T(8,128)(2,1)}, bf16[768,128]{1,0:T(8,128)(2,1)S(1)}, u32[]{:S(2)}) copy-start(bf16[768,128]{1,0:T(8,128)(2,1)S(1)} %collective-permute-done.3.right) | copy-start | bytes 589828
  29.2 0.7 copy-start.45
  61.5 15.8 %all-to-all-start = ((bf16[16,160,128]{2,1,0:T(8,128)(2,1)}), bf16[16,160,128]{2,1,0:T(8,128)(2,1)S(1)}, u32[]{:S(2)}, u32[]{:S(2)}) async-start(bf16[16,160,128]{2,1,0:T(8,128)(2,1)} %get-tuple-element.12), calls=%async_computation | async-start | bytes 1310720 | tf_op jit(solution)/shard_map/all_to_all | solution.py:460
  77.5 4.5 %collective-permute-start.4 = (f32[160,128]{1,0:T(8,128)S(1)}, f32[160,128]{1,0:T(8,128)S(1)}, u32[]{:S(2)}, u32[]{:S(2)}) collective-permute-start(f32[160,128]{1,0:T(8,128)S(1)} %convert_reduce_fusion), channel_id=1, source_target_pairs={{0,16},{16,0},{32,48},{48,32},{64,80},{80,64},{96,112},{112,96},{1... | collective-permute-start | bytes 245768 | tf_op jit(solution)/shard_map/ppermute | solution.py:464
  82.0 6.0 %collective-permute-start.5 = (f32[160,128]{1,0:T(8,128)S(1)}, f32[160,128]{1,0:T(8,128)S(1)}, u32[]{:S(2)}, u32[]{:S(2)}) collective-permute-start(f32[160,128]{1,0:T(8,128)S(1)} %add.49), channel_id=1, source_target_pairs={{0,32},{16,48},{32,0},{48,16},{64,96},{80,112},{96,64},{112,80},{1... | collective-permute-start | bytes 245768 | tf_op jit(solution)/shard_map/ppermute | solution.py:464
  88.0 6.0 %collective-permute-start.6 = (f32[160,128]{1,0:T(8,128)S(1)}, f32[160,128]{1,0:T(8,128)S(1)}, u32[]{:S(2)}, u32[]{:S(2)}) collective-permute-start(f32[160,128]{1,0:T(8,128)S(1)} %add.50), channel_id=1, source_target_pairs={{0,64},{16,80},{32,96},{48,112},{64,0},{80,16},{96,32},{112,48},{1... | collective-permute-start | bytes 245768 | tf_op jit(solution)/shard_map/ppermute | solution.py:464

commit v4 on v3

--- a/solution.py
+++ b/solution.py
@@ -90,10 +90,10 @@
 
 
 def kernel(
-    pos, clip, left, right, up, sel_mid, sel_side, spread, w1, b1, w2, b2, wb, wx, place,
+    pos, clip, left, right, up, sel_mid, sel_side, spread, w1, b1, w_second, b2, wx, place,
     x_out, g_out,
     ct, p2, mk, sl, hf_a, hf_b, h6_a, h6_b, dacc, sdf, d4, dt, hdf_a, hdf_b, hd4_a, hd4_b, hds, yt, xs, tp, tpt,
-    thf_a, thf_b, th6_a, th6_b, oacc, gacc, gf, strips, upf,
+    thf_a, thf_b, th6_a, th6_b, oacc, gacc, gf, strips, upf, w2, wb,
 ):
     r0, c0, rows, cols = pos[0], pos[1], pos[2], pos[3]
 
@@ -118,6 +118,23 @@
     sdf[480:496, :] = jnp.zeros((16, 128), F32)
     gf[...] = jnp.zeros(gf.shape, F32)
     upf[...] = jnp.zeros(upf.shape, F32)
+
+    for n, a in enumerate((2, 0, 1)):
+        for k, tap in enumerate(BLOCKS):
+            block = jnp.zeros((64, 128), BF16) if tap is None else w_second[a * 9 + tap[0] * 3 + tap[1]]
+            w2[k * 64 : (k + 1) * 64, n * 128 : (n + 1) * 128] = block
+    for n, a in enumerate((1, 2, 0)):
+        for dq in range(2):
+            for ds in range(2):
+                for rp in range(2):
+                    b = rp + 1 - 2 * dq
+                    pair = jnp.zeros((128, 128), F32)
+                    if b >= 0:
+                        taps = [w_second[a * 9 + b * 3 + c].astype(F32) for c in ((0,) if ds else (1, 2))]
+                        pair = jnp.concatenate([jnp.zeros((64, 128), F32)] * ds + taps, axis=0)
+                    to = (n * 4 + dq * 2 + ds) * 128
+                    wb[to : to + 128, rp * 128 : (rp + 1) * 128] = jnp.transpose(pair).astype(BF16)
+
     strips[0] = jnp.where(c0 > 0, left[...].astype(F32), 0.0)
     strips[1] = jnp.where(c0 + 32 < cols, right[...].astype(F32), 0.0)
     h6_b[...] = jnp.zeros(h6_b.shape, BF16)
@@ -256,16 +273,19 @@
         tpt[t + 1] = jnp.where(core_first, wide[:, 0:416], 0.0).astype(BF16)
         tp[t + 1, :, 0:48] = jnp.transpose(wide)[0:416].astype(BF16)
 
-    for n in range(T):
-        placed = dot(xs[n * 48 : (n + 1) * 48, :], place[...])
-        placed = placed[0:24] + placed[24:48]
-        for p in range(18):
-            for ro in range(2):
-                row = 2 * p - 3 + ro
-                if 0 <= row < 32:
-                    for ch in range(3):
-                        k = ro * 12 + ch
-                        x_out[ch, n, row : row + 1, :] = placed[k : k + 1, p * 32 : p * 32 + 32]
+    for first in range(0, T, 6):
+        frames = range(first, min(first + 6, T))
+        group = dot(xs[first * 48 : (frames[-1] + 1) * 48, :], place[...])
+        for n in frames:
+            at = (n - first) * 48
+            placed = group[at : at + 24] + group[at + 24 : at + 48]
+            for p in range(18):
+                for ro in range(2):
+                    row = 2 * p - 3 + ro
+                    if 0 <= row < 32:
+                        for ch in range(3):
+                            k = ro * 12 + ch
+                            x_out[ch, n, row : row + 1, :] = placed[k : k + 1, p * 32 : p * 32 + 32]
 
     def tangents(t, thf, th6):
         lhs = jnp.concatenate([tp[t], tp[t + 1], tp[t + 2]], axis=1)
@@ -278,8 +298,9 @@
         gacc[...] += dot(turned, hds[t + 1, 0:416, :])
 
     def odd_terms(p):
-        oacc[256:384, :] += dot(dt[jnp.maximum(p, 0)], th6_b[...])
-        oacc[0:128, :] += dot(dt[p + 1], th6_b[...])
+        both = dot(dt[pl.ds(jnp.maximum(p, 0), 2)].reshape(256, 384), th6_b[...])
+        oacc[256:384, :] += both[0:128]
+        oacc[0:128, :] += both[128:256]
 
     def even_terms(p):
         oacc[128:256, :] += dot(dt[p], th6_a[...])
@@ -328,7 +349,7 @@
             jax.ShapeDtypeStruct((3, T, 32, 32), F32),
             jax.ShapeDtypeStruct((16, 160, 128), BF16),
         ),
-        in_specs=[pl.BlockSpec(memory_space=pltpu.SMEM)] + [vmem] * 14,
+        in_specs=[pl.BlockSpec(memory_space=pltpu.SMEM)] + [vmem] * 13,
         out_specs=(vmem, vmem),
         scratch_shapes=[
             vm((4, T * S, 144)),
@@ -361,6 +382,8 @@
             vm((96, 64)),
             vm((2, 768, 128)),
             vm((480, 128)),
+            vm((768, 384), BF16),
+            vm((1536, 256), BF16),
         ],
         compiler_params=pltpu.CompilerParams(vmem_limit_bytes=60 * 1024 * 1024),
         cost_estimate=pl.CostEstimate(flops=10**10, bytes_accessed=2 * 10**7, transcendentals=0),
@@ -388,7 +411,6 @@
     above, below = swapped(
         packed(clip[:, :, 24:32], upstream[:, 14:16]), packed(clip[:, :, 0:8], upstream[:, 0:2]), "ha"
     )
-    above, below, w_second = lax.optimization_barrier((above, below, w_second))
     above = jnp.where(ha > 0, above, jnp.zeros_like(above))
     below = jnp.where(ha < lax.axis_size("ha") - 1, below, jnp.zeros_like(below))
     clip_part = lambda v, width: v[:408, :width].reshape(3, T, 8, width)
@@ -413,30 +435,6 @@
         "ko,bkl->lbo", w_flat, jnp.asarray(first_backward(), BF16), preferred_element_type=F32
     )
     wx = wx.astype(BF16).reshape(80, 1024)
-    nothing = jnp.zeros((64, 128), BF16)
-    w2 = jnp.concatenate(
-        [
-            jnp.concatenate(
-                [nothing if k is None else w_second[a, k[0], k[1]] for k in BLOCKS], axis=0
-            )
-            for a in (2, 0, 1)
-        ],
-        axis=1,
-    )
-    turned = jnp.swapaxes(w_second, 3, 4)
-    blank = jnp.zeros((128, 64), BF16)
-    pieces = []
-    for a in (1, 2, 0):
-        for dq in range(2):
-            for ds in range(2):
-                line = []
-                for rp in range(2):
-                    for cp in range(2):
-                        b, c = rp + 1 - 2 * dq, cp + 1 - 2 * ds
-                        line.append(turned[a, b, c] if b >= 0 and c >= 0 else blank)
-                pieces.append(jnp.concatenate(line, axis=1))
-    wb = jnp.concatenate(pieces, axis=0)
-
     middle, first8, last8 = pick_columns()
     input_grad, terms = run_kernel(
         pos,
@@ -449,9 +447,8 @@
         jnp.asarray(spread_rows(), BF16),
         w1,
         b_first[None],
-        w2,
+        w_second.reshape(27, 64, 128),
         b_second[None],
-        wb,
         wx,
         jnp.asarray(place_columns(), BF16),
     )
@@ -461,7 +458,9 @@
     part = part.astype(F32).sum(0)
     step = 1
     while step < lax.axis_size("ha"):
-        part = part + lax.ppermute(part, "ha", [(i, i ^ step) for i in range(lax.axis_size("ha"))])
+        sent = part.astype(BF16)
+        pairs = [(i, i ^ step) for i in range(lax.axis_size("ha"))]
+        part = sent.astype(F32) + lax.ppermute(sent, "ha", pairs).astype(F32)
         step *= 2
     part = part * scale
     lane = lax.broadcasted_iota(jnp.int32, (128, 16), 0)

time: 96.3 us -> 88.2 us (0.916)
  blocking collectives: 0 us -> 15.6 us
  waiting for transfers between devices: 28.3 us -> 16.5 us
  starting transfers between devices: 18.1 us -> 14.5 us
  Pallas kernels: 31.7 us -> 28.7 us
  local copies, waits for them, and re-layouts: 10 us -> 7.07 us
  other arithmetic: 3.86 us -> 2.01 us
    all_to_all x0 -> x1, blocking collectives: none -> 15.6 us  [body(): part = lax.all_to_all(terms, 'wa', 0, 0, tiled=True)]
    all_to_all x1 -> x0, waiting for transfers between devices: 12.2 us -> none  [body(): part = lax.all_to_all(terms, 'wa', 0, 0, tiled=True)]
    all_to_all x1 -> x0, starting transfers between devices: 3.59 us -> none  [body(): part = lax.all_to_all(terms, 'wa', 0, 0, tiled=True)]
    pallas_call x1, Pallas kernels: 31.7 us -> 28.7 us  [run_kernel(): pl.pallas_call(kernel, out_shape=(jax.ShapeDtypeStruct((3, T, 32, 32), F3...]
    ppermute x3, waiting for transfers between devices: 11.3 us -> 9.68 us  [body(): part = sent.astype(F32) + lax.ppermute(sent, 'ha', pairs).astype(F32)]
    squeeze x2 -> x0, local copies, waits for them, and re-layouts: 1.51 us -> none  [body(): line.append(turned[a, b, c] if b >= 0 and c >= 0 else blank)]
    ppermute x2, waiting for transfers between devices: 0.09 us -> 1.13 us  [swapped(): lax.ppermute(to_prev, axis, [(j, i) for i, j in ring])]
    ppermute x2, waiting for transfers between devices: 4.68 us -> 5.68 us  [swapped(): lax.ppermute(to_next, axis, ring)]
  transfers between devices with their start and end apart: 8 -> 7, of which waited for: 6 -> 6; matrix products, arithmetic and copies ran while one was open for 7% -> 6% of each run, Pallas kernels for 0% -> 0%
where the time goes in v4:
time: 88.2 us; the launch traced here: 87.8 us
  Pallas kernels  28.7 us (33%)
  waiting for transfers between devices  16.5 us (19%)
  blocking collectives  15.6 us (18%)
  starting transfers between devices  14.5 us (16%)
  local copies, waits for them, and re-layouts  7.07 us (8%)
  matrix products  2.38 us (3%)
  other arithmetic  2.01 us (2%)
  between operations  1.11 us (1%)
    pallas_call x1, Pallas kernels, run_kernel(): pl.pallas_call(kernel, out_shape=(jax.ShapeDtypeStruct((3, T, 32, 32), F3...  28.7 us
    all_to_all x1, blocking collectives, body(): part = lax.all_to_all(terms, 'wa', 0, 0, tiled=True)  15.6 us
    ppermute x3, waiting for transfers between devices, body(): part = sent.astype(F32) + lax.ppermute(sent, 'ha', pairs).astype(F32)  9.68 us
    ppermute x2, starting transfers between devices, swapped(): lax.ppermute(to_prev, axis, [(j, i) for i, j in ring])  6.67 us
    ppermute x2, waiting for transfers between devices, swapped(): lax.ppermute(to_next, axis, ring)  5.68 us
    ppermute x3, starting transfers between devices, body(): part = sent.astype(F32) + lax.ppermute(sent, 'ha', pairs).astype(F32)  5.55 us
    unnamed x41, local copies, waits for them, and re-layouts  2.38 us
    ppermute x2, starting transfers between devices, swapped(): lax.ppermute(to_next, axis, ring)  2.32 us
  transfers between devices with their start and end apart: 7, of which 6 were waited for; matrix products, arithmetic and copies ran while one was open for 6% of the time, Pallas kernels for 0%

profile of v4, /device:TPU:0, one launch (start us, length us, event | category | flops | bytes accessed | tf_op | source)
XLA Modules:
  0.0 87.8 jit_solution(11911084712895578919)
XLA Ops:
  0.6 0.0 copy-start.11
  0.6 0.0 copy-start.12
  0.7 0.0 copy-start.4
  0.7 0.0 copy-start.13
  0.7 1.0 %fusion.43 = (bf16[3,17,8,32]{3,2,1,0:T(8,128)(2,1)S(1)}, bf16[3,17,8,32]{3,2,1,0:T(8,128)(2,1)S(1)}) fusion(bf16[3,17,32,32]{3,2,1,0:T(8,128)(2,1)} %param.12), kind=kLoop, calls=%fused_computation.92 | loop fusion | bytes 104448 | tf_op jit(solution)/shard_map/slice | solution.py:412
  1.7 0.9 %fusion.42 = (bf16[9,2,16,128]{3,2,1,0:T(8,128)(2,1)S(1)}, bf16[9,2,16,128]{3,2,1,0:T(8,128)(2,1)S(1)}) fusion(bf16[9,16,16,128]{3,2,1,0:T(8,128)(2,1)} %param.17), kind=kLoop, calls=%fused_computation.91 | loop fusion | bytes 294912 | tf_op jit(solution)/shard_map/slice | solution.py:412
  2.7 0.0 copy-start.8
  2.7 2.1 %collective-permute-start = (bf16[696,128]{1,0:T(8,128)(2,1)S(1)}, bf16[696,128]{1,0:T(8,128)(2,1)S(1)}, u32[]{:S(2)}, u32[]{:S(2)}) collective-permute-start(bf16[696,128]{1,0:T(8,128)(2,1)S(1)} %fusion.10), channel_id=1, source_target_pairs={{0,16},{16,32},{32,48},{48,64},{64,80},{80,96},{96,112},{112,0},{1... | collective-permute-start | bytes 534536 | tf_op jit(solution)/shard_map/ppermute | solution.py:396
  4.8 4.8 %collective-permute-start.1 = (bf16[696,128]{1,0:T(8,128)(2,1)S(1)}, bf16[696,128]{1,0:T(8,128)(2,1)S(1)}, u32[]{:S(2)}, u32[]{:S(2)}) collective-permute-start(bf16[696,128]{1,0:T(8,128)(2,1)S(1)} %fusion.11), channel_id=1, source_target_pairs={{16,0},{32,16},{48,32},{64,48},{80,64},{96,80},{112,96},{0,112},{1... | collective-permute-start | bytes 534536 | tf_op jit(solution)/shard_map/ppermute | solution.py:396
  9.6 0.0 copy-done.13
  9.7 0.0 copy-done.11
  9.7 0.2 fusion.22
  9.8 0.0 copy-done.12
  9.8 0.0 copy-start.7
  9.9 0.2 fusion.20
  10.0 0.0 copy-done.4
  10.0 0.4 convolution_convert_fusion
  10.5 0.8 copy.61.wx
  11.3 0.0 copy-done.8
  11.3 0.3 convolution_add_fusion.2
  11.5 0.0 copy-done.7
  11.5 0.0 copy-start.5
  11.6 0.2 convolution_add_fusion.1
  11.8 0.0 copy-start.9
  11.8 0.3 fusion.2
  12.0 0.1 copy-done.6
  12.2 0.3 convolution_add_fusion.5
  12.4 0.0 copy-done.5
  12.5 0.2 convolution_add_fusion.4
  12.7 0.0 copy-done.9
  12.7 0.3 fusion.3
  13.0 1.1 %collective-permute-done = bf16[696,128]{1,0:T(8,128)(2,1)S(1)} collective-permute-done((bf16[696,128]{1,0:T(8,128)(2,1)S(1)}, bf16[696,128]{1,0:T(8,128)(2,1)S(1)}, u32[]{:S(2)}, u32[]{:S(2)}) %collective-permute-start) | collective-permute-done | bytes 178208 | tf_op jit(solution)/shard_map/ppermute | solution.py:396
  14.1 0.0 collective-permute-done.1
  14.2 0.1 pad_maximum_fusion.1.clip
  14.3 0.0 copy-start.3
  14.4 0.2 slice_bitcast_fusion
  14.6 0.6 copy-done
  15.2 0.2 copy.37
  15.4 0.2 copy-done.3
  15.6 0.1 pad_maximum_fusion.up
  15.7 0.0 copy-start.1
  15.7 0.1 slice_bitcast_fusion.2
  16.0 1.8 %collective-permute-start.3 = (bf16[768,128]{1,0:T(8,128)(2,1)S(1)}, bf16[768,128]{1,0:T(8,128)(2,1)S(1)}, u32[]{:S(2)}, u32[]{:S(2)}) collective-permute-start(bf16[768,128]{1,0:T(8,128)(2,1)S(1)} %fusion.9), channel_id=1, source_target_pairs={{1,0},{2,1},{3,2},{4,3},{5,4},{6,5},{7,6},{8,7},{9,8},{10,9},{11,1... | collective-permute-start | bytes 589832 | tf_op jit(solution)/shard_map/ppermute | solution.py:396
  17.8 0.2 copy.35
  18.2 0.3 collective-permute-start.2
  18.4 0.7 pad_add_fusion.pos
  19.1 0.8 pad_maximum_fusion.2.w1
  19.9 1.1 %collective-permute-done.3.right = bf16[768,128]{1,0:T(8,128)(2,1)S(1)} collective-permute-done((bf16[768,128]{1,0:T(8,128)(2,1)S(1)}, bf16[768,128]{1,0:T(8,128)(2,1)S(1)}, u32[]{:S(2)}, u32[]{:S(2)}) %collective-permute-start.3) | collective-permute-done | bytes 196640 | tf_op jit(solution)/shard_map/ppermute | solution.py:396
  21.0 4.6 %collective-permute-done.2.left = bf16[768,128]{1,0:T(8,128)(2,1)S(1)} collective-permute-done((bf16[768,128]{1,0:T(8,128)(2,1)S(1)}, bf16[768,128]{1,0:T(8,128)(2,1)S(1)}, u32[]{:S(2)}, u32[]{:S(2)}) %collective-permute-start.2) | collective-permute-done | bytes 196640 | tf_op jit(solution)/shard_map/ppermute | solution.py:396
  25.6 0.7 copy-done.15
  26.3 28.7 %shard_map.139 = (f32[3,17,32,32]{3,2,1,0:T(8,128)}, bf16[16,160,128]{2,1,0:T(8,128)(2,1)}) custom-call(s32[4]{0:T(128)} %pad_add_fusion.pos, bf16[3,17,48,32]{3,2,1,0:T(8,128)(2,1)} %copy-done, bf16[768,128]{1,0:T(8,128)(2,1)} %copy-done.15, bf16[768,128]{1,0:T(8,128)(2,1)} %copy-done.14, bf16[9,20,16,128]{3,2,1,0:T(8,128)(2,1)} %copy-done.1, ...), custom_call_target="tpu_custom_call" | custom-call | flops 10000000000 | bytes 20000000 | tf_op jit(solution)/shard_map/pallas_call | solution.py:346
  55.0 15.6 %all_to_all.5 = bf16[16,160,128]{2,1,0:T(8,128)(2,1)S(1)} all-to-all(bf16[16,160,128]{2,1,0:T(8,128)(2,1)} %get-tuple-element.6), channel_id=1, replica_groups=mesh['ha'=8,'wa'=16] {'wa'}, dimensions={0} | all-to-all | bytes 1310720 | tf_op jit(solution)/shard_map/all_to_all | solution.py:457
  70.6 0.1 reduce_sum.12
  70.6 0.1 collective-permute-start.4
  70.8 4.0 %collective-permute-done.4 = bf16[160,128]{1,0:T(8,128)(2,1)S(1)} collective-permute-done((bf16[160,128]{1,0:T(8,128)(2,1)S(1)}, bf16[160,128]{1,0:T(8,128)(2,1)S(1)}, u32[]{:S(2)}, u32[]{:S(2)}) %collective-permute-start.4) | collective-permute-done | bytes 40992 | tf_op jit(solution)/shard_map/ppermute | solution.py:463
  74.8 3.1 %collective-permute-start.5 = (bf16[160,128]{1,0:T(8,128)(2,1)S(1)}, bf16[160,128]{1,0:T(8,128)(2,1)S(1)}, u32[]{:S(2)}, u32[]{:S(2)}) collective-permute-start(bf16[160,128]{1,0:T(8,128)(2,1)S(1)} %add_convert_fusion.1), channel_id=1, source_target_pairs={{0,32},{16,48},{32,0},{48,16},{64,96},{80,112},{96,64},{112,80},{1... | collective-permute-start | bytes 122888 | tf_op jit(solution)/shard_map/ppermute | solution.py:463
  77.9 2.4 %collective-permute-done.5 = bf16[160,128]{1,0:T(8,128)(2,1)S(1)} collective-permute-done((bf16[160,128]{1,0:T(8,128)(2,1)S(1)}, bf16[160,128]{1,0:T(8,128)(2,1)S(1)}, u32[]{:S(2)}, u32[]{:S(2)}) %collective-permute-start.5) | collective-permute-done | bytes 40992 | tf_op jit(solution)/shard_map/ppermute | solution.py:463
  80.4 2.3 %collective-permute-start.6 = (bf16[160,128]{1,0:T(8,128)(2,1)S(1)}, bf16[160,128]{1,0:T(8,128)(2,1)S(1)}, u32[]{:S(2)}, u32[]{:S(2)}) collective-permute-start(bf16[160,128]{1,0:T(8,128)(2,1)S(1)} %add_convert_fusion), channel_id=1, source_target_pairs={{0,64},{16,80},{32,96},{48,112},{64,0},{80,16},{96,32},{112,48},{1... | collective-permute-start | bytes 122888 | tf_op jit(solution)/shard_map/ppermute | solution.py:463
  82.7 3.3 %collective-permute-done.6 = bf16[160,128]{1,0:T(8,128)(2,1)S(1)} collective-permute-done((bf16[160,128]{1,0:T(8,128)(2,1)S(1)}, bf16[160,128]{1,0:T(8,128)(2,1)S(1)}, u32[]{:S(2)}, u32[]{:S(2)}) %collective-permute-start.6) | collective-permute-done | bytes 40992 | tf_op jit(solution)/shard_map/ppermute | solution.py:463
  86.0 0.1 slice.131
  86.0 0.2 fusion.12
  86.3 0.2 reshape.79
  86.5 0.7 copy.50
  87.2 0.6 reshape.78
  (43 shorter events, 0.5 us)
Async XLA Ops:
  0.6 9.0 %copy-start.11 = (bf16[384,81]{1,0:T(8,128)(2,1)S(1)}, bf16[384,81]{1,0:T(8,128)(2,1)}, u32[]{:S(2)}) copy-start(bf16[384,81]{1,0:T(8,128)(2,1)} %constant.101) | copy-start | bytes 186628
  0.6 9.2 %copy-start.12 = (bf16[384,81]{1,0:T(8,128)(2,1)S(1)}, bf16[384,81]{1,0:T(8,128)(2,1)}, u32[]{:S(2)}) copy-start(bf16[384,81]{1,0:T(8,128)(2,1)} %constant.97) | copy-start | bytes 186628
  0.7 9.4 %copy-start.4 = (bf16[16,81,80]{1,2,0:T(8,128)(2,1)S(1)}, bf16[16,81,80]{1,2,0:T(8,128)(2,1)}, u32[]{:S(2)}) copy-start(bf16[16,81,80]{1,2,0:T(8,128)(2,1)} %constant.72.clone) | copy-start | bytes 622084
  0.7 9.0 %copy-start.13 = (bf16[3,3,3,3,64]{4,3,2,1,0:T(4,128)(2,1)S(1)}, bf16[3,3,3,3,64]{4,3,2,1,0:T(4,128)(2,1)}, u32[]{:S(2)}) copy-start(bf16[3,3,3,3,64]{4,3,2,1,0:T(4,128)(2,1)} %param.13) | copy-start | bytes 31108
  2.7 8.6 %copy-start.8 = (bf16[384,81]{1,0:T(8,128)(2,1)S(1)}, bf16[384,81]{1,0:T(8,128)(2,1)}, u32[]{:S(2)}) copy-start(bf16[384,81]{1,0:T(8,128)(2,1)} %constant.102) | copy-start | bytes 186628
  2.7 11.3 %collective-permute-start = (bf16[696,128]{1,0:T(8,128)(2,1)S(1)}, bf16[696,128]{1,0:T(8,128)(2,1)S(1)}, u32[]{:S(2)}, u32[]{:S(2)}) collective-permute-start(bf16[696,128]{1,0:T(8,128)(2,1)S(1)} %fusion.10), channel_id=1, source_target_pairs={{0,16},{16,32},{32,48},{48,64},{64,80},{80,96},{96,112},{112,0},{1... | collective-permute-start | bytes 534536 | tf_op jit(solution)/shard_map/ppermute | solution.py:396
  4.8 9.3 %collective-permute-start.1 = (bf16[696,128]{1,0:T(8,128)(2,1)S(1)}, bf16[696,128]{1,0:T(8,128)(2,1)S(1)}, u32[]{:S(2)}, u32[]{:S(2)}) collective-permute-start(bf16[696,128]{1,0:T(8,128)(2,1)S(1)} %fusion.11), channel_id=1, source_target_pairs={{16,0},{32,16},{48,32},{64,48},{80,64},{96,80},{112,96},{0,112},{1... | collective-permute-start | bytes 534536 | tf_op jit(solution)/shard_map/ppermute | solution.py:396
  9.8 1.7 %copy-start.7 = (bf16[384,81]{1,0:T(8,128)(2,1)S(1)}, bf16[384,81]{1,0:T(8,128)(2,1)}, u32[]{:S(2)}) copy-start(bf16[384,81]{1,0:T(8,128)(2,1)} %constant.103) | copy-start | bytes 186628
  10.4 1.3 %copy-start.10 = (bf16[384,81]{1,0:T(8,128)(2,1)S(1)}, bf16[384,81]{1,0:T(8,128)(2,1)}, u32[]{:S(2)}) copy-start(bf16[384,81]{1,0:T(8,128)(2,1)} %constant.104) | copy-start | bytes 186628
  11.3 0.9 %copy-start.6 = (bf16[384,81]{1,0:T(8,128)(2,1)S(1)}, bf16[384,81]{1,0:T(8,128)(2,1)}, u32[]{:S(2)}) copy-start(bf16[384,81]{1,0:T(8,128)(2,1)} %constant.98) | copy-start | bytes 186628
  11.5 0.9 %copy-start.5 = (bf16[384,81]{1,0:T(8,128)(2,1)S(1)}, bf16[384,81]{1,0:T(8,128)(2,1)}, u32[]{:S(2)}) copy-start(bf16[384,81]{1,0:T(8,128)(2,1)} %constant.99) | copy-start | bytes 186628
  11.8 0.9 %copy-start.9 = (bf16[384,81]{1,0:T(8,128)(2,1)S(1)}, bf16[384,81]{1,0:T(8,128)(2,1)}, u32[]{:S(2)}) copy-start(bf16[384,81]{1,0:T(8,128)(2,1)} %constant.100) | copy-start | bytes 186628
  12.7 1.5 %copy-start.2 = (bf16[3,17,32,32]{3,2,1,0:T(8,128)(2,1)S(1)}, bf16[3,17,32,32]{3,2,1,0:T(8,128)(2,1)}, u32[]{:S(2)}) copy-start(bf16[3,17,32,32]{3,2,1,0:T(8,128)(2,1)} %param.12) | copy-start | bytes 313348
  14.3 0.8 copy-start
  14.3 1.3 %copy-start.3 = (bf16[9,16,16,128]{3,2,1,0:T(8,128)(2,1)S(1)}, bf16[9,16,16,128]{3,2,1,0:T(8,128)(2,1)}, u32[]{:S(2)}) copy-start(bf16[9,16,16,128]{3,2,1,0:T(8,128)(2,1)} %param.17) | copy-start | bytes 1769476
  15.7 2.4 %copy-start.1 = (bf16[9,20,16,128]{3,2,1,0:T(8,128)(2,1)}, bf16[9,20,16,128]{3,2,1,0:T(8,128)(2,1)S(1)}, u32[]{:S(2)}) copy-start(bf16[9,20,16,128]{3,2,1,0:T(8,128)(2,1)S(1)} %pad_maximum_fusion.up) | copy-start | bytes 2211844
  16.0 5.0 %collective-permute-start.3 = (bf16[768,128]{1,0:T(8,128)(2,1)S(1)}, bf16[768,128]{1,0:T(8,128)(2,1)S(1)}, u32[]{:S(2)}, u32[]{:S(2)}) collective-permute-start(bf16[768,128]{1,0:T(8,128)(2,1)S(1)} %fusion.9), channel_id=1, source_target_pairs={{1,0},{2,1},{3,2},{4,3},{5,4},{6,5},{7,6},{8,7},{9,8},{10,9},{11,1... | collective-permute-start | bytes 589832 | tf_op jit(solution)/shard_map/ppermute | solution.py:396
  18.2 7.5 %collective-permute-start.2 = (bf16[768,128]{1,0:T(8,128)(2,1)S(1)}, bf16[768,128]{1,0:T(8,128)(2,1)S(1)}, u32[]{:S(2)}, u32[]{:S(2)}) collective-permute-start(bf16[768,128]{1,0:T(8,128)(2,1)S(1)} %fusion.8), channel_id=1, source_target_pairs={{0,1},{1,2},{2,3},{3,4},{4,5},{5,6},{6,7},{7,8},{8,9},{9,10},{10,1... | collective-permute-start | bytes 589832 | tf_op jit(solution)/shard_map/ppermute | solution.py:396
  21.0 4.6 %copy-start.14 = (bf16[768,128]{1,0:T(8,128)(2,1)}, bf16[768,128]{1,0:T(8,128)(2,1)S(1)}, u32[]{:S(2)}) copy-start(bf16[768,128]{1,0:T(8,128)(2,1)S(1)} %collective-permute-done.3.right) | copy-start | bytes 589828
  25.6 0.7 copy-start.15
  70.6 4.1 %collective-permute-start.4 = (bf16[160,128]{1,0:T(8,128)(2,1)S(1)}, bf16[160,128]{1,0:T(8,128)(2,1)S(1)}, u32[]{:S(2)}, u32[]{:S(2)}) collective-permute-start(bf16[160,128]{1,0:T(8,128)(2,1)S(1)} %reduce_sum.12), channel_id=1, source_target_pairs={{0,16},{16,0},{32,48},{48,32},{64,80},{80,64},{96,112},{112,96},{1... | collective-permute-start | bytes 122888 | tf_op jit(solution)/shard_map/ppermute | solution.py:463
  74.8 5.6 %collective-permute-start.5 = (bf16[160,128]{1,0:T(8,128)(2,1)S(1)}, bf16[160,128]{1,0:T(8,128)(2,1)S(1)}, u32[]{:S(2)}, u32[]{:S(2)}) collective-permute-start(bf16[160,128]{1,0:T(8,128)(2,1)S(1)} %add_convert_fusion.1), channel_id=1, source_target_pairs={{0,32},{16,48},{32,0},{48,16},{64,96},{80,112},{96,64},{112,80},{1... | collective-permute-start | bytes 122888 | tf_op jit(solution)/shard_map/ppermute | solution.py:463
  80.4 5.6 %collective-permute-start.6 = (bf16[160,128]{1,0:T(8,128)(2,1)S(1)}, bf16[160,128]{1,0:T(8,128)(2,1)S(1)}, u32[]{:S(2)}, u32[]{:S(2)}) collective-permute-start(bf16[160,128]{1,0:T(8,128)(2,1)S(1)} %add_convert_fusion), channel_id=1, source_target_pairs={{0,64},{16,80},{32,96},{48,112},{64,0},{80,16},{96,32},{112,48},{1... | collective-permute-start | bytes 122888 | tf_op jit(solution)/shard_map/ppermute | solution.py:463

commit v5 on v4

--- a/solution.py
+++ b/solution.py
@@ -20,6 +20,13 @@
 
 def dot_nt(a, b):
     return lax.dot_general(a, b, (((1,), (1,)), ((), ())), preferred_element_type=F32)
+
+
+HALVES = (0, 1)
+
+
+def part(k):
+    return slice(k * 128, (k + 1) * 128)
 
 
 def pick_columns():
@@ -49,7 +56,7 @@
                 for ch in range(3):
                     if 2 * q + k + 1 < 48:
                         m[d, ch * 48 + 2 * q + k + 1, q // 2, q % 2, k * 12 + d * 3 + ch] = 1
-    return m.reshape(4, 144, 11 * 128)
+    return m.reshape(576, 11 * 128)
 
 
 def first_forward():
@@ -157,16 +164,14 @@
         turned = dot_nt(sel_mid[...], middle) + dot(sel_side[...], edges)
         at = pl.ds(pl.multiple_of(t * S, 8), S)
         for d in range(4):
-            ct[d, at, :] = turned[d * S : (d + 1) * S]
+            ct[at, d * 144 : (d + 1) * 144] = turned[d * S : (d + 1) * S]
 
     for n in range(0, 11, 2):
         width = min(2, 11 - n) * 128
-        part = jnp.zeros((T * S, width), F32)
-        for d in range(4):
-            part += dot(ct[d].astype(BF16), spread[d, :, n * 128 : n * 128 + width])
+        window = dot(ct[...].astype(BF16), spread[:, n * 128 : n * 128 + width])
         for k in range(width // 128):
             q = n + k
-            p2[1 : T + 1, q * S : (q + 1) * S, :] = part[:, k * 128 : (k + 1) * 128].reshape(T, S, 128)
+            p2[1 : T + 1, q * S : (q + 1) * S, :] = window[:, part(k)].reshape(T, S, 128)
 
     for p in range(TO + 1):
         dacc[p] = jnp.broadcast_to(b2[...], (480, 128))
@@ -180,12 +185,15 @@
                 to = slice((2 * q + e) * S, (2 * q + e + 1) * S)
                 of = (slice(q * S, (q + 1) * S), slice(e * 256, (e + 1) * 256))
                 masked = slope[of] * mk[to, :]
-                sl[t, to, :] = masked
-                hf[to, :] = pre[of] * masked
-        h6[:, 0:256] = hf[25:505, :].astype(BF16)
-        h6[:, 256:512] = hf[24:504, :].astype(BF16)
-        h6[:, 512:640] = hf[1:481, 128:256].astype(BF16)
-        h6[:, 640:768] = hf[0:480, 128:256].astype(BF16)
+                active = pre[of] * masked
+                for h in HALVES:
+                    sl[t, h, to, :] = masked[:, part(h)]
+                    hf[h, to, :] = active[:, part(h)]
+        for h in HALVES:
+            h6[:, part(h)] = hf[h, 25:505, :].astype(BF16)
+            h6[:, part(h + 2)] = hf[h, 24:504, :].astype(BF16)
+        h6[:, 512:640] = hf[1, 1:481, :].astype(BF16)
+        h6[:, 640:768] = hf[1, 0:480, :].astype(BF16)
 
     def odd_second(p):
         both = dot(h6_b[...], w2[:, 0:256])
@@ -225,11 +233,13 @@
         dt[p] = jnp.transpose(sdf[50:434, :] * core).astype(BF16)
 
     def delta(t, back, hdf, hd4):
-        hdf[...] = back * sl[t, 25:489, :]
-        hds[t + 1] = hdf[25:457, :].astype(BF16)
-        hd4[:, 0:256] = hdf[0:432, :].astype(BF16)
-        hd4[:, 256:512] = hdf[1:433, :].astype(BF16)
-        hd4[:, 512:768] = hdf[24:456, :].astype(BF16)
+        for h in HALVES:
+            hdf[h] = back[:, part(h)] * sl[t, h, 25:489, :]
+        for h in HALVES:
+            hds[t + 1, :, part(h)] = hdf[h, 25:457, :].astype(BF16)
+            hd4[:, part(h)] = hdf[h, 0:432, :].astype(BF16)
+            hd4[:, part(h + 2)] = hdf[h, 1:433, :].astype(BF16)
+            hd4[:, part(h + 4)] = hdf[h, 24:456, :].astype(BF16)
 
     def products(t, hd4):
         yt[t + 2, :, 0:432] = dot_nt(wx[:, 0:768], hd4[...]) + dot_nt(wx[:, 768:1024], hds[t + 1])
@@ -289,11 +299,14 @@
 
     def tangents(t, thf, th6):
         lhs = jnp.concatenate([tp[t], tp[t + 1], tp[t + 2]], axis=1)
-        thf[...] = dot(lhs, w1[:, 0:256]) * sl[t, 50:466, :]
-        th6[:, 0:256] = thf[25:409, :].astype(BF16)
-        th6[:, 256:512] = thf[24:408, :].astype(BF16)
-        th6[:, 512:640] = thf[1:385, 128:256].astype(BF16)
-        th6[:, 640:768] = thf[0:384, 128:256].astype(BF16)
+        raw = dot(lhs, w1[:, 0:256])
+        for h in HALVES:
+            thf[h] = raw[:, part(h)] * sl[t, h, 50:466, :]
+        for h in HALVES:
+            th6[:, part(h)] = thf[h, 25:409, :].astype(BF16)
+            th6[:, part(h + 2)] = thf[h, 24:408, :].astype(BF16)
+        th6[:, 512:640] = thf[1, 1:385, :].astype(BF16)
+        th6[:, 640:768] = thf[1, 0:384, :].astype(BF16)
         turned = jnp.concatenate([tpt[t], tpt[t + 1], tpt[t + 2]], axis=0)
         gacc[...] += dot(turned, hds[t + 1, 0:416, :])
 
@@ -322,8 +335,8 @@
             for rp in range(2):
                 for cp in range(2):
                     start = a * 48 + (b + rp) * 12 + cp * 3
-                    part = (rp * 2 + cp) * 64
-                    total += gacc[start : start + 9, part : part + 64]
+                    tap = (rp * 2 + cp) * 64
+                    total += gacc[start : start + 9, tap : tap + 64]
             gf[a * 27 + b * 9 : a * 27 + b * 9 + 9, :] = total
 
     left_half = lax.broadcasted_iota(jnp.int32, (8, 128), 1) < 64
@@ -352,20 +365,20 @@
         in_specs=[pl.BlockSpec(memory_space=pltpu.SMEM)] + [vmem] * 13,
         out_specs=(vmem, vmem),
         scratch_shapes=[
-            vm((4, T * S, 144)),
+            vm((T * S, 576)),
             vm((T + 2, 264, 128)),
             vm((528, 256)),
-            vm((T, 528, 256)),
-            vm((528, 256)),
-            vm((528, 256)),
+            vm((T, 2, 528, 128)),
+            vm((2, 528, 128)),
+            vm((2, 528, 128)),
             vm((480, 768), BF16),
             vm((480, 768), BF16),
             vm((TO + 1, 480, 128)),
             vm((496, 128)),
             vm((TO, 464, 512), BF16),
             vm((TO, 128, 384), BF16),
-            vm((464, 256)),
-            vm((464, 256)),
+            vm((2, 464, 128)),
+            vm((2, 464, 128)),
             vm((432, 768), BF16),
             vm((432, 768), BF16),
             vm((T + 1, 432, 256), BF16),
@@ -373,8 +386,8 @@
             vm((T * 48, 1024), BF16),
             vm((T + 2, 416, 128), BF16),
             vm((T + 2, 48, 416), BF16),
-            vm((416, 256)),
-            vm((416, 256)),
+            vm((2, 416, 128)),
+            vm((2, 416, 128)),
             vm((384, 768), BF16),
             vm((384, 768), BF16),
             vm((384, 768)),
@@ -454,24 +467,24 @@
     )
 
     scale = 1.0 / (T * rows * cols)
-    part = lax.all_to_all(terms, "wa", 0, 0, tiled=True)
-    part = part.astype(F32).sum(0)
+    terms = lax.all_to_all(terms, "wa", 0, 0, tiled=True)
+    terms = terms.astype(F32).sum(0)
     step = 1
     while step < lax.axis_size("ha"):
-        sent = part.astype(BF16)
+        sent = terms.astype(BF16)
         pairs = [(i, i ^ step) for i in range(lax.axis_size("ha"))]
-        part = sent.astype(F32) + lax.ppermute(sent, "ha", pairs).astype(F32)
+        terms = sent.astype(F32) + lax.ppermute(sent, "ha", pairs).astype(F32)
         step *= 2
-    part = part * scale
+    terms = terms * scale
     lane = lax.broadcasted_iota(jnp.int32, (128, 16), 0)
     mine = lax.broadcasted_iota(jnp.int32, (128, 16), 1)
     pick = (lane == (mine // 8) * 64 + ha * 8 + mine % 8).astype(F32)
-    second = jnp.dot(part[0:120], pick, precision=lax.Precision.HIGHEST, preferred_element_type=F32)
+    second = jnp.dot(terms[0:120], pick, precision=lax.Precision.HIGHEST, preferred_element_type=F32)
     second = second.reshape(5, 3, 8, 2, 8)
     keep = [TAPS.index((b, c)) for b in range(3) for c in range(3)]
     second = second.transpose(0, 3, 1, 4, 2).reshape(10, 3, 8, 8)
     grad_second = jnp.stack([second[k] for k in keep], axis=1).reshape(3, 3, 3, 8, 8)
-    first = part[96:160]
+    first = terms[96:160]
     grad_first = jnp.concatenate([first[0:24, 0:64], first[24:53, 0:64], first[24:53, 64:128]], axis=0)
     grad_first = grad_first[:81].reshape(3, 3, 3, 3, 64)
     return (input_grad, grad_first, grad_second)

time: 88.2 us -> 87.6 us (level)
  no operation moved by 1% of the time
where the time goes in v5:
time: 87.6 us; the launch traced here: 87.3 us
  Pallas kernels  28.1 us (32%)
  waiting for transfers between devices  16.5 us (19%)
  blocking collectives  15.6 us (18%)
  starting transfers between devices  14.6 us (17%)
  local copies, waits for them, and re-layouts  7.07 us (8%)
  matrix products  2.38 us (3%)
  other arithmetic  2.01 us (2%)
  between operations  1.11 us (1%)
    pallas_call x1, Pallas kernels, run_kernel(): pl.pallas_call(kernel, out_shape=(jax.ShapeDtypeStruct((3, T, 32, 32), F3...  28.1 us
    all_to_all x1, blocking collectives, body(): terms = lax.all_to_all(terms, 'wa', 0, 0, tiled=True)  15.6 us
    ppermute x3, waiting for transfers between devices, body(): terms = sent.astype(F32) + lax.ppermute(sent, 'ha', pairs).astype(F32)  9.66 us
    ppermute x2, starting transfers between devices, swapped(): lax.ppermute(to_prev, axis, [(j, i) for i, j in ring])  6.67 us
    ppermute x2, waiting for transfers between devices, swapped(): lax.ppermute(to_next, axis, ring)  5.68 us
    ppermute x3, starting transfers between devices, body(): terms = sent.astype(F32) + lax.ppermute(sent, 'ha', pairs).astype(F32)  5.56 us
    unnamed x41, local copies, waits for them, and re-layouts  2.38 us
    ppermute x2, starting transfers between devices, swapped(): lax.ppermute(to_next, axis, ring)  2.32 us
  transfers between devices with their start and end apart: 7, of which 6 were waited for; matrix products, arithmetic and copies ran while one was open for 6% of the time, Pallas kernels for 0%

profile of v5, /device:TPU:0, one launch (start us, length us, event | category | flops | bytes accessed | tf_op | source)
XLA Modules:
  0.0 87.3 jit_solution(16132218476104524681)
XLA Ops:
  0.6 0.0 copy-start.11
  0.6 0.0 copy-start.12
  0.7 0.0 copy-start.4
  0.7 0.0 copy-start.13
  0.7 1.0 %fusion.43 = (bf16[3,17,8,32]{3,2,1,0:T(8,128)(2,1)S(1)}, bf16[3,17,8,32]{3,2,1,0:T(8,128)(2,1)S(1)}) fusion(bf16[3,17,32,32]{3,2,1,0:T(8,128)(2,1)} %param.12), kind=kLoop, calls=%fused_computation.92 | loop fusion | bytes 104448 | tf_op jit(solution)/shard_map/slice | solution.py:425
  1.7 0.9 %fusion.42 = (bf16[9,2,16,128]{3,2,1,0:T(8,128)(2,1)S(1)}, bf16[9,2,16,128]{3,2,1,0:T(8,128)(2,1)S(1)}) fusion(bf16[9,16,16,128]{3,2,1,0:T(8,128)(2,1)} %param.17), kind=kLoop, calls=%fused_computation.91 | loop fusion | bytes 294912 | tf_op jit(solution)/shard_map/slice | solution.py:425
  2.7 0.0 copy-start.8
  2.7 2.1 %collective-permute-start = (bf16[696,128]{1,0:T(8,128)(2,1)S(1)}, bf16[696,128]{1,0:T(8,128)(2,1)S(1)}, u32[]{:S(2)}, u32[]{:S(2)}) collective-permute-start(bf16[696,128]{1,0:T(8,128)(2,1)S(1)} %fusion.10), channel_id=1, source_target_pairs={{0,16},{16,32},{32,48},{48,64},{64,80},{80,96},{96,112},{112,0},{1... | collective-permute-start | bytes 534536 | tf_op jit(solution)/shard_map/ppermute | solution.py:409
  4.8 4.8 %collective-permute-start.1 = (bf16[696,128]{1,0:T(8,128)(2,1)S(1)}, bf16[696,128]{1,0:T(8,128)(2,1)S(1)}, u32[]{:S(2)}, u32[]{:S(2)}) collective-permute-start(bf16[696,128]{1,0:T(8,128)(2,1)S(1)} %fusion.11), channel_id=1, source_target_pairs={{16,0},{32,16},{48,32},{64,48},{80,64},{96,80},{112,96},{0,112},{1... | collective-permute-start | bytes 534536 | tf_op jit(solution)/shard_map/ppermute | solution.py:409
  9.6 0.0 copy-done.13
  9.7 0.0 copy-done.11
  9.7 0.2 fusion.22
  9.8 0.0 copy-done.12
  9.8 0.0 copy-start.7
  9.9 0.2 fusion.20
  10.0 0.0 copy-done.4
  10.0 0.4 convolution_convert_fusion
  10.5 0.8 copy.61.wx
  11.3 0.0 copy-done.8
  11.3 0.3 convolution_add_fusion.2
  11.5 0.0 copy-done.7
  11.5 0.0 copy-start.5
  11.6 0.2 convolution_add_fusion.1
  11.8 0.0 copy-start.9
  11.8 0.3 fusion.2
  12.0 0.1 copy-done.6
  12.2 0.3 convolution_add_fusion.5
  12.4 0.0 copy-done.5
  12.5 0.2 convolution_add_fusion.4
  12.7 0.0 copy-done.9
  12.7 0.3 fusion.3
  13.0 1.1 %collective-permute-done = bf16[696,128]{1,0:T(8,128)(2,1)S(1)} collective-permute-done((bf16[696,128]{1,0:T(8,128)(2,1)S(1)}, bf16[696,128]{1,0:T(8,128)(2,1)S(1)}, u32[]{:S(2)}, u32[]{:S(2)}) %collective-permute-start) | collective-permute-done | bytes 178208 | tf_op jit(solution)/shard_map/ppermute | solution.py:409
  14.1 0.0 collective-permute-done.1
  14.2 0.1 pad_maximum_fusion.1.clip
  14.3 0.0 copy-start.3
  14.4 0.2 slice_bitcast_fusion
  14.6 0.6 copy-done
  15.2 0.2 copy.37
  15.4 0.2 copy-done.3
  15.6 0.1 pad_maximum_fusion.up
  15.7 0.0 copy-start.1
  15.7 0.1 slice_bitcast_fusion.2
  16.0 1.8 %collective-permute-start.3 = (bf16[768,128]{1,0:T(8,128)(2,1)S(1)}, bf16[768,128]{1,0:T(8,128)(2,1)S(1)}, u32[]{:S(2)}, u32[]{:S(2)}) collective-permute-start(bf16[768,128]{1,0:T(8,128)(2,1)S(1)} %fusion.9), channel_id=1, source_target_pairs={{1,0},{2,1},{3,2},{4,3},{5,4},{6,5},{7,6},{8,7},{9,8},{10,9},{11,1... | collective-permute-start | bytes 589832 | tf_op jit(solution)/shard_map/ppermute | solution.py:409
  17.8 0.2 copy.35
  18.2 0.3 collective-permute-start.2
  18.4 0.7 pad_add_fusion.pos
  19.1 0.8 pad_maximum_fusion.2.w1
  19.9 1.1 %collective-permute-done.3.right = bf16[768,128]{1,0:T(8,128)(2,1)S(1)} collective-permute-done((bf16[768,128]{1,0:T(8,128)(2,1)S(1)}, bf16[768,128]{1,0:T(8,128)(2,1)S(1)}, u32[]{:S(2)}, u32[]{:S(2)}) %collective-permute-start.3) | collective-permute-done | bytes 196640 | tf_op jit(solution)/shard_map/ppermute | solution.py:409
  21.0 4.6 %collective-permute-done.2.left = bf16[768,128]{1,0:T(8,128)(2,1)S(1)} collective-permute-done((bf16[768,128]{1,0:T(8,128)(2,1)S(1)}, bf16[768,128]{1,0:T(8,128)(2,1)S(1)}, u32[]{:S(2)}, u32[]{:S(2)}) %collective-permute-start.2) | collective-permute-done | bytes 196640 | tf_op jit(solution)/shard_map/ppermute | solution.py:409
  25.6 0.7 copy-done.15
  26.3 28.1 %shard_map.139 = (f32[3,17,32,32]{3,2,1,0:T(8,128)}, bf16[16,160,128]{2,1,0:T(8,128)(2,1)}) custom-call(s32[4]{0:T(128)} %pad_add_fusion.pos, bf16[3,17,48,32]{3,2,1,0:T(8,128)(2,1)} %copy-done, bf16[768,128]{1,0:T(8,128)(2,1)} %copy-done.15, bf16[768,128]{1,0:T(8,128)(2,1)} %copy-done.14, bf16[9,20,16,128]{3,2,1,0:T(8,128)(2,1)} %copy-done.1, ...), custom_call_target="tpu_custom_call" | custom-call | flops 10000000000 | bytes 20000000 | tf_op jit(solution)/shard_map/pallas_call | solution.py:359
  54.4 15.6 %all_to_all.5 = bf16[16,160,128]{2,1,0:T(8,128)(2,1)S(1)} all-to-all(bf16[16,160,128]{2,1,0:T(8,128)(2,1)} %get-tuple-element.6), channel_id=1, replica_groups=mesh['ha'=8,'wa'=16] {'wa'}, dimensions={0} | all-to-all | bytes 1310720 | tf_op jit(solution)/shard_map/all_to_all | solution.py:470
  70.0 0.1 reduce_sum.12
  70.1 0.1 collective-permute-start.4
  70.2 4.0 %collective-permute-done.4 = bf16[160,128]{1,0:T(8,128)(2,1)S(1)} collective-permute-done((bf16[160,128]{1,0:T(8,128)(2,1)S(1)}, bf16[160,128]{1,0:T(8,128)(2,1)S(1)}, u32[]{:S(2)}, u32[]{:S(2)}) %collective-permute-start.4) | collective-permute-done | bytes 40992 | tf_op jit(solution)/shard_map/ppermute | solution.py:476
  74.2 3.2 %collective-permute-start.5 = (bf16[160,128]{1,0:T(8,128)(2,1)S(1)}, bf16[160,128]{1,0:T(8,128)(2,1)S(1)}, u32[]{:S(2)}, u32[]{:S(2)}) collective-permute-start(bf16[160,128]{1,0:T(8,128)(2,1)S(1)} %add_convert_fusion.1), channel_id=1, source_target_pairs={{0,32},{16,48},{32,0},{48,16},{64,96},{80,112},{96,64},{112,80},{1... | collective-permute-start | bytes 122888 | tf_op jit(solution)/shard_map/ppermute | solution.py:476
  77.3 2.4 %collective-permute-done.5 = bf16[160,128]{1,0:T(8,128)(2,1)S(1)} collective-permute-done((bf16[160,128]{1,0:T(8,128)(2,1)S(1)}, bf16[160,128]{1,0:T(8,128)(2,1)S(1)}, u32[]{:S(2)}, u32[]{:S(2)}) %collective-permute-start.5) | collective-permute-done | bytes 40992 | tf_op jit(solution)/shard_map/ppermute | solution.py:476
  79.8 2.3 %collective-permute-start.6 = (bf16[160,128]{1,0:T(8,128)(2,1)S(1)}, bf16[160,128]{1,0:T(8,128)(2,1)S(1)}, u32[]{:S(2)}, u32[]{:S(2)}) collective-permute-start(bf16[160,128]{1,0:T(8,128)(2,1)S(1)} %add_convert_fusion), channel_id=1, source_target_pairs={{0,64},{16,80},{32,96},{48,112},{64,0},{80,16},{96,32},{112,48},{1... | collective-permute-start | bytes 122888 | tf_op jit(solution)/shard_map/ppermute | solution.py:476
  82.1 3.3 %collective-permute-done.6 = bf16[160,128]{1,0:T(8,128)(2,1)S(1)} collective-permute-done((bf16[160,128]{1,0:T(8,128)(2,1)S(1)}, bf16[160,128]{1,0:T(8,128)(2,1)S(1)}, u32[]{:S(2)}, u32[]{:S(2)}) %collective-permute-start.6) | collective-permute-done | bytes 40992 | tf_op jit(solution)/shard_map/ppermute | solution.py:476
  85.4 0.1 slice.131
  85.5 0.2 fusion.12
  85.7 0.2 reshape.79
  86.0 0.7 copy.50
  86.6 0.6 reshape.78
  (43 shorter events, 0.5 us)
Async XLA Ops:
  0.6 9.0 %copy-start.11 = (bf16[384,81]{1,0:T(8,128)(2,1)S(1)}, bf16[384,81]{1,0:T(8,128)(2,1)}, u32[]{:S(2)}) copy-start(bf16[384,81]{1,0:T(8,128)(2,1)} %constant.101) | copy-start | bytes 186628
  0.6 9.2 %copy-start.12 = (bf16[384,81]{1,0:T(8,128)(2,1)S(1)}, bf16[384,81]{1,0:T(8,128)(2,1)}, u32[]{:S(2)}) copy-start(bf16[384,81]{1,0:T(8,128)(2,1)} %constant.97) | copy-start | bytes 186628
  0.7 9.4 %copy-start.4 = (bf16[16,81,80]{1,2,0:T(8,128)(2,1)S(1)}, bf16[16,81,80]{1,2,0:T(8,128)(2,1)}, u32[]{:S(2)}) copy-start(bf16[16,81,80]{1,2,0:T(8,128)(2,1)} %constant.72.clone) | copy-start | bytes 622084
  0.7 9.0 %copy-start.13 = (bf16[3,3,3,3,64]{4,3,2,1,0:T(4,128)(2,1)S(1)}, bf16[3,3,3,3,64]{4,3,2,1,0:T(4,128)(2,1)}, u32[]{:S(2)}) copy-start(bf16[3,3,3,3,64]{4,3,2,1,0:T(4,128)(2,1)} %param.13) | copy-start | bytes 31108
  2.7 8.6 %copy-start.8 = (bf16[384,81]{1,0:T(8,128)(2,1)S(1)}, bf16[384,81]{1,0:T(8,128)(2,1)}, u32[]{:S(2)}) copy-start(bf16[384,81]{1,0:T(8,128)(2,1)} %constant.102) | copy-start | bytes 186628
  2.7 11.3 %collective-permute-start = (bf16[696,128]{1,0:T(8,128)(2,1)S(1)}, bf16[696,128]{1,0:T(8,128)(2,1)S(1)}, u32[]{:S(2)}, u32[]{:S(2)}) collective-permute-start(bf16[696,128]{1,0:T(8,128)(2,1)S(1)} %fusion.10), channel_id=1, source_target_pairs={{0,16},{16,32},{32,48},{48,64},{64,80},{80,96},{96,112},{112,0},{1... | collective-permute-start | bytes 534536 | tf_op jit(solution)/shard_map/ppermute | solution.py:409
  4.8 9.3 %collective-permute-start.1 = (bf16[696,128]{1,0:T(8,128)(2,1)S(1)}, bf16[696,128]{1,0:T(8,128)(2,1)S(1)}, u32[]{:S(2)}, u32[]{:S(2)}) collective-permute-start(bf16[696,128]{1,0:T(8,128)(2,1)S(1)} %fusion.11), channel_id=1, source_target_pairs={{16,0},{32,16},{48,32},{64,48},{80,64},{96,80},{112,96},{0,112},{1... | collective-permute-start | bytes 534536 | tf_op jit(solution)/shard_map/ppermute | solution.py:409
  9.8 1.7 %copy-start.7 = (bf16[384,81]{1,0:T(8,128)(2,1)S(1)}, bf16[384,81]{1,0:T(8,128)(2,1)}, u32[]{:S(2)}) copy-start(bf16[384,81]{1,0:T(8,128)(2,1)} %constant.103) | copy-start | bytes 186628
  10.4 1.3 %copy-start.10 = (bf16[384,81]{1,0:T(8,128)(2,1)S(1)}, bf16[384,81]{1,0:T(8,128)(2,1)}, u32[]{:S(2)}) copy-start(bf16[384,81]{1,0:T(8,128)(2,1)} %constant.104) | copy-start | bytes 186628
  11.3 0.9 %copy-start.6 = (bf16[384,81]{1,0:T(8,128)(2,1)S(1)}, bf16[384,81]{1,0:T(8,128)(2,1)}, u32[]{:S(2)}) copy-start(bf16[384,81]{1,0:T(8,128)(2,1)} %constant.98) | copy-start | bytes 186628
  11.5 0.9 %copy-start.5 = (bf16[384,81]{1,0:T(8,128)(2,1)S(1)}, bf16[384,81]{1,0:T(8,128)(2,1)}, u32[]{:S(2)}) copy-start(bf16[384,81]{1,0:T(8,128)(2,1)} %constant.99) | copy-start | bytes 186628
  11.8 0.9 %copy-start.9 = (bf16[384,81]{1,0:T(8,128)(2,1)S(1)}, bf16[384,81]{1,0:T(8,128)(2,1)}, u32[]{:S(2)}) copy-start(bf16[384,81]{1,0:T(8,128)(2,1)} %constant.100) | copy-start | bytes 186628
  12.7 1.5 %copy-start.2 = (bf16[3,17,32,32]{3,2,1,0:T(8,128)(2,1)S(1)}, bf16[3,17,32,32]{3,2,1,0:T(8,128)(2,1)}, u32[]{:S(2)}) copy-start(bf16[3,17,32,32]{3,2,1,0:T(8,128)(2,1)} %param.12) | copy-start | bytes 313348
  14.3 0.8 copy-start
  14.3 1.3 %copy-start.3 = (bf16[9,16,16,128]{3,2,1,0:T(8,128)(2,1)S(1)}, bf16[9,16,16,128]{3,2,1,0:T(8,128)(2,1)}, u32[]{:S(2)}) copy-start(bf16[9,16,16,128]{3,2,1,0:T(8,128)(2,1)} %param.17) | copy-start | bytes 1769476
  15.7 2.4 %copy-start.1 = (bf16[9,20,16,128]{3,2,1,0:T(8,128)(2,1)}, bf16[9,20,16,128]{3,2,1,0:T(8,128)(2,1)S(1)}, u32[]{:S(2)}) copy-start(bf16[9,20,16,128]{3,2,1,0:T(8,128)(2,1)S(1)} %pad_maximum_fusion.up) | copy-start | bytes 2211844
  16.0 5.0 %collective-permute-start.3 = (bf16[768,128]{1,0:T(8,128)(2,1)S(1)}, bf16[768,128]{1,0:T(8,128)(2,1)S(1)}, u32[]{:S(2)}, u32[]{:S(2)}) collective-permute-start(bf16[768,128]{1,0:T(8,128)(2,1)S(1)} %fusion.9), channel_id=1, source_target_pairs={{1,0},{2,1},{3,2},{4,3},{5,4},{6,5},{7,6},{8,7},{9,8},{10,9},{11,1... | collective-permute-start | bytes 589832 | tf_op jit(solution)/shard_map/ppermute | solution.py:409
  18.2 7.5 %collective-permute-start.2 = (bf16[768,128]{1,0:T(8,128)(2,1)S(1)}, bf16[768,128]{1,0:T(8,128)(2,1)S(1)}, u32[]{:S(2)}, u32[]{:S(2)}) collective-permute-start(bf16[768,128]{1,0:T(8,128)(2,1)S(1)} %fusion.8), channel_id=1, source_target_pairs={{0,1},{1,2},{2,3},{3,4},{4,5},{5,6},{6,7},{7,8},{8,9},{9,10},{10,1... | collective-permute-start | bytes 589832 | tf_op jit(solution)/shard_map/ppermute | solution.py:409
  21.0 4.6 %copy-start.14 = (bf16[768,128]{1,0:T(8,128)(2,1)}, bf16[768,128]{1,0:T(8,128)(2,1)S(1)}, u32[]{:S(2)}) copy-start(bf16[768,128]{1,0:T(8,128)(2,1)S(1)} %collective-permute-done.3.right) | copy-start | bytes 589828
  25.6 0.7 copy-start.15
  70.1 4.1 %collective-permute-start.4 = (bf16[160,128]{1,0:T(8,128)(2,1)S(1)}, bf16[160,128]{1,0:T(8,128)(2,1)S(1)}, u32[]{:S(2)}, u32[]{:S(2)}) collective-permute-start(bf16[160,128]{1,0:T(8,128)(2,1)S(1)} %reduce_sum.12), channel_id=1, source_target_pairs={{0,16},{16,0},{32,48},{48,32},{64,80},{80,64},{96,112},{112,96},{1... | collective-permute-start | bytes 122888 | tf_op jit(solution)/shard_map/ppermute | solution.py:476
  74.2 5.6 %collective-permute-start.5 = (bf16[160,128]{1,0:T(8,128)(2,1)S(1)}, bf16[160,128]{1,0:T(8,128)(2,1)S(1)}, u32[]{:S(2)}, u32[]{:S(2)}) collective-permute-start(bf16[160,128]{1,0:T(8,128)(2,1)S(1)} %add_convert_fusion.1), channel_id=1, source_target_pairs={{0,32},{16,48},{32,0},{48,16},{64,96},{80,112},{96,64},{112,80},{1... | collective-permute-start | bytes 122888 | tf_op jit(solution)/shard_map/ppermute | solution.py:476
  79.8 5.6 %collective-permute-start.6 = (bf16[160,128]{1,0:T(8,128)(2,1)S(1)}, bf16[160,128]{1,0:T(8,128)(2,1)S(1)}, u32[]{:S(2)}, u32[]{:S(2)}) collective-permute-start(bf16[160,128]{1,0:T(8,128)(2,1)S(1)} %add_convert_fusion), channel_id=1, source_target_pairs={{0,64},{16,80},{32,96},{48,112},{64,0},{80,16},{96,32},{112,48},{1... | collective-permute-start | bytes 122888 | tf_op jit(solution)/shard_map/ppermute | solution.py:476

commit v6 on v5

--- a/solution.py
+++ b/solution.py
@@ -97,11 +97,19 @@
 
 
 def kernel(
-    pos, clip, left, right, up, sel_mid, sel_side, spread, w1, b1, w_second, b2, wx, place,
+    pos, clip, left, right, up_far, sel_mid, sel_side, spread, w1, b1, w_second, b2, wx, place_far,
     x_out, g_out,
     ct, p2, mk, sl, hf_a, hf_b, h6_a, h6_b, dacc, sdf, d4, dt, hdf_a, hdf_b, hd4_a, hd4_b, hds, yt, xs, tp, tpt,
-    thf_a, thf_b, th6_a, th6_b, oacc, gacc, gf, strips, upf, w2, wb,
+    thf_a, thf_b, th6_a, th6_b, oacc, gacc, gf, strips, upf, w2, wb, near, up, place, sems,
 ):
+    copies = [
+        pltpu.make_async_copy(left, near.at[0], sems.at[0]),
+        pltpu.make_async_copy(right, near.at[1], sems.at[1]),
+        pltpu.make_async_copy(up_far, up, sems.at[2]),
+        pltpu.make_async_copy(place_far, place, sems.at[3]),
+    ]
+    for copy in copies:
+        copy.start()
     r0, c0, rows, cols = pos[0], pos[1], pos[2], pos[3]
 
     def inside(r, c):
@@ -142,12 +150,15 @@
                     to = (n * 4 + dq * 2 + ds) * 128
                     wb[to : to + 128, rp * 128 : (rp + 1) * 128] = jnp.transpose(pair).astype(BF16)
 
-    strips[0] = jnp.where(c0 > 0, left[...].astype(F32), 0.0)
-    strips[1] = jnp.where(c0 + 32 < cols, right[...].astype(F32), 0.0)
     h6_b[...] = jnp.zeros(h6_b.shape, BF16)
     hd4_b[...] = jnp.zeros(hd4_b.shape, BF16)
     hds[0] = jnp.zeros(hds.shape[1:], BF16)
     th6_b[...] = jnp.zeros(th6_b.shape, BF16)
+
+    copies[0].wait()
+    copies[1].wait()
+    strips[0] = jnp.where(c0 > 0, near[0].astype(F32), 0.0)
+    strips[1] = jnp.where(c0 + 32 < cols, near[1].astype(F32), 0.0)
 
     @pl.loop(0, T, unroll=True)
     def _(t):
@@ -217,6 +228,7 @@
     at384 = lax.broadcasted_iota(jnp.int32, (384, 128), 0)
     core = jnp.where(at384 % S < 16, 1.0, 0.0)
 
+    copies[2].wait()
     for p in range(TO):
         slope = jnp.where(dacc[p + 1] > 0, 1.0, LEAK)
         for q in range(20):
@@ -283,6 +295,7 @@
         tpt[t + 1] = jnp.where(core_first, wide[:, 0:416], 0.0).astype(BF16)
         tp[t + 1, :, 0:48] = jnp.transpose(wide)[0:416].astype(BF16)
 
+    copies[3].wait()
     for first in range(0, T, 6):
         frames = range(first, min(first + 6, T))
         group = dot(xs[first * 48 : (frames[-1] + 1) * 48, :], place[...])
@@ -356,13 +369,14 @@
 def run_kernel(*args):
     vm = lambda shape, kind=F32: pltpu.VMEM(shape, kind)
     vmem = pl.BlockSpec(memory_space=pltpu.VMEM)
+    far = pl.BlockSpec(memory_space=pl.ANY)
     return pl.pallas_call(
         kernel,
         out_shape=(
             jax.ShapeDtypeStruct((3, T, 32, 32), F32),
             jax.ShapeDtypeStruct((16, 160, 128), BF16),
         ),
-        in_specs=[pl.BlockSpec(memory_space=pltpu.SMEM)] + [vmem] * 13,
+        in_specs=[pl.BlockSpec(memory_space=pltpu.SMEM)] + [vmem, far, far, far] + [vmem] * 8 + [far],
         out_specs=(vmem, vmem),
         scratch_shapes=[
             vm((T * S, 576)),
@@ -397,6 +411,10 @@
             vm((480, 128)),
             vm((768, 384), BF16),
             vm((1536, 256), BF16),
+            vm((2, 768, 128), BF16),
+            vm((TO, 20, 16, 128), BF16),
+            vm((1024, 576), BF16),
+            pltpu.SemaphoreType.DMA((4,)),
         ],
         compiler_params=pltpu.CompilerParams(vmem_limit_bytes=60 * 1024 * 1024),
         cost_estimate=pl.CostEstimate(flops=10**10, bytes_accessed=2 * 10**7, transcendentals=0),

time: 87.6 us -> 89.1 us (1.017)
  Pallas kernels: 28.1 us -> 29.5 us
    pallas_call x1, Pallas kernels: 28.1 us -> 29.5 us  [run_kernel(): pl.pallas_call(kernel, out_shape=(jax.ShapeDtypeStruct((3, T, 32, 32), F3...]
  transfers between devices with their start and end apart: 7 -> 7, of which waited for: 6 -> 6; matrix products, arithmetic and copies ran while one was open for 6% -> 5% of each run, Pallas kernels for 0% -> 0%
where the time goes in v6:
time: 89.1 us; the launch traced here: 88.7 us
  Pallas kernels  29.5 us (33%)
  waiting for transfers between devices  16.5 us (19%)
  blocking collectives  15.6 us (18%)
  starting transfers between devices  14.5 us (16%)
  local copies, waits for them, and re-layouts  7.07 us (8%)
  matrix products  2.38 us (3%)
  other arithmetic  2.01 us (2%)
  between operations  1.12 us (1%)
    pallas_call x1, Pallas kernels, run_kernel(): pl.pallas_call(kernel, out_shape=(jax.ShapeDtypeStruct((3, T, 32, 32), F3...  29.5 us
    all_to_all x1, blocking collectives, body(): terms = lax.all_to_all(terms, 'wa', 0, 0, tiled=True)  15.6 us
    ppermute x3, waiting for transfers between devices, body(): terms = sent.astype(F32) + lax.ppermute(sent, 'ha', pairs).astype(F32)  9.69 us
    ppermute x2, starting transfers between devices, swapped(): lax.ppermute(to_prev, axis, [(j, i) for i, j in ring])  6.67 us
    ppermute x2, waiting for transfers between devices, swapped(): lax.ppermute(to_next, axis, ring)  5.68 us
    ppermute x3, starting transfers between devices, body(): terms = sent.astype(F32) + lax.ppermute(sent, 'ha', pairs).astype(F32)  5.54 us
    unnamed x41, local copies, waits for them, and re-layouts  2.38 us
    ppermute x2, starting transfers between devices, swapped(): lax.ppermute(to_next, axis, ring)  2.32 us
  transfers between devices with their start and end apart: 7, of which 6 were waited for; matrix products, arithmetic and copies ran while one was open for 5% of the time, Pallas kernels for 0%

profile of v6, /device:TPU:0, one launch (start us, length us, event | category | flops | bytes accessed | tf_op | source)
XLA Modules:
  0.0 88.7 jit_solution(6584940853604622467)
XLA Ops:
  0.6 0.0 copy-start.11
  0.6 0.0 copy-start.12
  0.7 0.0 copy-start.4
  0.7 0.0 copy-start.13
  0.7 1.0 %fusion.43 = (bf16[3,17,8,32]{3,2,1,0:T(8,128)(2,1)S(1)}, bf16[3,17,8,32]{3,2,1,0:T(8,128)(2,1)S(1)}) fusion(bf16[3,17,32,32]{3,2,1,0:T(8,128)(2,1)} %param.12), kind=kLoop, calls=%fused_computation.92 | loop fusion | bytes 104448 | tf_op jit(solution)/shard_map/slice | solution.py:443
  1.7 0.9 %fusion.42 = (bf16[9,2,16,128]{3,2,1,0:T(8,128)(2,1)S(1)}, bf16[9,2,16,128]{3,2,1,0:T(8,128)(2,1)S(1)}) fusion(bf16[9,16,16,128]{3,2,1,0:T(8,128)(2,1)} %param.17), kind=kLoop, calls=%fused_computation.91 | loop fusion | bytes 294912 | tf_op jit(solution)/shard_map/slice | solution.py:443
  2.7 0.0 copy-start.8
  2.7 2.1 %collective-permute-start = (bf16[696,128]{1,0:T(8,128)(2,1)S(1)}, bf16[696,128]{1,0:T(8,128)(2,1)S(1)}, u32[]{:S(2)}, u32[]{:S(2)}) collective-permute-start(bf16[696,128]{1,0:T(8,128)(2,1)S(1)} %fusion.10), channel_id=1, source_target_pairs={{0,16},{16,32},{32,48},{48,64},{64,80},{80,96},{96,112},{112,0},{1... | collective-permute-start | bytes 534536 | tf_op jit(solution)/shard_map/ppermute | solution.py:427
  4.8 4.8 %collective-permute-start.1 = (bf16[696,128]{1,0:T(8,128)(2,1)S(1)}, bf16[696,128]{1,0:T(8,128)(2,1)S(1)}, u32[]{:S(2)}, u32[]{:S(2)}) collective-permute-start(bf16[696,128]{1,0:T(8,128)(2,1)S(1)} %fusion.11), channel_id=1, source_target_pairs={{16,0},{32,16},{48,32},{64,48},{80,64},{96,80},{112,96},{0,112},{1... | collective-permute-start | bytes 534536 | tf_op jit(solution)/shard_map/ppermute | solution.py:427
  9.6 0.0 copy-done.13
  9.7 0.0 copy-done.11
  9.7 0.2 fusion.22
  9.8 0.0 copy-done.12
  9.8 0.0 copy-start.7
  9.9 0.2 fusion.20
  10.0 0.0 copy-done.4
  10.0 0.4 convolution_convert_fusion
  10.5 0.8 copy.61.wx
  11.3 0.0 copy-done.8
  11.3 0.3 convolution_add_fusion.2
  11.5 0.0 copy-done.7
  11.5 0.0 copy-start.5
  11.6 0.2 convolution_add_fusion.1
  11.8 0.0 copy-start.9
  11.8 0.3 fusion.2
  12.0 0.1 copy-done.6
  12.2 0.3 convolution_add_fusion.5
  12.4 0.0 copy-done.5
  12.5 0.2 convolution_add_fusion.4
  12.7 0.0 copy-done.9
  12.7 0.3 fusion.3
  13.0 1.1 %collective-permute-done = bf16[696,128]{1,0:T(8,128)(2,1)S(1)} collective-permute-done((bf16[696,128]{1,0:T(8,128)(2,1)S(1)}, bf16[696,128]{1,0:T(8,128)(2,1)S(1)}, u32[]{:S(2)}, u32[]{:S(2)}) %collective-permute-start) | collective-permute-done | bytes 178208 | tf_op jit(solution)/shard_map/ppermute | solution.py:427
  14.1 0.0 collective-permute-done.1
  14.2 0.1 pad_maximum_fusion.1.clip
  14.3 0.0 copy-start.3
  14.4 0.2 slice_bitcast_fusion
  14.6 0.6 copy-done
  15.2 0.2 copy.37
  15.4 0.2 copy-done.3
  15.6 0.1 pad_maximum_fusion.up_far
  15.7 0.0 copy-start.1
  15.7 0.1 slice_bitcast_fusion.2
  16.0 1.8 %collective-permute-start.3 = (bf16[768,128]{1,0:T(8,128)(2,1)S(1)}, bf16[768,128]{1,0:T(8,128)(2,1)S(1)}, u32[]{:S(2)}, u32[]{:S(2)}) collective-permute-start(bf16[768,128]{1,0:T(8,128)(2,1)S(1)} %fusion.9), channel_id=1, source_target_pairs={{1,0},{2,1},{3,2},{4,3},{5,4},{6,5},{7,6},{8,7},{9,8},{10,9},{11,1... | collective-permute-start | bytes 589832 | tf_op jit(solution)/shard_map/ppermute | solution.py:427
  17.8 0.2 copy.35
  18.2 0.3 collective-permute-start.2
  18.4 0.7 pad_add_fusion.pos
  19.1 0.8 pad_maximum_fusion.2.w1
  19.9 1.1 %collective-permute-done.3.right = bf16[768,128]{1,0:T(8,128)(2,1)S(1)} collective-permute-done((bf16[768,128]{1,0:T(8,128)(2,1)S(1)}, bf16[768,128]{1,0:T(8,128)(2,1)S(1)}, u32[]{:S(2)}, u32[]{:S(2)}) %collective-permute-start.3) | collective-permute-done | bytes 196640 | tf_op jit(solution)/shard_map/ppermute | solution.py:427
  21.0 4.6 %collective-permute-done.2.left = bf16[768,128]{1,0:T(8,128)(2,1)S(1)} collective-permute-done((bf16[768,128]{1,0:T(8,128)(2,1)S(1)}, bf16[768,128]{1,0:T(8,128)(2,1)S(1)}, u32[]{:S(2)}, u32[]{:S(2)}) %collective-permute-start.2) | collective-permute-done | bytes 196640 | tf_op jit(solution)/shard_map/ppermute | solution.py:427
  25.6 0.7 copy-done.15
  26.3 29.5 %shard_map.139 = (f32[3,17,32,32]{3,2,1,0:T(8,128)}, bf16[16,160,128]{2,1,0:T(8,128)(2,1)}) custom-call(s32[4]{0:T(128)} %pad_add_fusion.pos, bf16[3,17,48,32]{3,2,1,0:T(8,128)(2,1)} %copy-done, bf16[768,128]{1,0:T(8,128)(2,1)} %copy-done.15, bf16[768,128]{1,0:T(8,128)(2,1)} %copy-done.14, bf16[9,20,16,128]{3,2,1,0:T(8,128)(2,1)} %copy-done.1, ...), custom_call_target="tpu_custom_call" | custom-call | flops 10000000000 | bytes 20000000 | tf_op jit(solution)/shard_map/pallas_call | solution.py:373
  55.8 15.6 %all_to_all.5 = bf16[16,160,128]{2,1,0:T(8,128)(2,1)S(1)} all-to-all(bf16[16,160,128]{2,1,0:T(8,128)(2,1)} %get-tuple-element.6), channel_id=1, replica_groups=mesh['ha'=8,'wa'=16] {'wa'}, dimensions={0} | all-to-all | bytes 1310720 | tf_op jit(solution)/shard_map/all_to_all | solution.py:488
  71.4 0.1 reduce_sum.12
  71.5 0.1 collective-permute-start.4
  71.6 4.0 %collective-permute-done.4 = bf16[160,128]{1,0:T(8,128)(2,1)S(1)} collective-permute-done((bf16[160,128]{1,0:T(8,128)(2,1)S(1)}, bf16[160,128]{1,0:T(8,128)(2,1)S(1)}, u32[]{:S(2)}, u32[]{:S(2)}) %collective-permute-start.4) | collective-permute-done | bytes 40992 | tf_op jit(solution)/shard_map/ppermute | solution.py:494
  75.6 3.1 %collective-permute-start.5 = (bf16[160,128]{1,0:T(8,128)(2,1)S(1)}, bf16[160,128]{1,0:T(8,128)(2,1)S(1)}, u32[]{:S(2)}, u32[]{:S(2)}) collective-permute-start(bf16[160,128]{1,0:T(8,128)(2,1)S(1)} %add_convert_fusion.1), channel_id=1, source_target_pairs={{0,32},{16,48},{32,0},{48,16},{64,96},{80,112},{96,64},{112,80},{1... | collective-permute-start | bytes 122888 | tf_op jit(solution)/shard_map/ppermute | solution.py:494
  78.7 2.4 %collective-permute-done.5 = bf16[160,128]{1,0:T(8,128)(2,1)S(1)} collective-permute-done((bf16[160,128]{1,0:T(8,128)(2,1)S(1)}, bf16[160,128]{1,0:T(8,128)(2,1)S(1)}, u32[]{:S(2)}, u32[]{:S(2)}) %collective-permute-start.5) | collective-permute-done | bytes 40992 | tf_op jit(solution)/shard_map/ppermute | solution.py:494
  81.2 2.3 %collective-permute-start.6 = (bf16[160,128]{1,0:T(8,128)(2,1)S(1)}, bf16[160,128]{1,0:T(8,128)(2,1)S(1)}, u32[]{:S(2)}, u32[]{:S(2)}) collective-permute-start(bf16[160,128]{1,0:T(8,128)(2,1)S(1)} %add_convert_fusion), channel_id=1, source_target_pairs={{0,64},{16,80},{32,96},{48,112},{64,0},{80,16},{96,32},{112,48},{1... | collective-permute-start | bytes 122888 | tf_op jit(solution)/shard_map/ppermute | solution.py:494
  83.5 3.3 %collective-permute-done.6 = bf16[160,128]{1,0:T(8,128)(2,1)S(1)} collective-permute-done((bf16[160,128]{1,0:T(8,128)(2,1)S(1)}, bf16[160,128]{1,0:T(8,128)(2,1)S(1)}, u32[]{:S(2)}, u32[]{:S(2)}) %collective-permute-start.6) | collective-permute-done | bytes 40992 | tf_op jit(solution)/shard_map/ppermute | solution.py:494
  86.8 0.1 slice.131
  86.9 0.2 fusion.12
  87.1 0.2 reshape.79
  87.4 0.7 copy.50
  88.0 0.6 reshape.78
  (43 shorter events, 0.5 us)
Async XLA Ops:
  0.6 9.0 %copy-start.11 = (bf16[384,81]{1,0:T(8,128)(2,1)S(1)}, bf16[384,81]{1,0:T(8,128)(2,1)}, u32[]{:S(2)}) copy-start(bf16[384,81]{1,0:T(8,128)(2,1)} %constant.101) | copy-start | bytes 186628
  0.6 9.2 %copy-start.12 = (bf16[384,81]{1,0:T(8,128)(2,1)S(1)}, bf16[384,81]{1,0:T(8,128)(2,1)}, u32[]{:S(2)}) copy-start(bf16[384,81]{1,0:T(8,128)(2,1)} %constant.97) | copy-start | bytes 186628
  0.7 9.4 %copy-start.4 = (bf16[16,81,80]{1,2,0:T(8,128)(2,1)S(1)}, bf16[16,81,80]{1,2,0:T(8,128)(2,1)}, u32[]{:S(2)}) copy-start(bf16[16,81,80]{1,2,0:T(8,128)(2,1)} %constant.72.clone) | copy-start | bytes 622084
  0.7 9.0 %copy-start.13 = (bf16[3,3,3,3,64]{4,3,2,1,0:T(4,128)(2,1)S(1)}, bf16[3,3,3,3,64]{4,3,2,1,0:T(4,128)(2,1)}, u32[]{:S(2)}) copy-start(bf16[3,3,3,3,64]{4,3,2,1,0:T(4,128)(2,1)} %param.13) | copy-start | bytes 31108
  2.7 8.6 %copy-start.8 = (bf16[384,81]{1,0:T(8,128)(2,1)S(1)}, bf16[384,81]{1,0:T(8,128)(2,1)}, u32[]{:S(2)}) copy-start(bf16[384,81]{1,0:T(8,128)(2,1)} %constant.102) | copy-start | bytes 186628
  2.7 11.3 %collective-permute-start = (bf16[696,128]{1,0:T(8,128)(2,1)S(1)}, bf16[696,128]{1,0:T(8,128)(2,1)S(1)}, u32[]{:S(2)}, u32[]{:S(2)}) collective-permute-start(bf16[696,128]{1,0:T(8,128)(2,1)S(1)} %fusion.10), channel_id=1, source_target_pairs={{0,16},{16,32},{32,48},{48,64},{64,80},{80,96},{96,112},{112,0},{1... | collective-permute-start | bytes 534536 | tf_op jit(solution)/shard_map/ppermute | solution.py:427
  4.8 9.3 %collective-permute-start.1 = (bf16[696,128]{1,0:T(8,128)(2,1)S(1)}, bf16[696,128]{1,0:T(8,128)(2,1)S(1)}, u32[]{:S(2)}, u32[]{:S(2)}) collective-permute-start(bf16[696,128]{1,0:T(8,128)(2,1)S(1)} %fusion.11), channel_id=1, source_target_pairs={{16,0},{32,16},{48,32},{64,48},{80,64},{96,80},{112,96},{0,112},{1... | collective-permute-start | bytes 534536 | tf_op jit(solution)/shard_map/ppermute | solution.py:427
  9.8 1.7 %copy-start.7 = (bf16[384,81]{1,0:T(8,128)(2,1)S(1)}, bf16[384,81]{1,0:T(8,128)(2,1)}, u32[]{:S(2)}) copy-start(bf16[384,81]{1,0:T(8,128)(2,1)} %constant.103) | copy-start | bytes 186628
  10.4 1.3 %copy-start.10 = (bf16[384,81]{1,0:T(8,128)(2,1)S(1)}, bf16[384,81]{1,0:T(8,128)(2,1)}, u32[]{:S(2)}) copy-start(bf16[384,81]{1,0:T(8,128)(2,1)} %constant.104) | copy-start | bytes 186628
  11.3 0.9 %copy-start.6 = (bf16[384,81]{1,0:T(8,128)(2,1)S(1)}, bf16[384,81]{1,0:T(8,128)(2,1)}, u32[]{:S(2)}) copy-start(bf16[384,81]{1,0:T(8,128)(2,1)} %constant.98) | copy-start | bytes 186628
  11.5 0.9 %copy-start.5 = (bf16[384,81]{1,0:T(8,128)(2,1)S(1)}, bf16[384,81]{1,0:T(8,128)(2,1)}, u32[]{:S(2)}) copy-start(bf16[384,81]{1,0:T(8,128)(2,1)} %constant.99) | copy-start | bytes 186628
  11.8 0.9 %copy-start.9 = (bf16[384,81]{1,0:T(8,128)(2,1)S(1)}, bf16[384,81]{1,0:T(8,128)(2,1)}, u32[]{:S(2)}) copy-start(bf16[384,81]{1,0:T(8,128)(2,1)} %constant.100) | copy-start | bytes 186628
  12.7 1.5 %copy-start.2 = (bf16[3,17,32,32]{3,2,1,0:T(8,128)(2,1)S(1)}, bf16[3,17,32,32]{3,2,1,0:T(8,128)(2,1)}, u32[]{:S(2)}) copy-start(bf16[3,17,32,32]{3,2,1,0:T(8,128)(2,1)} %param.12) | copy-start | bytes 313348
  14.3 0.8 copy-start
  14.3 1.3 %copy-start.3 = (bf16[9,16,16,128]{3,2,1,0:T(8,128)(2,1)S(1)}, bf16[9,16,16,128]{3,2,1,0:T(8,128)(2,1)}, u32[]{:S(2)}) copy-start(bf16[9,16,16,128]{3,2,1,0:T(8,128)(2,1)} %param.17) | copy-start | bytes 1769476
  15.7 2.4 %copy-start.1 = (bf16[9,20,16,128]{3,2,1,0:T(8,128)(2,1)}, bf16[9,20,16,128]{3,2,1,0:T(8,128)(2,1)S(1)}, u32[]{:S(2)}) copy-start(bf16[9,20,16,128]{3,2,1,0:T(8,128)(2,1)S(1)} %pad_maximum_fusion.up_far) | copy-start | bytes 2211844
  16.0 5.0 %collective-permute-start.3 = (bf16[768,128]{1,0:T(8,128)(2,1)S(1)}, bf16[768,128]{1,0:T(8,128)(2,1)S(1)}, u32[]{:S(2)}, u32[]{:S(2)}) collective-permute-start(bf16[768,128]{1,0:T(8,128)(2,1)S(1)} %fusion.9), channel_id=1, source_target_pairs={{1,0},{2,1},{3,2},{4,3},{5,4},{6,5},{7,6},{8,7},{9,8},{10,9},{11,1... | collective-permute-start | bytes 589832 | tf_op jit(solution)/shard_map/ppermute | solution.py:427
  18.2 7.5 %collective-permute-start.2 = (bf16[768,128]{1,0:T(8,128)(2,1)S(1)}, bf16[768,128]{1,0:T(8,128)(2,1)S(1)}, u32[]{:S(2)}, u32[]{:S(2)}) collective-permute-start(bf16[768,128]{1,0:T(8,128)(2,1)S(1)} %fusion.8), channel_id=1, source_target_pairs={{0,1},{1,2},{2,3},{3,4},{4,5},{5,6},{6,7},{7,8},{8,9},{9,10},{10,1... | collective-permute-start | bytes 589832 | tf_op jit(solution)/shard_map/ppermute | solution.py:427
  21.0 4.6 %copy-start.14 = (bf16[768,128]{1,0:T(8,128)(2,1)}, bf16[768,128]{1,0:T(8,128)(2,1)S(1)}, u32[]{:S(2)}) copy-start(bf16[768,128]{1,0:T(8,128)(2,1)S(1)} %collective-permute-done.3.right) | copy-start | bytes 589828
  25.6 0.7 copy-start.15
  71.5 4.1 %collective-permute-start.4 = (bf16[160,128]{1,0:T(8,128)(2,1)S(1)}, bf16[160,128]{1,0:T(8,128)(2,1)S(1)}, u32[]{:S(2)}, u32[]{:S(2)}) collective-permute-start(bf16[160,128]{1,0:T(8,128)(2,1)S(1)} %reduce_sum.12), channel_id=1, source_target_pairs={{0,16},{16,0},{32,48},{48,32},{64,80},{80,64},{96,112},{112,96},{1... | collective-permute-start | bytes 122888 | tf_op jit(solution)/shard_map/ppermute | solution.py:494
  75.6 5.6 %collective-permute-start.5 = (bf16[160,128]{1,0:T(8,128)(2,1)S(1)}, bf16[160,128]{1,0:T(8,128)(2,1)S(1)}, u32[]{:S(2)}, u32[]{:S(2)}) collective-permute-start(bf16[160,128]{1,0:T(8,128)(2,1)S(1)} %add_convert_fusion.1), channel_id=1, source_target_pairs={{0,32},{16,48},{32,0},{48,16},{64,96},{80,112},{96,64},{112,80},{1... | collective-permute-start | bytes 122888 | tf_op jit(solution)/shard_map/ppermute | solution.py:494
  81.2 5.6 %collective-permute-start.6 = (bf16[160,128]{1,0:T(8,128)(2,1)S(1)}, bf16[160,128]{1,0:T(8,128)(2,1)S(1)}, u32[]{:S(2)}, u32[]{:S(2)}) collective-permute-start(bf16[160,128]{1,0:T(8,128)(2,1)S(1)} %add_convert_fusion), channel_id=1, source_target_pairs={{0,64},{16,80},{32,96},{48,112},{64,0},{80,16},{96,32},{112,48},{1... | collective-permute-start | bytes 122888 | tf_op jit(solution)/shard_map/ppermute | solution.py:494
